TPU v7x, 512 devices: a whole 4x4x16 slice. The times are simulated.
512 devices in a mesh: seq: 64 (over y_lo, z, core), head: 8 (over x, y_hi).
Axes of the slice: x: 4, y: 4 (y_hi: 2, y_lo: 2; y = y_hi * 2 + y_lo), z: 16, core: 2. Of those that a mesh axis runs over, the one named last changes fastest.
Arguments:
- queries: bfloat16 [65536, 2048], P(('seq', 'head')), may hold values from -6 to 6
- keys: bfloat16 [65536, 2048], P(('seq', 'head')), may hold values from -6 to 6
- values: bfloat16 [65536, 2048], P(('seq', 'head')), may hold values from -6 to 6
- out_grad: bfloat16 [65536, 3072], P(('seq', 'head')), may hold values from -24 to 24
- out_weight: bfloat16 [3072, 2048], P('seq', 'head'), may hold values from -0.125 to 0.125
Outputs:
- query_grad: bfloat16 [65536, 2048], P(('seq', 'head'))
- key_grad: bfloat16 [65536, 2048], P(('seq', 'head'))
- value_grad: bfloat16 [65536, 2048], P(('seq', 'head'))
- weight_grad: float32 [3072, 2048], P('seq', 'head')
All inputs are finite; a program needn't handle non-finite values.
Results may differ from a plain program's by a relative error of at most 0.039.
Values may be sent and summed in bfloat16 or wider, within the bound.
No kernel may reach another device: no remote copies, remote signals or barrier semaphores. Data moves between devices by JAX's collectives and lax.ppermute only.
A program may use at most 128 MiB of HBM per device.

v0:
```python
import math

import jax
import jax.numpy as jnp
from jax import lax
from jax.sharding import PartitionSpec as P

HEAD_DIM = 128
TILE = 256


def with_halo(array, sides, width):
    for axis, dim in sides:
        size, length = (lax.axis_size(axis), array.shape[dim])
        up = [(i, (i + 1) % size) for i in range(size - 1)]
        down = [(j, i) for i, j in up]
        last = lax.slice_in_dim(array, length - width, length, axis=dim)
        first = lax.slice_in_dim(array, 0, width, axis=dim)
        before = lax.ppermute(last, axis, up)
        after = lax.ppermute(first, axis, down)
        array = jnp.concatenate([before, array, after], axis=dim)
    return array


def passed_along(array, axis, by):
    length = lax.axis_size(axis)
    pairs = [(i, i + by) for i in range(length) if 0 <= i + by < length]
    return lax.ppermute(array, axis, pairs)


def per_device(queries, keys, values, out_grad, out_weight):
    q_local, k_local, v_local = (
        lax.all_to_all(queries, "head", split_axis=1, concat_axis=0, tiled=True),
        lax.all_to_all(keys, "head", split_axis=1, concat_axis=0, tiled=True),
        lax.all_to_all(values, "head", split_axis=1, concat_axis=0, tiled=True),
    )
    tok_rows = q_local.shape[0]
    feat_width = q_local.shape[1]
    heads_here = feat_width // HEAD_DIM
    tiles_here = tok_rows // TILE
    score_scale = 1.0 / math.sqrt(HEAD_DIM)
    grad_rows = lax.all_gather(out_grad, "head", axis=0, tiled=True)
    columns = grad_rows
    dout_rows = jnp.dot(
        columns,
        lax.all_gather(out_weight, "seq", axis=0, tiled=True),
        preferred_element_type=jnp.float32,
    ).astype(jnp.bfloat16)
    seq_place = lax.axis_index("seq")
    seq_count = lax.axis_size("seq")
    stacked = jnp.stack([k_local, v_local])
    extended = with_halo(stacked, (("seq", 1),), TILE)
    ext_tiles = extended.reshape(2, tiles_here + 2, TILE, feat_width)
    window = jnp.concatenate(
        [ext_tiles[:, offset : offset + tiles_here] for offset in range(3)], axis=2
    )
    tile_total = seq_count * tiles_here
    key_tile = (
        seq_place * tiles_here
        - 1
        + jnp.arange(tiles_here, dtype=jnp.int32)[:, None]
        + (jnp.arange(3 * TILE, dtype=jnp.int32) // TILE)[None, :]
    )
    in_window = jnp.logical_and(key_tile >= 0, key_tile < tile_total)
    per_group = math.gcd(tiles_here, max(1, 512 // TILE))
    group_count = tiles_here // per_group
    query_tiles = q_local.reshape(tiles_here, TILE, feat_width)
    dout_tiles = dout_rows.reshape(tiles_here, TILE, feat_width)

    def grouped(array):
        return array.reshape((group_count, per_group) + array.shape[1:])

    def tile_pass(operands):
        query_block, dout_block, key_block, value_block, mask_block = operands
        count = query_block.shape[0]
        query_heads = query_block.reshape(count, TILE, heads_here, HEAD_DIM)
        dout_heads = dout_block.reshape(count, TILE, heads_here, HEAD_DIM)
        key_heads = key_block.reshape(count, 3 * TILE, heads_here, HEAD_DIM)
        value_heads = value_block.reshape(count, 3 * TILE, heads_here, HEAD_DIM)
        scores = (
            jnp.einsum(
                "nqhd,nkhd->nhqk", query_heads, key_heads, preferred_element_type=jnp.float32
            )
            * score_scale
        )
        scores = jnp.where(mask_block[:, None, None, :], scores, -jnp.inf)
        row_top = jnp.max(scores, axis=3)
        log_total = row_top + jnp.log(jnp.sum(jnp.exp(scores - row_top[..., None]), axis=3))
        attend = jnp.exp(scores - log_total[..., None])
        weights = attend.astype(jnp.bfloat16)
        attn_heads = jnp.einsum(
            "nhqk,nkhd->nqhd", weights, value_heads, preferred_element_type=jnp.float32
        )
        attn_block = attn_heads.reshape(count, TILE, feat_width).astype(jnp.bfloat16)
        attn_back = attn_block.reshape(count, TILE, heads_here, HEAD_DIM).astype(jnp.float32)
        row_delta = jnp.sum(dout_heads.astype(jnp.float32) * attn_back, axis=3).transpose(0, 2, 1)
        dprobs = jnp.einsum(
            "nqhd,nkhd->nhqk", dout_heads, value_heads, preferred_element_type=jnp.float32
        )
        dscore = (score_scale * attend * (dprobs - row_delta[..., None])).astype(jnp.bfloat16)
        dq_block = (
            jnp.einsum("nhqk,nkhd->nqhd", dscore, key_heads, preferred_element_type=jnp.float32)
            .reshape(count, TILE, feat_width)
            .astype(jnp.bfloat16)
        )
        dk_block = jnp.einsum(
            "nhqk,nqhd->nkhd", dscore, query_heads, preferred_element_type=jnp.float32
        ).reshape(count, 3 * TILE, feat_width)
        dv_block = jnp.einsum(
            "nhqk,nqhd->nkhd", weights, dout_heads, preferred_element_type=jnp.float32
        ).reshape(count, 3 * TILE, feat_width)
        return (attn_block, dq_block, dk_block, dv_block, log_total, row_delta)

    attn_g, dq_g, dk_g, dv_g, log_g, delta_g = lax.map(
        tile_pass,
        (
            grouped(query_tiles),
            grouped(dout_tiles),
            grouped(window[0]),
            grouped(window[1]),
            grouped(in_window),
        ),
    )
    attn_rows = attn_g.reshape(tok_rows, feat_width)
    dq_out = dq_g.reshape(tok_rows, feat_width)
    key_parts = jnp.stack(
        [
            dk_g.reshape(tiles_here, 3, TILE, feat_width),
            dv_g.reshape(tiles_here, 3, TILE, feat_width),
        ]
    )
    spread = jnp.pad(key_parts[:, :, 0], ((0, 0), (0, 2), (0, 0), (0, 0)))
    spread = spread + jnp.pad(key_parts[:, :, 1], ((0, 0), (1, 1), (0, 0), (0, 0)))
    spread = spread + jnp.pad(key_parts[:, :, 2], ((0, 0), (2, 0), (0, 0), (0, 0)))
    own_grads = spread[:, 1 : tiles_here + 1]
    from_left = passed_along(spread[:, tiles_here + 1].astype(jnp.bfloat16), "seq", 1).astype(
        jnp.float32
    )
    from_right = passed_along(spread[:, 0].astype(jnp.bfloat16), "seq", -1).astype(jnp.float32)
    own_grads = own_grads.at[:, 0].add(from_left)
    own_grads = own_grads.at[:, tiles_here - 1].add(from_right)
    dk_total = own_grads[0].reshape(tok_rows, feat_width).astype(jnp.bfloat16)
    dv_total = own_grads[1].reshape(tok_rows, feat_width).astype(jnp.bfloat16)
    query_grad, key_grad, value_grad = (
        lax.all_to_all(dq_out, "head", split_axis=0, concat_axis=1, tiled=True),
        lax.all_to_all(dk_total, "head", split_axis=0, concat_axis=1, tiled=True),
        lax.all_to_all(dv_total, "head", split_axis=0, concat_axis=1, tiled=True),
    )
    columns = grad_rows
    weight_grad = lax.psum_scatter(
        lax.dot_general(
            columns, attn_rows, (((0,), (0,)), ((), ())), preferred_element_type=jnp.float32
        ),
        "seq",
        scatter_dimension=0,
        tiled=True,
    )
    return (query_grad, key_grad, value_grad, weight_grad)


def solution(mesh):
    in_specs = (
        P(("seq", "head"), None),
        P(("seq", "head"), None),
        P(("seq", "head"), None),
        P(("seq", "head"), None),
        P("seq", "head"),
    )
    out_specs = (
        P(("seq", "head"), None),
        P(("seq", "head"), None),
        P(("seq", "head"), None),
        P("seq", "head"),
    )
    return jax.shard_map(
        per_device, mesh=mesh, in_specs=in_specs, out_specs=out_specs, check_vma=False
    )
```

profile of v0, /device:TPU:24, one launch (start us, length us, event | category | flops | bytes accessed | tf_op | source)
XLA Modules:
  0.0 537.4 jit_solution(2378844515008675400)
XLA Ops:
  8.7 2.0 copy.101
  10.7 7.3 %all-to-all-start = ((bf16[128,8,256]{0,2,1:T(8,128)(2,1)}), bf16[128,8,256]{0,2,1:T(8,128)(2,1)S(1)}, u32[]{:S(2)}, u32[]{:S(2)}) async-start(bf16[128,8,256]{0,2,1:T(8,128)(2,1)} %bitcast.14), calls=%async_computation | async-start | bytes 1048576 | tf_op jit(solution)/shard_map/all_to_all | solution.py:34
  19.0 7.9 %all-to-all-done = bf16[128,8,256]{0,2,1:T(8,128)(2,1)S(1)} async-done(((bf16[128,8,256]{0,2,1:T(8,128)(2,1)}), bf16[128,8,256]{0,2,1:T(8,128)(2,1)S(1)}, u32[]{:S(2)}, u32[]{:S(2)}) %all-to-all-start) | async-done | bytes 524320 | tf_op jit(solution)/shard_map/all_to_all | solution.py:34
  26.9 5.4 %all-to-all-start.1 = ((bf16[128,8,256]{0,2,1:T(8,128)(2,1)}), bf16[128,8,256]{0,2,1:T(8,128)(2,1)S(1)}, u32[]{:S(2)}, u32[]{:S(2)}) async-start(bf16[128,8,256]{0,2,1:T(8,128)(2,1)} %bitcast.17), calls=%async_computation.1 | async-start | bytes 1048576 | tf_op jit(solution)/shard_map/all_to_all | solution.py:35
  33.5 7.3 %all-to-all-done.1 = bf16[128,8,256]{0,2,1:T(8,128)(2,1)S(1)} async-done(((bf16[128,8,256]{0,2,1:T(8,128)(2,1)}), bf16[128,8,256]{0,2,1:T(8,128)(2,1)S(1)}, u32[]{:S(2)}, u32[]{:S(2)}) %all-to-all-start.1) | async-done | bytes 524320 | tf_op jit(solution)/shard_map/all_to_all | solution.py:35
  40.8 5.5 %all-to-all-start.2 = ((bf16[128,8,256]{0,2,1:T(8,128)(2,1)}), bf16[128,8,256]{0,2,1:T(8,128)(2,1)S(1)}, u32[]{:S(2)}, u32[]{:S(2)}) async-start(bf16[128,8,256]{0,2,1:T(8,128)(2,1)} %bitcast.22), calls=%async_computation.2 | async-start | bytes 1048576 | tf_op jit(solution)/shard_map/all_to_all | solution.py:33
  46.6 1.9 collective-permute-start
  48.5 10.2 %collective-permute-start.1 = (bf16[2,256,256]{2,1,0:T(8,128)(2,1)S(1)}, bf16[2,256,256]{2,1,0:T(8,128)(2,1)S(1)}, u32[]{:S(2)}, u32[]{:S(2)}) collective-permute-start(bf16[2,256,256]{2,1,0:T(8,128)(2,1)S(1)} %get-tuple-element.200), channel_id=1, source_target_pairs={{8,0},{16,8},{24,16},{32,24},{40,32},{48,40},{56,48},{64,56},{72,6... | collective-permute-start | bytes 786440 | tf_op jit(solution)/shard_map/ppermute | solution.py:20
  59.9 1.1 collective-permute-done
  60.9 1.8 collective-permute-done.1
  63.8 1.6 copy.108
  65.4 1.6 copy.105
  66.9 69.0 %all-gather.5.cloned.1.call-done = bf16[3072,256]{1,0:T(8,128)(2,1)} async-done(((bf16[48,256]{1,0:T(8,128)(2,1)}), bf16[3072,256]{1,0:T(8,128)(2,1)}) %all-gather.5.cloned.1.call-update) | async-done | bytes 1572880 | tf_op jit(solution)/shard_map/all_gather | solution.py:46
  135.9 103.8 %all-gather.3.cloned.1.call-done = bf16[1024,3072]{1,0:T(8,128)(2,1)} async-done(((bf16[128,3072]{1,0:T(8,128)(2,1)}), bf16[1024,3072]{1,0:T(8,128)(2,1)}) %all-gather.3.cloned.1.call-update) | async-done | bytes 6291472 | tf_op jit(solution)/shard_map/all_gather | solution.py:42
  239.7 5.8 %convolution_convert_fusion.2 = bf16[1024,256]{1,0:T(8,128)(2,1)} fusion(bf16[1024,3072]{1,0:T(8,128)(2,1)} %all-gather.3.cloned.1.call-done, bf16[3072,256]{1,0:T(8,128)(2,1)} %all-gather.5.cloned.1.call-done), kind=kOutput, calls=%fused_computation.38 | convolution fusion | flops 1610874880 | bytes 8388608 | tf_op jit(solution)/shard_map/dot_general | solution.py:44
  245.5 46.2 %while.18 = (s32[]{:T(128)}, bf16[2,2,256,256]{3,2,1,0:T(8,128)(2,1)}, bf16[2,2,256,256]{3,2,1,0:T(8,128)(2,1)}, f32[2,2,768,256]{3,2,1,0:T(8,128)}, f32[2,2,768...) while((s32[]{:T(128)}, ...), condition=%wide.region_4.5_spmd, body=%wide.region_0.4_spmd.sunk | while | flops 1226045440 | bytes 61135672 | solution.py:114
  248.4 1.2 constant_dynamic-slice_fusion.8
  249.6 1.5 constant_dynamic-slice_fusion.11
  252.7 1.7 multiply_reduce_fusion.2
  254.4 1.8 copy.160
  256.2 2.4 multiply_convert_fusion.2
  258.6 2.0 fusion.65
  263.0 1.9 copy.161
  264.9 1.8 constant_dynamic-update-slice_fusion.6
  266.7 1.9 constant_dynamic-update-slice_fusion.7
  271.5 1.2 constant_dynamic-slice_fusion.8
  272.7 1.5 constant_dynamic-slice_fusion.11
  275.8 1.7 multiply_reduce_fusion.2
  277.4 1.8 copy.160
  279.3 2.4 multiply_convert_fusion.2
  281.7 2.0 fusion.65
  286.0 1.9 copy.161
  288.0 1.8 constant_dynamic-update-slice_fusion.6
  289.7 1.9 constant_dynamic-update-slice_fusion.7
  291.7 4.8 convolution_bitcast_fusion
  296.5 2.3 copy.131
  298.8 1.9 copy-done.6
  300.7 2.4 fusion.12
  304.6 1.9 collective-permute-start.2
  306.5 6.0 %collective-permute-start.3 = (bf16[2,256,256]{2,1,0:T(8,128)(2,1)}, bf16[2,256,256]{2,1,0:T(8,128)(2,1)S(1)}, u32[]{:S(2)}, u32[]{:S(2)}) collective-permute-start(bf16[2,256,256]{2,1,0:T(8,128)(2,1)} %get-tuple-element.192), channel_id=1, source_target_pairs={{8,0},{16,8},{24,16},{32,24},{40,32},{48,40},{56,48},{64,56},{72,6... | collective-permute-start | bytes 786440 | tf_op jit(solution)/shard_map/ppermute | solution.py:28
  312.5 6.3 %all-to-all-start.3 = ((bf16[8,128,256]{2,1,0:T(8,128)(2,1)}), bf16[8,128,256]{2,1,0:T(8,128)(2,1)}, u32[]{:S(2)}, u32[]{:S(2)}) async-start(bf16[8,128,256]{2,1,0:T(8,128)(2,1)} %bitcast.162), calls=%async_computation.3 | async-start | bytes 1048576 | tf_op jit(solution)/shard_map/all_to_all | solution.py:145
  321.1 5.2 all-to-all-done.3
  326.4 12.7 %all_to_all.99 = bf16[8,128,256]{2,1,0:T(8,128)(2,1)S(1)} all-to-all(bf16[8,128,256]{2,1,0:T(8,128)(2,1)S(1)} %bitcast.160), channel_id=1, replica_groups=mesh['seq'=64,'head'=8] {'head'}, dimensions={0} | all-to-all | bytes 1048576 | tf_op jit(solution)/shard_map/all_to_all | solution.py:146
  339.1 5.7 %all-to-all-start.5 = ((bf16[8,128,256]{2,1,0:T(8,128)(2,1)}), bf16[8,128,256]{2,1,0:T(8,128)(2,1)S(1)}, u32[]{:S(2)}, u32[]{:S(2)}) async-start(bf16[8,128,256]{2,1,0:T(8,128)(2,1)} %bitcast.42), calls=%async_computation.5 | async-start | bytes 1048576 | tf_op jit(solution)/shard_map/all_to_all | solution.py:147
  344.8 1.3 copy.112
  347.4 1.0 copy.124
  348.4 3.9 all-to-all-done.5
  353.6 177.2 %reduce-scatter.4.cloned.1.call-done = f32[48,256]{1,0:T(8,128)} async-done(((f32[3072,256]{1,0:T(8,128)}), f32[48,256]{1,0:T(8,128)}) %reduce-scatter.4.cloned.1.call-update) | async-done | bytes 49168
  (91 shorter events, 26.1 us)
Async XLA Ops:
  7.2 10.8 %copy-start.7 = (bf16[128,2048]{1,0:T(8,128)(2,1)S(1)}, bf16[128,2048]{1,0:T(8,128)(2,1)}, u32[]{:S(2)}) copy-start(bf16[128,2048]{1,0:T(8,128)(2,1)} %param.13) | copy-start | bytes 1572868
  7.2 25.1 %copy-start.8 = (bf16[128,2048]{1,0:T(8,128)(2,1)S(1)}, bf16[128,2048]{1,0:T(8,128)(2,1)}, u32[]{:S(2)}) copy-start(bf16[128,2048]{1,0:T(8,128)(2,1)} %param.11) | copy-start | bytes 1572868
  7.2 128.7 %all-gather.5.cloned.1.call-start = ((), (), s32[]{:S(2)}) async-start(), calls=%async_computation.8 | async-start | bytes 1597440 | tf_op jit(solution)/shard_map/all_gather | solution.py:46
  7.9 231.8 %all-gather.3.cloned.1.call-start = ((), (), s32[]{:S(2)}) async-start(), calls=%async_computation.7 | async-start | bytes 7077888 | tf_op jit(solution)/shard_map/all_gather | solution.py:42
  10.7 16.2 %all-to-all-start = ((bf16[128,8,256]{0,2,1:T(8,128)(2,1)}), bf16[128,8,256]{0,2,1:T(8,128)(2,1)S(1)}, u32[]{:S(2)}, u32[]{:S(2)}) async-start(bf16[128,8,256]{0,2,1:T(8,128)(2,1)} %bitcast.14), calls=%async_computation | async-start | bytes 1048576 | tf_op jit(solution)/shard_map/all_to_all | solution.py:34
  26.9 13.9 %all-to-all-start.1 = ((bf16[128,8,256]{0,2,1:T(8,128)(2,1)}), bf16[128,8,256]{0,2,1:T(8,128)(2,1)S(1)}, u32[]{:S(2)}, u32[]{:S(2)}) async-start(bf16[128,8,256]{0,2,1:T(8,128)(2,1)} %bitcast.17), calls=%async_computation.1 | async-start | bytes 1048576 | tf_op jit(solution)/shard_map/all_to_all | solution.py:35
  40.8 18.0 %all-to-all-start.2 = ((bf16[128,8,256]{0,2,1:T(8,128)(2,1)}), bf16[128,8,256]{0,2,1:T(8,128)(2,1)S(1)}, u32[]{:S(2)}, u32[]{:S(2)}) async-start(bf16[128,8,256]{0,2,1:T(8,128)(2,1)} %bitcast.22), calls=%async_computation.2 | async-start | bytes 1048576 | tf_op jit(solution)/shard_map/all_to_all | solution.py:33
  46.3 484.5 %reduce-scatter.4.cloned.1.call-start = ((), (), s32[]{:S(2)}) async-start(), calls=%async_computation.9 | async-start | bytes 3194880
  46.6 14.3 %collective-permute-start = (bf16[2,256,256]{2,1,0:T(8,128)(2,1)S(1)}, bf16[2,256,256]{2,1,0:T(8,128)(2,1)S(1)}, u32[]{:S(2)}, u32[]{:S(2)}) collective-permute-start(bf16[2,256,256]{2,1,0:T(8,128)(2,1)S(1)} %get-tuple-element.199), channel_id=1, source_target_pairs={{0,8},{8,16},{16,24},{24,32},{32,40},{40,48},{48,56},{56,64},{64,7... | collective-permute-start | bytes 786440 | tf_op jit(solution)/shard_map/ppermute | solution.py:19
  48.5 14.2 %collective-permute-start.1 = (bf16[2,256,256]{2,1,0:T(8,128)(2,1)S(1)}, bf16[2,256,256]{2,1,0:T(8,128)(2,1)S(1)}, u32[]{:S(2)}, u32[]{:S(2)}) collective-permute-start(bf16[2,256,256]{2,1,0:T(8,128)(2,1)S(1)} %get-tuple-element.200), channel_id=1, source_target_pairs={{8,0},{16,8},{24,16},{32,24},{40,32},{48,40},{56,48},{64,56},{72,6... | collective-permute-start | bytes 786440 | tf_op jit(solution)/shard_map/ppermute | solution.py:20
  249.6 1.5 copy-start
  251.1 1.6 copy-start.5
  251.1 1.6 copy-start.2
  256.2 2.4 copy-start.3
  258.6 2.0 copy-start.1
  263.0 1.9 copy-start.4
  272.7 1.5 copy-start
  274.2 1.6 copy-start.5
  274.2 1.6 copy-start.2
  279.3 2.4 copy-start.3
  281.7 2.0 copy-start.1
  286.0 1.9 copy-start.4
  298.8 1.9 copy-start.6
  304.6 14.5 %collective-permute-start.2 = (bf16[2,256,256]{2,1,0:T(8,128)(2,1)}, bf16[2,256,256]{2,1,0:T(8,128)(2,1)}, u32[]{:S(2)}, u32[]{:S(2)}) collective-permute-start(bf16[2,256,256]{2,1,0:T(8,128)(2,1)} %get-tuple-element.193), channel_id=1, source_target_pairs={{0,8},{8,16},{16,24},{24,32},{32,40},{40,48},{48,56},{56,64},{64,7... | collective-permute-start | bytes 786440 | tf_op jit(solution)/shard_map/ppermute | solution.py:28
  306.5 13.5 %collective-permute-start.3 = (bf16[2,256,256]{2,1,0:T(8,128)(2,1)}, bf16[2,256,256]{2,1,0:T(8,128)(2,1)S(1)}, u32[]{:S(2)}, u32[]{:S(2)}) collective-permute-start(bf16[2,256,256]{2,1,0:T(8,128)(2,1)} %get-tuple-element.192), channel_id=1, source_target_pairs={{8,0},{16,8},{24,16},{32,24},{40,32},{48,40},{56,48},{64,56},{72,6... | collective-permute-start | bytes 786440 | tf_op jit(solution)/shard_map/ppermute | solution.py:28
  312.5 13.9 %all-to-all-start.3 = ((bf16[8,128,256]{2,1,0:T(8,128)(2,1)}), bf16[8,128,256]{2,1,0:T(8,128)(2,1)}, u32[]{:S(2)}, u32[]{:S(2)}) async-start(bf16[8,128,256]{2,1,0:T(8,128)(2,1)} %bitcast.162), calls=%async_computation.3 | async-start | bytes 1048576 | tf_op jit(solution)/shard_map/all_to_all | solution.py:145
  339.1 13.3 %all-to-all-start.5 = ((bf16[8,128,256]{2,1,0:T(8,128)(2,1)}), bf16[8,128,256]{2,1,0:T(8,128)(2,1)S(1)}, u32[]{:S(2)}, u32[]{:S(2)}) async-start(bf16[8,128,256]{2,1,0:T(8,128)(2,1)} %bitcast.42), calls=%async_computation.5 | async-start | bytes 1048576 | tf_op jit(solution)/shard_map/all_to_all | solution.py:147
Sparse Core Ops, SparseCore 0:
  10.2 125.6 all-gather.4
  139.1 100.5 all-gather.2
  298.9 231.8 reduce-scatter.3
where the time goes:
time: 539 us; the launch traced here: 537 us
  waiting for transfers between devices  379 us (70%)
  starting transfers between devices  50.2 us (9%)
  local copies, waits for them, and re-layouts  48.9 us (9%)
  matrix products  26.2 us (5%)
  between operations  14 us (3%)
  blocking collectives  12.7 us (2%)
  other arithmetic  6.58 us (1%)
    unnamed x4, waiting for transfers between devices  179 us
    all_gather x1, waiting for transfers between devices, per_device(): grad_rows = lax.all_gather(out_grad, 'head', axis=0, tiled=True)  104 us
    all_gather x1, waiting for transfers between devices, per_device(): lax.all_gather(out_weight, 'seq', axis=0, tiled=True)  69 us
    dynamic_update_slice x12, local copies, waits for them, and re-layouts, per_device(): lax.map(tile_pass, (grouped(query_tiles), grouped(dout_tiles), grouped(wi...  17.4 us
    all_to_all x1, blocking collectives, per_device(): lax.all_to_all(dk_total, 'head', split_axis=0, concat_axis=1, tiled=True)  12.7 us
    unnamed x14, local copies, waits for them, and re-layouts  11.4 us
    dynamic_slice x12, local copies, waits for them, and re-layouts, per_device(): lax.map(tile_pass, (grouped(query_tiles), grouped(dout_tiles), grouped(wi...  11.1 us
  transfers between devices with their start and end apart: 12, of which 9 were waited for; matrix products, arithmetic and copies ran while one was open for 4% of the time, Pallas kernels for 0%

commit v1 on v0

v1 whole, which is shorter than its diff:
```python
import math

import jax
import jax.numpy as jnp
from jax import lax
from jax.experimental import pallas as pl
from jax.experimental.pallas import tpu as pltpu
from jax.sharding import Mesh, PartitionSpec as P

HEAD_DIM = 128
TILE = 256
SCALE = 1.0 / math.sqrt(HEAD_DIM)
F32 = jnp.float32
BF16 = jnp.bfloat16
SEQ = ("ylo", "z", "core")
HEAD = ("x", "yhi")
NT = (((1,), (1,)), ((), ()))
TN = (((0,), (0,)), ((), ()))


def tile_of(ref, u, before, after, count):
    if u < 0:
        return before[...]
    if u >= count:
        return after[...]
    return ref[u * TILE : (u + 1) * TILE, :]


def forward_kernel(bias, q, k, v, kb, vb, ka, va, attn, pt):
    count = q.shape[0] // TILE
    for t in range(count):
        rows = slice(t * TILE, (t + 1) * TILE)
        q_t = q[rows, :]
        parts = []
        for j in range(3):
            u = t + j - 1
            s = lax.dot_general(
                tile_of(k, u, kb, ka, count), q_t, NT, preferred_element_type=F32
            )
            if u < 0:
                s = s + bias[0]
            if u >= count:
                s = s + bias[1]
            parts.append(s)
        top = jnp.maximum(jnp.maximum(parts[0], parts[1]), parts[2])
        top = jnp.max(top, axis=0, keepdims=True)
        parts = [jnp.exp((s - top) * SCALE) for s in parts]
        total = jnp.sum(parts[0] + parts[1] + parts[2], axis=0, keepdims=True)
        inverse = 1.0 / total
        out = jnp.zeros((TILE, HEAD_DIM), F32)
        for j in range(3):
            w = (parts[j] * inverse).astype(BF16)
            pt[0, t, j * TILE : (j + 1) * TILE, :] = w
            out += lax.dot_general(
                w, tile_of(v, t + j - 1, vb, va, count), TN, preferred_element_type=F32
            )
        attn[rows, :] = out.astype(BF16)


def backward_kernel(q, k, v, kb, vb, ka, va, pt, keep, recv, dx, hb, ha):
    count = q.shape[0] // TILE
    h = pl.program_id(0)
    width = 2 * HEAD_DIM
    dk = [jnp.zeros((TILE, HEAD_DIM), F32) for _ in range(count + 2)]
    dv = [jnp.zeros((TILE, HEAD_DIM), F32) for _ in range(count + 2)]
    col = [pl.ds(pl.multiple_of(n * width + h * HEAD_DIM, HEAD_DIM), HEAD_DIM) for n in range(3)]
    for t in range(count):
        rows = slice(t * TILE, (t + 1) * TILE)
        q_t = q[rows, :]
        do = (keep[rows, :] + recv[rows, :].astype(F32)).astype(BF16)
        dps, ws = [], []
        delta = jnp.zeros((1, TILE), F32)
        for j in range(3):
            dp = lax.dot_general(
                tile_of(v, t + j - 1, vb, va, count), do, NT, preferred_element_type=F32
            )
            w = pt[0, t, j * TILE : (j + 1) * TILE, :]
            delta += jnp.sum(w.astype(F32) * dp, axis=0, keepdims=True)
            dps.append(dp)
            ws.append(w)
        dq = jnp.zeros((TILE, HEAD_DIM), F32)
        for j in range(3):
            ds = (ws[j].astype(F32) * (dps[j] - delta)).astype(BF16)
            dv[t + j] += jnp.dot(ws[j], do, preferred_element_type=F32)
            dk[t + j] += jnp.dot(ds, q_t, preferred_element_type=F32)
            dq += lax.dot_general(
                ds, tile_of(k, t + j - 1, kb, ka, count), TN, preferred_element_type=F32
            )
        dx[rows, col[0]] = (dq * SCALE).astype(BF16)
    for u in range(count + 2):
        a = (dk[u] * SCALE).astype(BF16)
        b = dv[u].astype(BF16)
        if u == 0:
            hb[:, col[0]] = a
            hb[:, col[1]] = b
        elif u == count + 1:
            ha[:, col[0]] = a
            ha[:, col[1]] = b
        else:
            rows = slice((u - 1) * TILE, u * TILE)
            dx[rows, col[1]] = a
            dx[rows, col[2]] = b


def column(rows, offset):
    return pl.BlockSpec((rows, HEAD_DIM), lambda h: (0, offset + h))


def tile_specs(rows):
    return [
        column(rows, 0),
        column(rows, 2),
        column(rows, 4),
        column(TILE, 0),
        column(TILE, 2),
        column(TILE, 0),
        column(TILE, 2),
    ]


def attention_forward(bias, x, before, after):
    rows = x.shape[0]
    count = rows // TILE
    return pl.pallas_call(
        forward_kernel,
        grid=(2,),
        in_specs=[pl.BlockSpec(memory_space=pltpu.SMEM)] + tile_specs(rows),
        out_specs=[
            column(rows, 0),
            pl.BlockSpec((1, count, 3 * TILE, TILE), lambda h: (h, 0, 0, 0)),
        ],
        out_shape=[
            jax.ShapeDtypeStruct((rows, 2 * HEAD_DIM), BF16),
            jax.ShapeDtypeStruct((2, count, 3 * TILE, TILE), BF16),
        ],
        compiler_params=pltpu.CompilerParams(vmem_limit_bytes=40 * 1024 * 1024),
        cost_estimate=pl.CostEstimate(
            flops=2 * 2 * 2 * rows * 3 * TILE * HEAD_DIM,
            bytes_accessed=6 * 1024 * 1024,
            transcendentals=2 * rows * 3 * TILE,
        ),
        name="forward",
    )(bias, x, x, x, before, before, after, after)


def attention_backward(x, before, after, pt, keep, recv):
    rows = x.shape[0]
    count = rows // TILE
    return pl.pallas_call(
        backward_kernel,
        grid=(2,),
        in_specs=tile_specs(rows)
        + [
            pl.BlockSpec((1, count, 3 * TILE, TILE), lambda h: (h, 0, 0, 0)),
            column(rows, 0),
            column(rows, 0),
        ],
        out_specs=[
            pl.BlockSpec((rows, 6 * HEAD_DIM), lambda h: (0, 0)),
            pl.BlockSpec((TILE, 4 * HEAD_DIM), lambda h: (0, 0)),
            pl.BlockSpec((TILE, 4 * HEAD_DIM), lambda h: (0, 0)),
        ],
        out_shape=[
            jax.ShapeDtypeStruct((rows, 6 * HEAD_DIM), BF16),
            jax.ShapeDtypeStruct((TILE, 4 * HEAD_DIM), BF16),
            jax.ShapeDtypeStruct((TILE, 4 * HEAD_DIM), BF16),
        ],
        compiler_params=pltpu.CompilerParams(vmem_limit_bytes=40 * 1024 * 1024),
        cost_estimate=pl.CostEstimate(
            flops=2 * 4 * 2 * rows * 3 * TILE * HEAD_DIM,
            bytes_accessed=9 * 1024 * 1024,
            transcendentals=0,
        ),
        name="backward",
    )(x, x, x, before, before, after, after, pt, keep, recv)


def swapped(array, axis):
    return lax.ppermute(array, axis, [(0, 1), (1, 0)])


def crossed(array):
    return lax.ppermute(array, ("ylo", "yhi"), [(0, 0), (1, 2), (2, 1), (3, 3)])


def to_neighbours(down_part, up_part):
    count = lax.axis_size(SEQ)
    up = [(i, i + 1) for i in range(count - 1)]
    down = [(j, i) for i, j in up]
    return lax.ppermute(up_part, SEQ, up), lax.ppermute(down_part, SEQ, down)


def gathered_along_z(array):
    size = lax.axis_size("z")
    place = lax.axis_index("z")
    held = array[None]
    step = size // 2
    while step >= 1:
        other = lax.ppermute(held, "z", [(i, i ^ step) for i in range(size)])
        low = (place // step) % 2 == 0
        first = jnp.where(low, held, other)
        second = jnp.where(low, other, held)
        held = jnp.stack([first, second], axis=1).reshape((-1,) + array.shape)
        step //= 2
    return held


def per_device(queries, keys, values, out_grad, out_weight):
    ylo, core, yhi = (lax.axis_index(a) for a in ("ylo", "core", "yhi"))
    z_count = lax.axis_size("z")
    place = lax.axis_index(SEQ)
    groups = lax.axis_size(HEAD)
    across = lax.axis_size("x")
    width = 2 * HEAD_DIM
    rows_own = queries.shape[0]
    half = out_grad.shape[1] // 2

    packed = jnp.concatenate(
        [a.reshape(rows_own, groups, width) for a in (queries, keys, values)], axis=2
    ).transpose(1, 0, 2)
    x = lax.all_to_all(packed, HEAD, 0, 0, tiled=True).reshape(-1, 3 * width)
    rows = x.shape[0]

    w_part = gathered_along_z(crossed(out_weight))
    w_other = swapped(w_part, "ylo")
    own_is_low = core == 0
    w_pair = jnp.concatenate([w_part, w_other], axis=2)
    w_pair_other = swapped(w_pair, "core")
    w_first = jnp.where(own_is_low, w_pair, w_pair_other)
    w_second = jnp.where(own_is_low, w_pair_other, w_pair)
    w_all = jnp.stack([w_first, w_second], axis=1).reshape(half, 2 * width)
    same = ylo == yhi
    w_keep = jnp.where(same, w_all[:, :width], w_all[:, width:])
    w_send = jnp.where(same, w_all[:, width:], w_all[:, :width])

    og_keep = lax.dynamic_slice_in_dim(out_grad, yhi * half, half, 1)
    og_send = lax.dynamic_slice_in_dim(out_grad, (1 - yhi) * half, half, 1)
    og_other = swapped(og_send, "yhi")
    og_rows = jnp.concatenate(
        [jnp.where(yhi == 0, og_keep, og_other), jnp.where(yhi == 0, og_other, og_keep)], axis=0
    )
    og = lax.all_to_all(
        jnp.broadcast_to(og_rows[None], (across,) + og_rows.shape), "x", 0, 0, tiled=True
    ).reshape(rows, half)

    before, after = to_neighbours(x[:TILE, width:], x[rows - TILE :, width:])
    edge = jnp.stack([place == 0, place == lax.axis_size(SEQ) - 1])
    bias = jnp.where(edge, -1e30, 0.0).astype(F32)
    attn, pt = attention_forward(bias, x, before, after)
    attn_other = swapped(attn, "yhi")

    dout_send = jnp.dot(og, w_send, preferred_element_type=F32).astype(BF16)
    dout_recv = swapped(dout_send, "yhi")
    dout_keep = jnp.dot(og, w_keep, preferred_element_type=F32)

    attn_all = jnp.concatenate(
        [jnp.where(yhi == 0, attn, attn_other), jnp.where(yhi == 0, attn_other, attn)], axis=1
    )
    grad = lax.dot_general(og, attn_all, TN, preferred_element_type=F32)
    grad = grad.reshape(z_count, 2, -1, 2 * width)
    mine = lax.dynamic_index_in_dim(grad, core, 1, keepdims=False)
    other = lax.dynamic_index_in_dim(grad, 1 - core, 1, keepdims=False)
    grad = mine + swapped(other.astype(BF16), "core").astype(F32)
    mine = lax.dynamic_slice_in_dim(grad, ylo * width, width, 2)
    other = lax.dynamic_slice_in_dim(grad, (1 - ylo) * width, width, 2)
    grad = mine + swapped(other.astype(BF16), "ylo").astype(F32)
    grad = lax.all_to_all(grad.astype(BF16), "z", 0, 0, tiled=True)
    weight_grad = crossed(jnp.sum(grad.astype(F32), axis=0))

    dx, dx_before, dx_after = attention_backward(x, before, after, pt, dout_keep, dout_recv)
    from_left, from_right = to_neighbours(dx_before, dx_after)
    dx = dx.at[:TILE, width:].add(from_left)
    dx = dx.at[rows - TILE :, width:].add(from_right)
    dx = lax.all_to_all(dx.reshape(groups, rows_own, 3 * width), HEAD, 0, 0, tiled=True)
    dx = dx.transpose(1, 0, 2).reshape(rows_own, groups, 3, width)
    grads = [dx[:, :, n].reshape(rows_own, groups * width) for n in range(3)]
    return (*grads, weight_grad)


def solution(mesh):
    sizes = (2, mesh.shape["seq"] // 4, 2, mesh.shape["head"] // 2, 2)
    fine = Mesh(mesh.devices.reshape(sizes), ("ylo", "z", "core", "x", "yhi"))
    tokens = P((*SEQ, *HEAD), None)
    weight = P(SEQ, HEAD)
    return jax.shard_map(
        per_device,
        mesh=fine,
        in_specs=(tokens, tokens, tokens, tokens, weight),
        out_specs=(tokens, tokens, tokens, weight),
        check_vma=False,
    )
```

time: 539 us -> 236 us (0.44)
  waiting for transfers between devices: 379 us -> 49.6 us
  starting transfers between devices: 50.2 us -> 116 us
  matrix products: 26.2 us -> 9.06 us
  local copies, waits for them, and re-layouts: 48.9 us -> 33 us
  between operations: 14 us -> 1.26 us
  blocking collectives: 12.7 us -> 0 us
  Pallas kernels: 0 us -> 11.5 us
  other arithmetic: 6.58 us -> 13.4 us
    unnamed x4 -> x0, waiting for transfers between devices: 179 us -> none
    all_gather x2 -> x0, waiting for transfers between devices: 173 us -> none  [the longest x1 104 us: per_device(): grad_rows = lax.all_gather(out_grad, 'head', axis=0, tiled=True)]
    ppermute x4 -> x17, starting transfers between devices: 20 us -> 87.1 us  [the longest x4 32.2 us: gathered_along_z(): other = lax.ppermute(held, 'z', [(i, i ^ step) for i in range(size)])]
    ppermute x4 -> x17, waiting for transfers between devices: 2.82 us -> 32.1 us  [the longest x7 17.8 us: swapped(): return lax.ppermute(array, axis, [(0, 1), (1, 0)])]
    dynamic_update_slice x12 -> x0, local copies, waits for them, and re-layouts: 17.4 us -> none  [per_device(): lax.map(tile_pass, (grouped(query_tiles), grouped(dout_tiles), grouped(wi...]
    dot_general x14 -> x3, matrix products: 26.2 us -> 9.06 us  [the longest x1 3.83 us: per_device(): grad = lax.dot_general(og, attn_all, TN, preferred_element_type=F32)]
    all_to_all x1 -> x0, blocking collectives: 12.7 us -> none  [per_device(): lax.all_to_all(dk_total, 'head', split_axis=0, concat_axis=1, tiled=True)]
    pallas_call x0 -> x2, Pallas kernels: none -> 11.5 us  [the longest x1 5.83 us: attention_backward(): pl.pallas_call(backward_kernel, grid=(2,), in_specs=tile_specs(rows) + [p...]
  transfers between devices with their start and end apart: 12 -> 21, of which waited for: 9 -> 10; matrix products, arithmetic and copies ran while one was open for 4% -> 18% of each run, Pallas kernels for 0% -> 5%
where the time goes in v1:
time: 236 us; the launch traced here: 234 us
  starting transfers between devices  116 us (49%)
  waiting for transfers between devices  49.6 us (21%)
  local copies, waits for them, and re-layouts  33 us (14%)
  other arithmetic  13.4 us (6%)
  Pallas kernels  11.5 us (5%)
  matrix products  9.06 us (4%)
    ppermute x4, starting transfers between devices, gathered_along_z(): other = lax.ppermute(held, 'z', [(i, i ^ step) for i in range(size)])  32.2 us
    ppermute x4, starting transfers between devices, to_neighbours(): return (lax.ppermute(up_part, SEQ, up), lax.ppermute(down_part, SEQ, down))  29.8 us
    ppermute x7, starting transfers between devices, swapped(): return lax.ppermute(array, axis, [(0, 1), (1, 0)])  23.8 us
    ppermute x7, waiting for transfers between devices, swapped(): return lax.ppermute(array, axis, [(0, 1), (1, 0)])  17.8 us
    all_to_all x1, waiting for transfers between devices, per_device(): lax.all_to_all(dx.reshape(groups, rows_own, 3 * width), HEAD, 0, 0, tiled...  17.5 us
    all_to_all x1, starting transfers between devices, per_device(): grad = lax.all_to_all(grad.astype(BF16), 'z', 0, 0, tiled=True)  9.3 us
    unnamed x26, local copies, waits for them, and re-layouts  9.29 us
    ppermute x4, waiting for transfers between devices, gathered_along_z(): other = lax.ppermute(held, 'z', [(i, i ^ step) for i in range(size)])  8.87 us
  transfers between devices with their start and end apart: 21, of which 10 were waited for; matrix products, arithmetic and copies ran while one was open for 18% of the time, Pallas kernels for 5%

profile of v1, /device:TPU:24, one launch (start us, length us, event | category | flops | bytes accessed | tf_op | source)
XLA Modules:
  0.0 233.9 jit_solution(13023133080620719664)
XLA Ops:
  0.6 1.1 copy.97
  1.7 1.3 copy_bitcast_fusion
  3.0 1.3 maximum_bitcast_fusion
  4.3 7.4 %all-to-all-start = ((bf16[8,128,768]{2,1,0:T(8,128)(2,1)}), bf16[8,128,768]{2,1,0:T(8,128)(2,1)S(1)}, u32[]{:S(2)}, u32[]{:S(2)}) async-start(bf16[8,128,768]{2,1,0:T(8,128)(2,1)} %maximum_bitcast_fusion), calls=%async_computation | async-start | bytes 3145728 | tf_op jit(solution)/shard_map/all_to_all | solution.py:221
  11.7 1.9 collective-permute-start.2
  14.4 15.7 %collective-permute-start.4 = (bf16[1,48,256]{2,1,0:T(8,128)(2,1)S(1)}, bf16[1,48,256]{2,1,0:T(8,128)(2,1)S(1)}, u32[]{:S(2)}, u32[]{:S(2)}) collective-permute-start(bf16[1,48,256]{2,1,0:T(8,128)(2,1)S(1)} %bitcast.106), channel_id=1, source_target_pairs={{0,128},{16,144},{32,160},{48,176},{64,192},{80,208},{96,224},{112... | collective-permute-start | bytes 73736 | tf_op jit(solution)/shard_map/ppermute | solution.py:199
  30.1 1.8 collective-permute-done.4
  31.9 5.7 %collective-permute-done.2 = bf16[128,1536]{1,0:T(8,128)(2,1)S(1)} collective-permute-done((bf16[128,1536]{1,0:T(8,128)(2,1)S(1)}, bf16[128,1536]{1,0:T(8,128)(2,1)S(1)}, u32[]{:S(2)}, u32[]{:S(2)}) %collective-permute-start.2) | collective-permute-done | bytes 393248 | tf_op jit(solution)/shard_map/ppermute | solution.py:179
  38.1 1.9 broadcast_in_dim.19
  40.0 4.6 %all-to-all-start.1 = ((bf16[4,256,1536]{1,2,0:T(8,128)(2,1)}), bf16[4,256,1536]{1,2,0:T(8,128)(2,1)}, u32[]{:S(2)}, u32[]{:S(2)}) async-start(bf16[4,256,1536]{1,2,0:T(8,128)(2,1)} %broadcast_in_dim.19), calls=%async_computation.1 | async-start | bytes 6291456 | tf_op jit(solution)/shard_map/all_to_all | solution.py:242
  44.7 9.1 %collective-permute-start.5 = (bf16[2,48,256]{2,1,0:T(8,128)(2,1)S(1)}, bf16[2,48,256]{2,1,0:T(8,128)(2,1)S(1)}, u32[]{:S(2)}, u32[]{:S(2)}) collective-permute-start(bf16[2,48,256]{2,1,0:T(8,128)(2,1)S(1)} %maximum_bitcast_fusion.3), channel_id=1, source_target_pairs={{0,64},{16,80},{32,96},{48,112},{64,0},{80,16},{96,32},{112,48},{1... | collective-permute-start | bytes 147464 | tf_op jit(solution)/shard_map/ppermute | solution.py:199
  53.9 2.5 %collective-permute-done.5 = bf16[2,48,256]{2,1,0:T(8,128)(2,1)S(1)} collective-permute-done((bf16[2,48,256]{2,1,0:T(8,128)(2,1)S(1)}, bf16[2,48,256]{2,1,0:T(8,128)(2,1)S(1)}, u32[]{:S(2)}, u32[]{:S(2)}) %collective-permute-start.5) | collective-permute-done | bytes 49184 | tf_op jit(solution)/shard_map/ppermute | solution.py:199
  56.4 5.2 %collective-permute-start.6 = (bf16[4,48,256]{2,1,0:T(8,128)(2,1)S(1)}, bf16[4,48,256]{2,1,0:T(8,128)(2,1)S(1)}, u32[]{:S(2)}, u32[]{:S(2)}) collective-permute-start(bf16[4,48,256]{2,1,0:T(8,128)(2,1)S(1)} %bitcast.105), channel_id=1, source_target_pairs={{0,32},{16,48},{32,0},{48,16},{64,96},{80,112},{96,64},{112,80},{1... | collective-permute-start | bytes 294920 | tf_op jit(solution)/shard_map/ppermute | solution.py:199
  61.7 4.6 %collective-permute-done.6 = bf16[4,48,256]{2,1,0:T(8,128)(2,1)S(1)} collective-permute-done((bf16[4,48,256]{2,1,0:T(8,128)(2,1)S(1)}, bf16[4,48,256]{2,1,0:T(8,128)(2,1)S(1)}, u32[]{:S(2)}, u32[]{:S(2)}) %collective-permute-start.6) | collective-permute-done | bytes 98336 | tf_op jit(solution)/shard_map/ppermute | solution.py:199
  66.4 2.2 collective-permute-start.7
  68.6 1.9 collective-permute-start
  70.5 20.2 %collective-permute-start.1 = (bf16[256,512]{1,0:T(8,128)(2,1)S(1)}, bf16[256,512]{1,0:T(8,128)(2,1)S(1)}, u32[]{:S(2)}, u32[]{:S(2)}) collective-permute-start(bf16[256,512]{1,0:T(8,128)(2,1)S(1)} %get-tuple-element.67), channel_id=1, source_target_pairs={{8,0},{16,8},{24,16},{32,24},{40,32},{48,40},{56,48},{64,56},{72,6... | collective-permute-start | bytes 786440 | tf_op jit(solution)/shard_map/ppermute | solution.py:190
  90.9 3.0 %collective-permute-start.8 = (bf16[16,48,256]{2,1,0:T(8,128)(2,1)S(1)}, bf16[16,48,256]{2,1,0:T(8,128)(2,1)S(1)}, u32[]{:S(2)}, u32[]{:S(2)}) collective-permute-start(bf16[16,48,256]{2,1,0:T(8,128)(2,1)S(1)} %bitcast.91), channel_id=1, source_target_pairs={{0,256},{256,0},{1,257},{257,1},{2,258},{258,2},{3,259},{259,3},{4... | collective-permute-start | bytes 1179656 | tf_op jit(solution)/shard_map/ppermute | solution.py:179
  94.6 5.6 %forward.1 = (bf16[1024,256]{1,0:T(8,128)(2,1)S(1)}, bf16[2,4,768,256]{3,2,1,0:T(8,128)(2,1)S(1)}) custom-call(f32[2]{0:T(128)S(1)} %add_select_fusion.1.bias, bf16[1024,768]{1,0:T(8,128)(2,1)S(1)} %bitcast.80, bf16[1024,768]{1,0:T(8,128)(2,1)S(1)} %bitcast.81, bf16[1024,768]{1,0:T(8,128)(2,1)S(1)} %bitcast.82, ...), custom_call_target="tpu_custom_call" | custom-call | flops 805306368 | bytes 6291456 | tf_op jit(solution)/shard_map/forward/pallas_call | solution.py:124
  100.3 1.6 copy-done
  101.9 7.7 %collective-permute-start.13 = (bf16[1024,256]{1,0:T(8,128)(2,1)S(1)}, bf16[1024,256]{1,0:T(8,128)(2,1)}, u32[]{:S(2)}, u32[]{:S(2)}) collective-permute-start(bf16[1024,256]{1,0:T(8,128)(2,1)S(1)} %get-tuple-element.37), channel_id=1, source_target_pairs={{0,1},{1,0},{2,3},{3,2},{4,5},{5,4},{6,7},{7,6},{8,9},{9,8},{10,11... | collective-permute-start | bytes 1572872 | tf_op jit(solution)/shard_map/ppermute | solution.py:179
  110.6 2.2 collective-permute-start.9
  112.8 9.6 %collective-permute-done.13 = bf16[1024,256]{1,0:T(8,128)(2,1)} collective-permute-done((bf16[1024,256]{1,0:T(8,128)(2,1)S(1)}, bf16[1024,256]{1,0:T(8,128)(2,1)}, u32[]{:S(2)}, u32[]{:S(2)}) %collective-permute-start.13) | collective-permute-done | bytes 524320 | tf_op jit(solution)/shard_map/ppermute | solution.py:179
  122.3 2.1 broadcast_select_fusion.1
  124.4 4.6 %copy.80 = bf16[4,256,1536]{2,1,0:T(8,128)(2,1)} copy(bf16[4,256,1536]{1,2,0:T(8,128)(2,1)} %all-to-all-done.1) | data formatting | bytes 6291456 | tf_op jit(solution)/shard_map/all_to_all | solution.py:242
  129.0 4.7 %copy.86 = bf16[1536,1024]{1,0:T(8,128)(2,1)} copy(bf16[1536,1024]{0,1:T(8,128)(2,1)} %bitcast.87) | data formatting | bytes 6291456 | tf_op jit(solution)/shard_map/dot_general | solution.py:259
  133.7 3.8 %fusion = f32[16,2,48,512]{3,2,1,0:T(8,128)S(1)} fusion(bf16[16,2,48,1024]{3,2,1,0:T(8,128)(2,1)} %bitcast.94, bf16[1024,256]{1,0:T(8,128)(2,1)} %get-tuple-element.72, bf16[1024,256]{1,0:T(8,128)(2,1)S(1)} %copy-done.8), kind=kOutput, calls=%fused_computation.6 | convolution fusion | flops 1612709888 | bytes 7340032 | tf_op jit(solution)/shard_map/dot_general | solution.py:259
  137.6 1.7 copy-done.4
  140.3 1.9 collective-permute-start.14
  142.3 1.6 select_bitcast_fusion.1
  144.8 1.4 bitcast_add_fusion
  146.3 1.9 collective-permute-start.15
  148.6 2.3 copy-done.3
  150.9 1.8 convolution_convert_fusion
  152.6 5.1 %collective-permute-start.10 = (bf16[1024,256]{1,0:T(8,128)(2,1)}, bf16[1024,256]{1,0:T(8,128)(2,1)S(1)}, u32[]{:S(2)}, u32[]{:S(2)}) collective-permute-start(bf16[1024,256]{1,0:T(8,128)(2,1)} %convolution_convert_fusion), channel_id=1, source_target_pairs={{0,1},{1,0},{2,3},{3,2},{4,5},{5,4},{6,7},{7,6},{8,9},{9,8},{10,11... | collective-permute-start | bytes 1572872 | tf_op jit(solution)/shard_map/ppermute | solution.py:179
  157.8 1.6 collective-permute-done.15
  160.3 9.3 %all-to-all-start.3 = ((bf16[16,48,256]{2,1,0:T(8,128)(2,1)}), bf16[16,48,256]{2,1,0:T(8,128)(2,1)S(1)}, u32[]{:S(2)}, u32[]{:S(2)}) async-start(bf16[16,48,256]{2,1,0:T(8,128)(2,1)} %add_convert_fusion), calls=%async_computation.3 | async-start | bytes 786432 | tf_op jit(solution)/shard_map/all_to_all | solution.py:267
  169.6 3.5 %fusion.5.keep = f32[1024,256]{1,0:T(8,128)S(1)} fusion(bf16[1024,1536]{1,0:T(8,128)(2,1)} %bitcast.88, pred[]{:T(512)S(6)} %eq.38, bf16[1536,512]{1,0:T(8,128)(2,1)} %bitcast.100), kind=kOutput, calls=%fused_computation.16 | convolution fusion | flops 805699584 | bytes 5767169 | tf_op jit(solution)/shard_map/dot_general | solution.py:254
  173.1 5.8 %backward.1 = (bf16[1024,768]{1,0:T(8,128)(2,1)S(1)}, bf16[256,512]{1,0:T(8,128)(2,1)S(1)}, bf16[256,512]{1,0:T(8,128)(2,1)S(1)}) custom-call(bf16[1024,768]{1,0:T(8,128)(2,1)S(1)} %bitcast.83, bf16[1024,768]{1,0:T(8,128)(2,1)S(1)} %bitcast.84, bf16[1024,768]{1,0:T(8,128)(2,1)S(1)} %bitcast.85, bf16[256,512]{1,0:T(8,128)(2,1)S(1)} %collective-permute-done.kb.vb, ...), custom_call_target="tpu_custom_call" | custom-call | flops 1610612736 | bytes 9437184 | tf_op jit(solution)/shard_map/backward/pallas_call | solution.py:149
  178.9 1.9 collective-permute-start.11
  181.5 5.7 %collective-permute-start.12 = (bf16[256,512]{1,0:T(8,128)(2,1)S(1)}, bf16[256,512]{1,0:T(8,128)(2,1)S(1)}, u32[]{:S(2)}, u32[]{:S(2)}) collective-permute-start(bf16[256,512]{1,0:T(8,128)(2,1)S(1)} %get-tuple-element.36), channel_id=1, source_target_pairs={{8,0},{16,8},{24,16},{32,24},{40,32},{48,40},{56,48},{64,56},{72,6... | collective-permute-start | bytes 786440 | tf_op jit(solution)/shard_map/ppermute | solution.py:190
  187.8 4.8 %collective-permute-done.11 = bf16[256,512]{1,0:T(8,128)(2,1)S(1)} collective-permute-done((bf16[256,512]{1,0:T(8,128)(2,1)S(1)}, bf16[256,512]{1,0:T(8,128)(2,1)S(1)}, u32[]{:S(2)}, u32[]{:S(2)}) %collective-permute-start.11) | collective-permute-done | bytes 262176 | tf_op jit(solution)/shard_map/ppermute | solution.py:190
  192.6 2.1 add_select_fusion
  194.7 5.2 %scatter-add.6 = bf16[1024,768]{1,0:T(8,128)(2,1)} dynamic-update-slice(bf16[1024,768]{1,0:T(8,128)(2,1)} %copy-done.2, bf16[256,512]{1,0:T(8,128)(2,1)S(1)} %add_select_fusion, s32[]{:T(128)} %bitcast.22, s32[]{:T(128)} %bitcast.23) | dynamic-update-slice | bytes 524292 | tf_op jit(solution)/shard_map/scatter-add | solution.py:272
  199.9 1.7 fusion.13
  201.6 2.6 %copy.85 = bf16[8,128,768]{1,2,0:T(8,128)(2,1)} copy(bf16[8,128,768]{2,1,0:T(8,128)(2,1)} %bitcast.86) | data formatting | bytes 3145728 | tf_op jit(solution)/shard_map/reshape | solution.py:274
  204.2 7.7 %all-to-all-start.2 = ((bf16[8,128,768]{1,2,0:T(8,128)(2,1)}), bf16[8,128,768]{1,2,0:T(8,128)(2,1)S(1)}, u32[]{:S(2)}, u32[]{:S(2)}) async-start(bf16[8,128,768]{1,2,0:T(8,128)(2,1)} %copy.85), calls=%async_computation.2 | async-start | bytes 3145728 | tf_op jit(solution)/shard_map/all_to_all | solution.py:274
  212.7 17.5 %all-to-all-done.2 = bf16[8,128,768]{1,2,0:T(8,128)(2,1)S(1)} async-done(((bf16[8,128,768]{1,2,0:T(8,128)(2,1)}), bf16[8,128,768]{1,2,0:T(8,128)(2,1)S(1)}, u32[]{:S(2)}, u32[]{:S(2)}) %all-to-all-start.2) | async-done | bytes 1572896 | tf_op jit(solution)/shard_map/all_to_all | solution.py:274
  (65 shorter events, 12.1 us)
Async XLA Ops:
  4.3 7.4 %copy-start.7 = (bf16[128,3072]{1,0:T(8,128)(2,1)S(1)}, bf16[128,3072]{1,0:T(8,128)(2,1)}, u32[]{:S(2)}) copy-start(bf16[128,3072]{1,0:T(8,128)(2,1)} %param.12) | copy-start | bytes 2359300
  4.3 9.4 %copy-start.9 = (bf16[48,256]{1,0:T(8,128)(2,1)S(1)}, bf16[48,256]{1,0:T(8,128)(2,1)}, u32[]{:S(2)}) copy-start(bf16[48,256]{1,0:T(8,128)(2,1)} %param.13) | copy-start | bytes 73732
  4.3 33.8 %all-to-all-start = ((bf16[8,128,768]{2,1,0:T(8,128)(2,1)}), bf16[8,128,768]{2,1,0:T(8,128)(2,1)S(1)}, u32[]{:S(2)}, u32[]{:S(2)}) async-start(bf16[8,128,768]{2,1,0:T(8,128)(2,1)} %maximum_bitcast_fusion), calls=%async_computation | async-start | bytes 3145728 | tf_op jit(solution)/shard_map/all_to_all | solution.py:221
  11.7 25.9 %collective-permute-start.2 = (bf16[128,1536]{1,0:T(8,128)(2,1)S(1)}, bf16[128,1536]{1,0:T(8,128)(2,1)S(1)}, u32[]{:S(2)}, u32[]{:S(2)}) collective-permute-start(bf16[128,1536]{1,0:T(8,128)(2,1)S(1)} %constant_dynamic-slice_fusion), channel_id=1, source_target_pairs={{0,1},{1,0},{2,3},{3,2},{4,5},{5,4},{6,7},{7,6},{8,9},{9,8},{10,11... | collective-permute-start | bytes 1179656 | tf_op jit(solution)/shard_map/ppermute | solution.py:179
  13.7 0.7 collective-permute-start.3
  14.4 17.5 %collective-permute-start.4 = (bf16[1,48,256]{2,1,0:T(8,128)(2,1)S(1)}, bf16[1,48,256]{2,1,0:T(8,128)(2,1)S(1)}, u32[]{:S(2)}, u32[]{:S(2)}) collective-permute-start(bf16[1,48,256]{2,1,0:T(8,128)(2,1)S(1)} %bitcast.106), channel_id=1, source_target_pairs={{0,128},{16,144},{32,160},{48,176},{64,192},{80,208},{96,224},{112... | collective-permute-start | bytes 73736 | tf_op jit(solution)/shard_map/ppermute | solution.py:199
  40.0 84.4 %all-to-all-start.1 = ((bf16[4,256,1536]{1,2,0:T(8,128)(2,1)}), bf16[4,256,1536]{1,2,0:T(8,128)(2,1)}, u32[]{:S(2)}, u32[]{:S(2)}) async-start(bf16[4,256,1536]{1,2,0:T(8,128)(2,1)} %broadcast_in_dim.19), calls=%async_computation.1 | async-start | bytes 6291456 | tf_op jit(solution)/shard_map/all_to_all | solution.py:242
  44.7 11.7 %collective-permute-start.5 = (bf16[2,48,256]{2,1,0:T(8,128)(2,1)S(1)}, bf16[2,48,256]{2,1,0:T(8,128)(2,1)S(1)}, u32[]{:S(2)}, u32[]{:S(2)}) collective-permute-start(bf16[2,48,256]{2,1,0:T(8,128)(2,1)S(1)} %maximum_bitcast_fusion.3), channel_id=1, source_target_pairs={{0,64},{16,80},{32,96},{48,112},{64,0},{80,16},{96,32},{112,48},{1... | collective-permute-start | bytes 147464 | tf_op jit(solution)/shard_map/ppermute | solution.py:199
  56.4 9.9 %collective-permute-start.6 = (bf16[4,48,256]{2,1,0:T(8,128)(2,1)S(1)}, bf16[4,48,256]{2,1,0:T(8,128)(2,1)S(1)}, u32[]{:S(2)}, u32[]{:S(2)}) collective-permute-start(bf16[4,48,256]{2,1,0:T(8,128)(2,1)S(1)} %bitcast.105), channel_id=1, source_target_pairs={{0,32},{16,48},{32,0},{48,16},{64,96},{80,112},{96,64},{112,80},{1... | collective-permute-start | bytes 294920 | tf_op jit(solution)/shard_map/ppermute | solution.py:199
  66.4 24.4 %collective-permute-start.7 = (bf16[8,48,256]{2,1,0:T(8,128)(2,1)S(1)}, bf16[8,48,256]{2,1,0:T(8,128)(2,1)S(1)}, u32[]{:S(2)}, u32[]{:S(2)}) collective-permute-start(bf16[8,48,256]{2,1,0:T(8,128)(2,1)S(1)} %bitcast.101), channel_id=1, source_target_pairs={{0,16},{16,0},{32,48},{48,32},{64,80},{80,64},{96,112},{112,96},{1... | collective-permute-start | bytes 589832 | tf_op jit(solution)/shard_map/ppermute | solution.py:199
  68.6 25.3 %collective-permute-start = (bf16[256,512]{1,0:T(8,128)(2,1)S(1)}, bf16[256,512]{1,0:T(8,128)(2,1)S(1)}, u32[]{:S(2)}, u32[]{:S(2)}) collective-permute-start(bf16[256,512]{1,0:T(8,128)(2,1)S(1)} %get-tuple-element.68), channel_id=1, source_target_pairs={{0,8},{8,16},{16,24},{24,32},{32,40},{40,48},{48,56},{56,64},{64,7... | collective-permute-start | bytes 786440 | tf_op jit(solution)/shard_map/ppermute | solution.py:190
  70.5 24.1 %collective-permute-start.1 = (bf16[256,512]{1,0:T(8,128)(2,1)S(1)}, bf16[256,512]{1,0:T(8,128)(2,1)S(1)}, u32[]{:S(2)}, u32[]{:S(2)}) collective-permute-start(bf16[256,512]{1,0:T(8,128)(2,1)S(1)} %get-tuple-element.67), channel_id=1, source_target_pairs={{8,0},{16,8},{24,16},{32,24},{40,32},{48,40},{56,48},{64,56},{72,6... | collective-permute-start | bytes 786440 | tf_op jit(solution)/shard_map/ppermute | solution.py:190
  90.9 18.7 %collective-permute-start.8 = (bf16[16,48,256]{2,1,0:T(8,128)(2,1)S(1)}, bf16[16,48,256]{2,1,0:T(8,128)(2,1)S(1)}, u32[]{:S(2)}, u32[]{:S(2)}) collective-permute-start(bf16[16,48,256]{2,1,0:T(8,128)(2,1)S(1)} %bitcast.91), channel_id=1, source_target_pairs={{0,256},{256,0},{1,257},{257,1},{2,258},{258,2},{3,259},{259,3},{4... | collective-permute-start | bytes 1179656 | tf_op jit(solution)/shard_map/ppermute | solution.py:179
  100.3 1.6 copy-start
  101.9 20.4 %collective-permute-start.13 = (bf16[1024,256]{1,0:T(8,128)(2,1)S(1)}, bf16[1024,256]{1,0:T(8,128)(2,1)}, u32[]{:S(2)}, u32[]{:S(2)}) collective-permute-start(bf16[1024,256]{1,0:T(8,128)(2,1)S(1)} %get-tuple-element.37), channel_id=1, source_target_pairs={{0,1},{1,0},{2,3},{3,2},{4,5},{5,4},{6,7},{7,6},{8,9},{9,8},{10,11... | collective-permute-start | bytes 1572872 | tf_op jit(solution)/shard_map/ppermute | solution.py:179
  110.6 31.6 %collective-permute-start.9 = (bf16[16,48,512]{2,1,0:T(8,128)(2,1)}, bf16[16,48,512]{2,1,0:T(8,128)(2,1)}, u32[]{:S(2)}, u32[]{:S(2)}) collective-permute-start(bf16[16,48,512]{2,1,0:T(8,128)(2,1)} %pad_maximum_fusion.2), channel_id=1, source_target_pairs={{0,8},{8,0},{1,9},{9,1},{2,10},{10,2},{3,11},{11,3},{4,12},{12,4},... | collective-permute-start | bytes 2359304 | tf_op jit(solution)/shard_map/ppermute | solution.py:179
  129.0 4.7 %copy-start.8 = (bf16[1024,256]{1,0:T(8,128)(2,1)S(1)}, bf16[1024,256]{1,0:T(8,128)(2,1)}, u32[]{:S(2)}) copy-start(bf16[1024,256]{1,0:T(8,128)(2,1)} %get-tuple-element.71) | copy-start | bytes 1572868
  137.6 1.7 copy-start.4
  140.3 4.5 %collective-permute-start.14 = (bf16[16,48,512]{2,1,0:T(8,128)(2,1)}, bf16[16,48,512]{2,1,0:T(8,128)(2,1)}, u32[]{:S(2)}, u32[]{:S(2)}) collective-permute-start(bf16[16,48,512]{2,1,0:T(8,128)(2,1)} %fusion.3), channel_id=1, source_target_pairs={{0,8},{8,0},{1,9},{9,1},{2,10},{10,2},{3,11},{11,3},{4,12},{12,4},... | collective-permute-start | bytes 2359304 | tf_op jit(solution)/shard_map/ppermute | solution.py:179
  142.2 2.6 %copy-start.5 = (f32[16,2,48,512]{3,2,1,0:T(8,128)S(1)}, f32[16,2,48,512]{3,2,1,0:T(8,128)}, u32[]{:S(2)}) copy-start(f32[16,2,48,512]{3,2,1,0:T(8,128)} %copy-done.4) | copy-start | bytes 9437188
  146.3 13.1 %collective-permute-start.15 = (bf16[16,48,256]{2,1,0:T(8,128)(2,1)S(1)}, bf16[16,48,256]{2,1,0:T(8,128)(2,1)S(1)}, u32[]{:S(2)}, u32[]{:S(2)}) collective-permute-start(bf16[16,48,256]{2,1,0:T(8,128)(2,1)S(1)} %dynamic-slice_convert_fusion.1), channel_id=1, source_target_pairs={{0,256},{256,0},{1,257},{257,1},{2,258},{258,2},{3,259},{259,3},{4... | collective-permute-start | bytes 1179656 | tf_op jit(solution)/shard_map/ppermute | solution.py:179
  148.4 2.5 %copy-start.3 = (bf16[4,256,1536]{2,1,0:T(8,128)(2,1)S(1)}, bf16[4,256,1536]{2,1,0:T(8,128)(2,1)}, u32[]{:S(2)}) copy-start(bf16[4,256,1536]{2,1,0:T(8,128)(2,1)} %copy.80) | copy-start | bytes 9437188
  148.6 4.1 %copy-start.6 = (bf16[16,2,48,512]{3,2,1,0:T(8,128)(2,1)}, bf16[16,2,48,512]{3,2,1,0:T(8,128)(2,1)S(1)}, u32[]{:S(2)}) copy-start(bf16[16,2,48,512]{3,2,1,0:T(8,128)(2,1)S(1)} %copy.84) | copy-start | bytes 4718596
  152.6 20.4 %collective-permute-start.10 = (bf16[1024,256]{1,0:T(8,128)(2,1)}, bf16[1024,256]{1,0:T(8,128)(2,1)S(1)}, u32[]{:S(2)}, u32[]{:S(2)}) collective-permute-start(bf16[1024,256]{1,0:T(8,128)(2,1)} %convolution_convert_fusion), channel_id=1, source_target_pairs={{0,1},{1,0},{2,3},{3,2},{4,5},{5,4},{6,7},{7,6},{8,9},{9,8},{10,11... | collective-permute-start | bytes 1572872 | tf_op jit(solution)/shard_map/ppermute | solution.py:179
  160.3 44.0 %all-to-all-start.3 = ((bf16[16,48,256]{2,1,0:T(8,128)(2,1)}), bf16[16,48,256]{2,1,0:T(8,128)(2,1)S(1)}, u32[]{:S(2)}, u32[]{:S(2)}) async-start(bf16[16,48,256]{2,1,0:T(8,128)(2,1)} %add_convert_fusion), calls=%async_computation.3 | async-start | bytes 786432 | tf_op jit(solution)/shard_map/all_to_all | solution.py:267
  169.6 3.5 %copy-start.1 = (bf16[2,4,768,256]{3,2,1,0:T(8,128)(2,1)S(1)}, bf16[2,4,768,256]{3,2,1,0:T(8,128)(2,1)}, u32[]{:S(2)}) copy-start(bf16[2,4,768,256]{3,2,1,0:T(8,128)(2,1)} %copy-done) | copy-start | bytes 9437188
  173.1 7.8 %copy-start.10 = (s32[2]{0:T(128)S(1)}, s32[2]{0:T(128)}, u32[]{:S(2)}) copy-start(s32[2]{0:T(128)} %constant.151.clone.1) | copy-start | bytes 28
  178.9 13.7 %copy-start.2 = (bf16[1024,768]{1,0:T(8,128)(2,1)}, bf16[1024,768]{1,0:T(8,128)(2,1)S(1)}, u32[]{:S(2)}) copy-start(bf16[1024,768]{1,0:T(8,128)(2,1)S(1)} %get-tuple-element.34) | copy-start | bytes 4718596
  178.9 13.7 %collective-permute-start.11 = (bf16[256,512]{1,0:T(8,128)(2,1)S(1)}, bf16[256,512]{1,0:T(8,128)(2,1)S(1)}, u32[]{:S(2)}, u32[]{:S(2)}) collective-permute-start(bf16[256,512]{1,0:T(8,128)(2,1)S(1)} %get-tuple-element.35), channel_id=1, source_target_pairs={{0,8},{8,16},{16,24},{24,32},{32,40},{40,48},{48,56},{56,64},{64,7... | collective-permute-start | bytes 786440 | tf_op jit(solution)/shard_map/ppermute | solution.py:190
  181.5 18.4 %collective-permute-start.12 = (bf16[256,512]{1,0:T(8,128)(2,1)S(1)}, bf16[256,512]{1,0:T(8,128)(2,1)S(1)}, u32[]{:S(2)}, u32[]{:S(2)}) collective-permute-start(bf16[256,512]{1,0:T(8,128)(2,1)S(1)} %get-tuple-element.36), channel_id=1, source_target_pairs={{8,0},{16,8},{24,16},{32,24},{40,32},{48,40},{56,48},{64,56},{72,6... | collective-permute-start | bytes 786440 | tf_op jit(solution)/shard_map/ppermute | solution.py:190
  204.2 25.9 %all-to-all-start.2 = ((bf16[8,128,768]{1,2,0:T(8,128)(2,1)}), bf16[8,128,768]{1,2,0:T(8,128)(2,1)S(1)}, u32[]{:S(2)}, u32[]{:S(2)}) async-start(bf16[8,128,768]{1,2,0:T(8,128)(2,1)} %copy.85), calls=%async_computation.2 | async-start | bytes 3145728 | tf_op jit(solution)/shard_map/all_to_all | solution.py:274
  212.0 21.3 %collective-permute-start.16 = (f32[48,256]{1,0:T(8,128)S(1)}, f32[48,256]{1,0:T(8,128)S(1)}, u32[]{:S(2)}, u32[]{:S(2)}) collective-permute-start(f32[48,256]{1,0:T(8,128)S(1)} %convert_reduce_fusion), channel_id=1, source_target_pairs={{0,0},{1,256},{256,1},{257,257},{2,2},{3,258},{258,3},{259,259},{4... | collective-permute-start | bytes 147464 | tf_op jit(solution)/shard_map/ppermute | solution.py:183

commit v2 on v1

--- a/solution.py
+++ b/solution.py
@@ -175,12 +175,220 @@
     )(x, x, x, before, before, after, after, pt, keep, recv)
 
 
+def pack_kernel(q, k, v, out):
+    width = 2 * HEAD_DIM
+    for g in range(out.shape[0]):
+        for n, ref in enumerate((q, k, v)):
+            out[g, :, n * width : (n + 1) * width] = ref[:, g * width : (g + 1) * width]
+
+
+def pack(q, k, v):
+    rows, full = q.shape
+    width = 2 * HEAD_DIM
+    groups = full // width
+    part = pl.BlockSpec((rows, 2 * width), lambda i: (0, i))
+    return pl.pallas_call(
+        pack_kernel,
+        grid=(groups // 2,),
+        in_specs=[part] * 3,
+        out_specs=pl.BlockSpec((2, rows, 3 * width), lambda i: (i, 0, 0)),
+        out_shape=jax.ShapeDtypeStruct((groups, rows, 3 * width), BF16),
+        cost_estimate=pl.CostEstimate(flops=0, bytes_accessed=3 << 20, transcendentals=0),
+        name="pack",
+    )(q, k, v)
+
+
+def unpack_kernel(dx, q, k, v):
+    width = 2 * HEAD_DIM
+    for g in range(dx.shape[0]):
+        for n, ref in enumerate((q, k, v)):
+            ref[:, g * width : (g + 1) * width] = dx[g, :, n * width : (n + 1) * width]
+
+
+def unpack(dx):
+    groups, rows, _ = dx.shape
+    width = 2 * HEAD_DIM
+    part = pl.BlockSpec((rows, 2 * width), lambda i: (0, i))
+    return pl.pallas_call(
+        unpack_kernel,
+        grid=(groups // 2,),
+        in_specs=[pl.BlockSpec((2, rows, 3 * width), lambda i: (i, 0, 0))],
+        out_specs=[part] * 3,
+        out_shape=[jax.ShapeDtypeStruct((rows, groups * width), BF16)] * 3,
+        cost_estimate=pl.CostEstimate(flops=0, bytes_accessed=3 << 20, transcendentals=0),
+        name="unpack",
+    )(dx)
+
+
+def copies_kernel(yhi, own, other, after, out):
+    rows = own.shape[0]
+    out[0, pl.ds(pl.multiple_of(yhi[0] * rows, rows), rows), :] = own[...]
+    out[0, pl.ds(pl.multiple_of((1 - yhi[0]) * rows, rows), rows), :] = other[...]
+
+
+def copies(yhi, out_grad, other, after, count):
+    rows, half = other.shape
+    return pl.pallas_call(
+        copies_kernel,
+        grid_spec=pltpu.PrefetchScalarGridSpec(
+            num_scalar_prefetch=1,
+            grid=(count,),
+            in_specs=[
+                pl.BlockSpec((rows, half), lambda i, y: (0, y[0])),
+                pl.BlockSpec((rows, half), lambda i, y: (0, 0)),
+                pl.BlockSpec(memory_space=pl.ANY),
+            ],
+            out_specs=pl.BlockSpec((1, 2 * rows, half), lambda i, y: (i, 0, 0)),
+        ),
+        out_shape=jax.ShapeDtypeStruct((count, 2 * rows, half), BF16),
+        cost_estimate=pl.CostEstimate(flops=0, bytes_accessed=5 << 20, transcendentals=0),
+        name="copies",
+    )(yhi, out_grad, other, after)
+
+
+def reversed_bits(value, size):
+    bits = size.bit_length() - 1
+    out = 0
+    for b in range(bits):
+        out = out + ((value >> b) & 1) * (1 << (bits - 1 - b))
+    return out
+
+
+def dout_kernel(where, og, own_near, own_far, other_near, other_far, keep, send, weight):
+    size, rows, width = own_near.shape
+
+    @pl.when(pl.program_id(0) == 0)
+    def _():
+        near = pl.ds(pl.multiple_of((1 - where[2]) * width, width), width)
+        far = pl.ds(pl.multiple_of(where[2] * width, width), width)
+        own = where[1] * rows
+        for n in range(size):
+            at = reversed_bits(jnp.bitwise_xor(where[0], n), size)
+            first = pl.ds(pl.multiple_of(2 * n * rows + own, rows), rows)
+            second = pl.ds(pl.multiple_of((2 * n + 1) * rows - own, rows), rows)
+            weight[first, near] = own_near[at]
+            weight[first, far] = own_far[at]
+            weight[second, near] = other_near[at]
+            weight[second, far] = other_far[at]
+
+    out = jnp.dot(og[...], weight[...], preferred_element_type=F32)
+    keep[...] = out[:, :width]
+    send[...] = out[:, width:].astype(BF16)
+
+
+def dout_parts(where, og, parts):
+    rows, half = og.shape
+    size, depth, width = parts[0].shape
+    block = rows // 4
+    whole = pl.BlockSpec((size, depth, width), lambda i, w: (0, 0, 0))
+    return pl.pallas_call(
+        dout_kernel,
+        grid_spec=pltpu.PrefetchScalarGridSpec(
+            num_scalar_prefetch=1,
+            grid=(4,),
+            in_specs=[pl.BlockSpec((block, half), lambda i, w: (i, 0))] + [whole] * 4,
+            out_specs=[pl.BlockSpec((block, width), lambda i, w: (i, 0))] * 2,
+            scratch_shapes=[pltpu.VMEM((half, 2 * width), BF16)],
+        ),
+        out_shape=[
+            jax.ShapeDtypeStruct((rows, width), F32),
+            jax.ShapeDtypeStruct((rows, width), BF16),
+        ],
+        compiler_params=pltpu.CompilerParams(vmem_limit_bytes=40 * 1024 * 1024),
+        cost_estimate=pl.CostEstimate(
+            flops=2 * rows * half * 2 * width, bytes_accessed=7 << 20, transcendentals=0
+        ),
+        name="dout",
+    )(where, og, *parts)
+
+
+def projection_kernel(where, og, attn, attn_other, after, mine, other, total):
+    depth = mine.shape[1]
+    width = attn.shape[1]
+    near = pl.ds(pl.multiple_of((1 - where[2]) * width, width), width)
+    far = pl.ds(pl.multiple_of(where[2] * width, width), width)
+    total[:, near] = lax.dot_general(og[...], attn[...], TN, preferred_element_type=F32)
+    total[:, far] = lax.dot_general(og[...], attn_other[...], TN, preferred_element_type=F32)
+    own = where[1] * depth
+    for n in range(mine.shape[0]):
+        first = pl.ds(pl.multiple_of(2 * n * depth + own, depth), depth)
+        second = pl.ds(pl.multiple_of((2 * n + 1) * depth - own, depth), depth)
+        mine[n] = total[first, :]
+        other[n] = total[second, :].astype(BF16)
+
+
+def projection_grad(where, og, attn, attn_other, after, size):
+    rows, half = og.shape
+    width = attn.shape[1]
+    depth = half // (2 * size)
+    steps = 4
+    whole = pl.BlockSpec((rows, width), lambda i, w: (0, 0))
+    part = pl.BlockSpec((size // steps, depth, 2 * width), lambda i, w: (i, 0, 0))
+    return pl.pallas_call(
+        projection_kernel,
+        grid_spec=pltpu.PrefetchScalarGridSpec(
+            num_scalar_prefetch=1,
+            grid=(steps,),
+            in_specs=[pl.BlockSpec((rows, half // steps), lambda i, w: (0, i)), whole, whole]
+            + [pl.BlockSpec(memory_space=pl.ANY)],
+            out_specs=[part, part],
+            scratch_shapes=[pltpu.VMEM((half // steps, 2 * width), F32)],
+        ),
+        out_shape=[
+            jax.ShapeDtypeStruct((size, depth, 2 * width), F32),
+            jax.ShapeDtypeStruct((size, depth, 2 * width), BF16),
+        ],
+        compiler_params=pltpu.CompilerParams(vmem_limit_bytes=40 * 1024 * 1024),
+        cost_estimate=pl.CostEstimate(
+            flops=2 * rows * half * 2 * width, bytes_accessed=7 << 20, transcendentals=0
+        ),
+        name="projection",
+    )(where, og, attn, attn_other, after)
+
+
+def edges_kernel(dx, low, high, out):
+    width = 2 * HEAD_DIM
+    out[:, :width] = dx[:, :width]
+    added = jnp.where(pl.program_id(0) == 0, low[...].astype(F32), high[...].astype(F32))
+    out[:, width:] = (dx[:, width:].astype(F32) + added).astype(BF16)
+
+
+def add_edges(dx, low, high):
+    rows, full = dx.shape
+    last = rows // TILE - 1
+    part = pl.BlockSpec((TILE, full), lambda i: (i * last, 0))
+    edge = pl.BlockSpec(low.shape, lambda i: (0, 0))
+    return pl.pallas_call(
+        edges_kernel,
+        grid=(2,),
+        in_specs=[part, edge, edge],
+        out_specs=part,
+        out_shape=jax.ShapeDtypeStruct(dx.shape, BF16),
+        input_output_aliases={0: 0},
+        cost_estimate=pl.CostEstimate(flops=0, bytes_accessed=2 << 20, transcendentals=0),
+        name="edges",
+    )(dx, low, high)
+
+
 def swapped(array, axis):
     return lax.ppermute(array, axis, [(0, 1), (1, 0)])
 
 
-def crossed(array):
-    return lax.ppermute(array, ("ylo", "yhi"), [(0, 0), (1, 2), (2, 1), (3, 3)])
+Y = ("ylo", "yhi")
+FAR = [(2, 0), (1, 3), (0, 1), (3, 2)]
+NEAR = [(1, 2), (2, 1)]
+
+
+def from_owners(block, same):
+    far = lax.ppermute(block, Y, [(j, i) for i, j in FAR])
+    near = lax.ppermute(block, Y, NEAR)
+    return jnp.where(same, block, near), far
+
+
+def to_owners(near, far, same):
+    from_far = lax.ppermute(far.astype(BF16), Y, FAR).astype(F32)
+    from_near = lax.ppermute(near.astype(BF16), Y, NEAR).astype(F32)
+    return jnp.where(same, near, from_near) + from_far
 
 
 def to_neighbours(down_part, up_part):
@@ -190,23 +398,31 @@
     return lax.ppermute(up_part, SEQ, up), lax.ppermute(down_part, SEQ, down)
 
 
-def gathered_along_z(array):
+def gathered_along_z(held, steps):
+    size = lax.axis_size("z")
+    for step in steps:
+        other = lax.ppermute(held, "z", [(i, i ^ step) for i in range(size)])
+        held = jnp.concatenate([held, other], axis=0)
+    return held
+
+
+def reduced_along_z(array):
     size = lax.axis_size("z")
     place = lax.axis_index("z")
-    held = array[None]
-    step = size // 2
-    while step >= 1:
-        other = lax.ppermute(held, "z", [(i, i ^ step) for i in range(size)])
-        low = (place // step) % 2 == 0
-        first = jnp.where(low, held, other)
-        second = jnp.where(low, other, held)
-        held = jnp.stack([first, second], axis=1).reshape((-1,) + array.shape)
-        step //= 2
-    return held
+    step = 1
+    while step < size:
+        halves = array.reshape((-1, 2) + array.shape[1:])
+        bit = (place // step) % 2
+        own = lax.dynamic_index_in_dim(halves, bit, 1, keepdims=False)
+        send = lax.dynamic_index_in_dim(halves, 1 - bit, 1, keepdims=False)
+        other = lax.ppermute(send.astype(BF16), "z", [(i, i ^ step) for i in range(size)])
+        array = own + other.astype(F32)
+        step *= 2
+    return array[0]
 
 
 def per_device(queries, keys, values, out_grad, out_weight):
-    ylo, core, yhi = (lax.axis_index(a) for a in ("ylo", "core", "yhi"))
+    ylo, z, core, yhi = (lax.axis_index(a) for a in ("ylo", "z", "core", "yhi"))
     z_count = lax.axis_size("z")
     place = lax.axis_index(SEQ)
     groups = lax.axis_size(HEAD)
@@ -214,34 +430,24 @@
     width = 2 * HEAD_DIM
     rows_own = queries.shape[0]
     half = out_grad.shape[1] // 2
-
-    packed = jnp.concatenate(
-        [a.reshape(rows_own, groups, width) for a in (queries, keys, values)], axis=2
-    ).transpose(1, 0, 2)
-    x = lax.all_to_all(packed, HEAD, 0, 0, tiled=True).reshape(-1, 3 * width)
+    same = ylo == yhi
+    where = jnp.stack([z, core, same.astype(jnp.int32)]).astype(jnp.int32)
+
+    x = lax.all_to_all(pack(queries, keys, values), HEAD, 0, 0, tiled=True)
+    x = x.reshape(-1, 3 * width)
     rows = x.shape[0]
 
-    w_part = gathered_along_z(crossed(out_weight))
-    w_other = swapped(w_part, "ylo")
-    own_is_low = core == 0
-    w_pair = jnp.concatenate([w_part, w_other], axis=2)
-    w_pair_other = swapped(w_pair, "core")
-    w_first = jnp.where(own_is_low, w_pair, w_pair_other)
-    w_second = jnp.where(own_is_low, w_pair_other, w_pair)
-    w_all = jnp.stack([w_first, w_second], axis=1).reshape(half, 2 * width)
-    same = ylo == yhi
-    w_keep = jnp.where(same, w_all[:, :width], w_all[:, width:])
-    w_send = jnp.where(same, w_all[:, width:], w_all[:, :width])
-
-    og_keep = lax.dynamic_slice_in_dim(out_grad, yhi * half, half, 1)
+    steps = [z_count >> (n + 1) for n in range(z_count.bit_length() - 1)]
+    blocks = gathered_along_z(out_weight[None], steps[:3])
+
     og_send = lax.dynamic_slice_in_dim(out_grad, (1 - yhi) * half, half, 1)
     og_other = swapped(og_send, "yhi")
-    og_rows = jnp.concatenate(
-        [jnp.where(yhi == 0, og_keep, og_other), jnp.where(yhi == 0, og_other, og_keep)], axis=0
-    )
-    og = lax.all_to_all(
-        jnp.broadcast_to(og_rows[None], (across,) + og_rows.shape), "x", 0, 0, tiled=True
-    ).reshape(rows, half)
+    sent = copies(yhi[None].astype(jnp.int32), out_grad, og_other, blocks, across)
+    og = lax.all_to_all(sent, "x", 0, 0, tiled=True).reshape(rows, half)
+
+    own_near, own_far = from_owners(gathered_along_z(blocks, steps[3:]), same)
+    other_near = swapped(own_near, "core")
+    other_far = swapped(own_far, "core")
 
     before, after = to_neighbours(x[:TILE, width:], x[rows - TILE :, width:])
     edge = jnp.stack([place == 0, place == lax.axis_size(SEQ) - 1])
@@ -249,32 +455,18 @@
     attn, pt = attention_forward(bias, x, before, after)
     attn_other = swapped(attn, "yhi")
 
-    dout_send = jnp.dot(og, w_send, preferred_element_type=F32).astype(BF16)
+    dout_keep, dout_send = dout_parts(where, og, (own_near, own_far, other_near, other_far))
     dout_recv = swapped(dout_send, "yhi")
-    dout_keep = jnp.dot(og, w_keep, preferred_element_type=F32)
-
-    attn_all = jnp.concatenate(
-        [jnp.where(yhi == 0, attn, attn_other), jnp.where(yhi == 0, attn_other, attn)], axis=1
-    )
-    grad = lax.dot_general(og, attn_all, TN, preferred_element_type=F32)
-    grad = grad.reshape(z_count, 2, -1, 2 * width)
-    mine = lax.dynamic_index_in_dim(grad, core, 1, keepdims=False)
-    other = lax.dynamic_index_in_dim(grad, 1 - core, 1, keepdims=False)
-    grad = mine + swapped(other.astype(BF16), "core").astype(F32)
-    mine = lax.dynamic_slice_in_dim(grad, ylo * width, width, 2)
-    other = lax.dynamic_slice_in_dim(grad, (1 - ylo) * width, width, 2)
-    grad = mine + swapped(other.astype(BF16), "ylo").astype(F32)
-    grad = lax.all_to_all(grad.astype(BF16), "z", 0, 0, tiled=True)
-    weight_grad = crossed(jnp.sum(grad.astype(F32), axis=0))
+
+    mine, other = projection_grad(where, og, attn, attn_other, dout_send, z_count)
+    grad = mine + swapped(other, "core").astype(F32)
+    weight_grad = reduced_along_z(to_owners(grad[:, :, :width], grad[:, :, width:], same))
 
     dx, dx_before, dx_after = attention_backward(x, before, after, pt, dout_keep, dout_recv)
     from_left, from_right = to_neighbours(dx_before, dx_after)
-    dx = dx.at[:TILE, width:].add(from_left)
-    dx = dx.at[rows - TILE :, width:].add(from_right)
+    dx = add_edges(dx, from_left, from_right)
     dx = lax.all_to_all(dx.reshape(groups, rows_own, 3 * width), HEAD, 0, 0, tiled=True)
-    dx = dx.transpose(1, 0, 2).reshape(rows_own, groups, 3, width)
-    grads = [dx[:, :, n].reshape(rows_own, groups * width) for n in range(3)]
-    return (*grads, weight_grad)
+    return (*unpack(dx), weight_grad)
 
 
 def solution(mesh):

time: 236 us -> 212 us (0.90)
  Pallas kernels: 11.5 us -> 37 us
  local copies, waits for them, and re-layouts: 33 us -> 17.1 us
  starting transfers between devices: 116 us -> 104 us
  other arithmetic: 13.4 us -> 4.17 us
  matrix products: 9.06 us -> 0 us
  waiting for transfers between devices: 49.6 us -> 46.7 us
    ppermute x2 -> x8, starting transfers between devices: 1.33 us -> 30.1 us  [the longest x4 16.4 us: reduced_along_z(): lax.ppermute(send.astype(BF16), 'z', [(i, i ^ step) for i in range(size)])]
    pallas_call x0 -> x6, Pallas kernels: none -> 23.5 us  [the longest x1 5.6 us: dout_parts(): pl.pallas_call(dout_kernel, grid_spec=pltpu.PrefetchScalarGridSpec(num_sc...]
    all_to_all x1, waiting for transfers between devices: 17.5 us -> 0.01 us  [per_device(): lax.all_to_all(dx.reshape(groups, rows_own, 3 * width), HEAD, 0, 0, tiled...]
    ppermute x2 -> x8, waiting for transfers between devices: 0.01 us -> 17.3 us  [the longest x4 17.3 us: reduced_along_z(): lax.ppermute(send.astype(BF16), 'z', [(i, i ^ step) for i in range(size)])]
    ppermute x4, starting transfers between devices: 29.8 us -> 15.3 us  [to_neighbours(): return (lax.ppermute(up_part, SEQ, up), lax.ppermute(down_part, SEQ, down))]
    ppermute x7 -> x6, starting transfers between devices: 23.8 us -> 12.3 us  [swapped(): return lax.ppermute(array, axis, [(0, 1), (1, 0)])]
    dot_general x3 -> x0, matrix products: 9.06 us -> none  [the longest x1 3.83 us: per_device(): grad = lax.dot_general(og, attn_all, TN, preferred_element_type=F32)]
    all_to_all x3 -> x2, starting transfers between devices: 21.3 us -> 12.4 us  [the longest x1 7.39 us: per_device(): x = lax.all_to_all(pack(queries, keys, values), HEAD, 0, 0, tiled=True)]
  transfers between devices with their start and end apart: 21 -> 25, of which waited for: 10 -> 8; matrix products, arithmetic and copies ran while one was open for 18% -> 5% of each run, Pallas kernels for 5% -> 12%
where the time goes in v2:
time: 212 us; the launch traced here: 210 us
  starting transfers between devices  104 us (49%)
  waiting for transfers between devices  46.7 us (22%)
  Pallas kernels  37 us (17%)
  local copies, waits for them, and re-layouts  17.1 us (8%)
  other arithmetic  4.17 us (2%)
    ppermute x4, starting transfers between devices, gathered_along_z(): other = lax.ppermute(held, 'z', [(i, i ^ step) for i in range(size)])  25.9 us
    ppermute x4, waiting for transfers between devices, reduced_along_z(): lax.ppermute(send.astype(BF16), 'z', [(i, i ^ step) for i in range(size)])  17.3 us
    ppermute x4, starting transfers between devices, reduced_along_z(): lax.ppermute(send.astype(BF16), 'z', [(i, i ^ step) for i in range(size)])  16.4 us
    ppermute x4, starting transfers between devices, to_neighbours(): return (lax.ppermute(up_part, SEQ, up), lax.ppermute(down_part, SEQ, down))  15.3 us
    ppermute x4, waiting for transfers between devices, gathered_along_z(): other = lax.ppermute(held, 'z', [(i, i ^ step) for i in range(size)])  14.9 us
    ppermute x6, waiting for transfers between devices, swapped(): return lax.ppermute(array, axis, [(0, 1), (1, 0)])  14.5 us
    unnamed x36, local copies, waits for them, and re-layouts  13.9 us
    ppermute x6, starting transfers between devices, swapped(): return lax.ppermute(array, axis, [(0, 1), (1, 0)])  12.3 us
  transfers between devices with their start and end apart: 25, of which 8 were waited for; matrix products, arithmetic and copies ran while one was open for 5% of the time, Pallas kernels for 12%

profile of v2, /device:TPU:24, one launch (start us, length us, event | category | flops | bytes accessed | tf_op | source)
XLA Modules:
  0.0 209.9 jit_solution(13171309202343621791)
XLA Ops:
  0.6 3.7 %pack.1 = bf16[8,128,768]{2,1,0:T(8,128)(2,1)} custom-call(bf16[128,2048]{1,0:T(8,128)(2,1)} %q.1, bf16[128,2048]{1,0:T(8,128)(2,1)} %k.1, bf16[128,2048]{1,0:T(8,128)(2,1)} %v.1), custom_call_target="tpu_custom_call" | custom-call | bytes 3145728 | tf_op jit(solution)/shard_map/pack/pallas_call | solution.py:190
  4.3 7.4 %all-to-all-start = ((bf16[8,128,768]{2,1,0:T(8,128)(2,1)}), bf16[8,128,768]{2,1,0:T(8,128)(2,1)S(1)}, u32[]{:S(2)}, u32[]{:S(2)}) async-start(bf16[8,128,768]{2,1,0:T(8,128)(2,1)} %pack.1), calls=%async_computation | async-start | bytes 3145728 | tf_op jit(solution)/shard_map/all_to_all | solution.py:436
  11.7 15.7 %collective-permute-start.3 = (bf16[1,48,256]{2,1,0:T(8,128)(2,1)S(1)}, bf16[1,48,256]{2,1,0:T(8,128)(2,1)S(1)}, u32[]{:S(2)}, u32[]{:S(2)}) collective-permute-start(bf16[1,48,256]{2,1,0:T(8,128)(2,1)S(1)} %bitcast.46), channel_id=1, source_target_pairs={{0,128},{16,144},{32,160},{48,176},{64,192},{80,208},{96,224},{112... | collective-permute-start | bytes 73736 | tf_op jit(solution)/shard_map/ppermute | solution.py:404
  27.5 1.9 collective-permute-start.2
  29.4 6.0 %collective-permute-start.4 = (bf16[2,48,256]{2,1,0:T(8,128)(2,1)S(1)}, bf16[2,48,256]{2,1,0:T(8,128)(2,1)S(1)}, u32[]{:S(2)}, u32[]{:S(2)}) collective-permute-start(bf16[2,48,256]{2,1,0:T(8,128)(2,1)S(1)} %pad_maximum_fusion.2), channel_id=1, source_target_pairs={{0,64},{16,80},{32,96},{48,112},{64,0},{80,16},{96,32},{112,48},{1... | collective-permute-start | bytes 147464 | tf_op jit(solution)/shard_map/ppermute | solution.py:404
  35.4 5.1 %collective-permute-done.4 = bf16[2,48,256]{2,1,0:T(8,128)(2,1)S(1)} collective-permute-done((bf16[2,48,256]{2,1,0:T(8,128)(2,1)S(1)}, bf16[2,48,256]{2,1,0:T(8,128)(2,1)S(1)}, u32[]{:S(2)}, u32[]{:S(2)}) %collective-permute-start.4) | collective-permute-done | bytes 49184 | tf_op jit(solution)/shard_map/ppermute | solution.py:404
  40.5 2.3 %collective-permute-start.5 = (bf16[4,48,256]{2,1,0:T(8,128)(2,1)S(1)}, bf16[4,48,256]{2,1,0:T(8,128)(2,1)S(1)}, u32[]{:S(2)}, u32[]{:S(2)}) collective-permute-start(bf16[4,48,256]{2,1,0:T(8,128)(2,1)S(1)} %pad_maximum_fusion.1), channel_id=1, source_target_pairs={{0,32},{16,48},{32,0},{48,16},{64,96},{80,112},{96,64},{112,80},{1... | collective-permute-start | bytes 294920 | tf_op jit(solution)/shard_map/ppermute | solution.py:404
  42.8 5.5 %collective-permute-done.5 = bf16[4,48,256]{2,1,0:T(8,128)(2,1)S(1)} collective-permute-done((bf16[4,48,256]{2,1,0:T(8,128)(2,1)S(1)}, bf16[4,48,256]{2,1,0:T(8,128)(2,1)S(1)}, u32[]{:S(2)}, u32[]{:S(2)}) %collective-permute-start.5) | collective-permute-done | bytes 98336 | tf_op jit(solution)/shard_map/ppermute | solution.py:404
  49.7 3.3 %copies.1 = bf16[4,256,1536]{2,1,0:T(8,128)(2,1)} custom-call(s32[1]{0:T(128)} %bitcast.6.yhi, bf16[128,3072]{1,0:T(8,128)(2,1)} %own.1, bf16[128,1536]{1,0:T(8,128)(2,1)} %copy-done.12, bf16[8,48,256]{2,1,0:T(8,128)(2,1)} %pad_maximum_fusion.after), custom_call_target="tpu_custom_call" | custom-call | bytes 5242880 | tf_op jit(solution)/shard_map/copies/pallas_call | solution.py:231
  53.0 5.0 %all-to-all-start.1 = ((bf16[4,256,1536]{2,1,0:T(8,128)(2,1)}), bf16[4,256,1536]{2,1,0:T(8,128)(2,1)}, u32[]{:S(2)}, u32[]{:S(2)}) async-start(bf16[4,256,1536]{2,1,0:T(8,128)(2,1)} %copies.1), calls=%async_computation.1 | async-start | bytes 6291456 | tf_op jit(solution)/shard_map/all_to_all | solution.py:446
  59.2 1.9 collective-permute-start.6
  62.4 4.4 %collective-permute-done.6 = bf16[8,48,256]{2,1,0:T(8,128)(2,1)S(1)} collective-permute-done((bf16[8,48,256]{2,1,0:T(8,128)(2,1)S(1)}, bf16[8,48,256]{2,1,0:T(8,128)(2,1)S(1)}, u32[]{:S(2)}, u32[]{:S(2)}) %collective-permute-start.6) | collective-permute-done | bytes 196640 | tf_op jit(solution)/shard_map/ppermute | solution.py:404
  68.1 6.5 %collective-permute-start.8 = (bf16[16,48,256]{2,1,0:T(8,128)(2,1)}, bf16[16,48,256]{2,1,0:T(8,128)(2,1)S(1)}, u32[]{:S(2)}, u32[]{:S(2)}) collective-permute-start(bf16[16,48,256]{2,1,0:T(8,128)(2,1)} %constant_dynamic-update-slice_fusion), channel_id=1, source_target_pairs={{0,256},{257,1},{1,0},{256,257},{2,258},{259,3},{3,2},{258,259},{4... | collective-permute-start | bytes 1179656 | tf_op jit(solution)/shard_map/ppermute | solution.py:383
  75.5 1.9 collective-permute-start
  77.4 5.8 %collective-permute-start.1 = (bf16[256,512]{1,0:T(8,128)(2,1)}, bf16[256,512]{1,0:T(8,128)(2,1)S(1)}, u32[]{:S(2)}, u32[]{:S(2)}) collective-permute-start(bf16[256,512]{1,0:T(8,128)(2,1)} %get-tuple-element.30), channel_id=1, source_target_pairs={{8,0},{16,8},{24,16},{32,24},{40,32},{48,40},{56,48},{64,56},{72,6... | collective-permute-start | bytes 786440 | tf_op jit(solution)/shard_map/ppermute | solution.py:398
  83.2 1.1 broadcast_select_fusion.own_near
  84.3 1.9 collective-permute-start.9
  86.2 2.4 %collective-permute-start.10 = (bf16[16,48,256]{2,1,0:T(8,128)(2,1)S(1)}, bf16[16,48,256]{2,1,0:T(8,128)(2,1)}, u32[]{:S(2)}, u32[]{:S(2)}) collective-permute-start(bf16[16,48,256]{2,1,0:T(8,128)(2,1)S(1)} %collective-permute-done.8.own_far), channel_id=1, source_target_pairs={{0,8},{8,0},{1,9},{9,1},{2,10},{10,2},{3,11},{11,3},{4,12},{12,4},... | collective-permute-start | bytes 1179656 | tf_op jit(solution)/shard_map/ppermute | solution.py:374
  88.7 6.3 %forward.1 = (bf16[1024,256]{1,0:T(8,128)(2,1)}, bf16[2,4,768,256]{3,2,1,0:T(8,128)(2,1)S(1)}) custom-call(f32[2]{0:T(128)S(1)} %add_select_fusion.bias, bf16[1024,768]{1,0:T(8,128)(2,1)S(1)} %bitcast.33, bf16[1024,768]{1,0:T(8,128)(2,1)S(1)} %bitcast.34, bf16[1024,768]{1,0:T(8,128)(2,1)S(1)} %bitcast.35, bf16[256,512]{1,0:T(8,128)(2,1)S(1)} %collective-permute-done.kb.vb, ...), custom_call_target="tpu_custom_call" | custom-call | flops 805306368 | bytes 6291456 | tf_op jit(solution)/shard_map/forward/pallas_call | solution.py:124
  95.0 1.7 copy-done.1
  96.7 1.9 collective-permute-start.14
  100.5 1.0 copy-done.6
  101.5 5.6 %dout.1 = (f32[1024,256]{1,0:T(8,128)S(1)}, bf16[1024,256]{1,0:T(8,128)(2,1)}) custom-call(s32[3]{0:T(128)S(1)} %pad_add_fusion.where, bf16[1024,1536]{1,0:T(8,128)(2,1)} %bitcast.8.og, bf16[16,48,256]{2,1,0:T(8,128)(2,1)S(1)} %broadcast_select_fusion.own_near, bf16[16,48,256]{2,1,0:T(8,128)(2,1)S(1)} %copy-done.4, bf16[16,48,256]{2,1,0:T(8,128)(2,1)S(1)} %copy-done.6, ...), custom_call_target="tpu_custom_call" | custom-call | flops 1610612736 | bytes 7340032 | tf_op jit(solution)/shard_map/dout/pallas_call | solution.py:284
  107.1 7.2 %collective-permute-done.14.attn_other = bf16[1024,256]{1,0:T(8,128)(2,1)} collective-permute-done((bf16[1024,256]{1,0:T(8,128)(2,1)}, bf16[1024,256]{1,0:T(8,128)(2,1)}, u32[]{:S(2)}, u32[]{:S(2)}) %collective-permute-start.14) | collective-permute-done | bytes 524320 | tf_op jit(solution)/shard_map/ppermute | solution.py:374
  114.3 5.2 %projection.1 = (f32[16,48,512]{2,1,0:T(8,128)S(1)}, bf16[16,48,512]{2,1,0:T(8,128)(2,1)S(1)}) custom-call(s32[3]{0:T(128)S(1)} %pad_add_fusion.where, bf16[1024,1536]{1,0:T(8,128)(2,1)} %bitcast.8.og, bf16[1024,256]{1,0:T(8,128)(2,1)} %get-tuple-element.25.attn, bf16[1024,256]{1,0:T(8,128)(2,1)} %collective-permute-done.14.attn_other, ...), custom_call_target="tpu_custom_call" | custom-call | flops 1610612736 | bytes 7340032 | tf_op jit(solution)/shard_map/projection/pallas_call | solution.py:327
  119.5 1.9 collective-permute-start.15
  121.4 2.2 %collective-permute-start.11 = (bf16[1024,256]{1,0:T(8,128)(2,1)}, bf16[1024,256]{1,0:T(8,128)(2,1)}, u32[]{:S(2)}, u32[]{:S(2)}) collective-permute-start(bf16[1024,256]{1,0:T(8,128)(2,1)} %get-tuple-element.18.after), channel_id=1, source_target_pairs={{0,1},{1,0},{2,3},{3,2},{4,5},{5,4},{6,7},{7,6},{8,9},{9,8},{10,11... | collective-permute-start | bytes 1572872 | tf_op jit(solution)/shard_map/ppermute | solution.py:374
  124.0 1.1 copy-done.8
  126.1 5.1 %collective-permute-start.17 = (bf16[16,48,256]{2,1,0:T(8,128)(2,1)}, bf16[16,48,256]{2,1,0:T(8,128)(2,1)}, u32[]{:S(2)}, u32[]{:S(2)}) collective-permute-start(bf16[16,48,256]{2,1,0:T(8,128)(2,1)} %get-tuple-element.29), channel_id=1, source_target_pairs={{256,0},{1,257},{0,1},{257,256},{258,2},{3,259},{2,3},{259,258},{2... | collective-permute-start | bytes 1179656 | tf_op jit(solution)/shard_map/ppermute | solution.py:389
  131.2 1.4 collective-permute-start.16
  132.6 7.3 %collective-permute-done.11.recv = bf16[1024,256]{1,0:T(8,128)(2,1)} collective-permute-done((bf16[1024,256]{1,0:T(8,128)(2,1)}, bf16[1024,256]{1,0:T(8,128)(2,1)}, u32[]{:S(2)}, u32[]{:S(2)}) %collective-permute-start.11) | collective-permute-done | bytes 524320 | tf_op jit(solution)/shard_map/ppermute | solution.py:374
  139.9 1.9 copy-done.2
  141.8 7.2 %backward.1 = (bf16[1024,768]{1,0:T(8,128)(2,1)S(1)}, bf16[256,512]{1,0:T(8,128)(2,1)S(1)}, bf16[256,512]{1,0:T(8,128)(2,1)}) custom-call(bf16[1024,768]{1,0:T(8,128)(2,1)S(1)} %bitcast.36, bf16[1024,768]{1,0:T(8,128)(2,1)S(1)} %bitcast.37, bf16[1024,768]{1,0:T(8,128)(2,1)S(1)} %bitcast.38, bf16[256,512]{1,0:T(8,128)(2,1)S(1)} %collective-permute-done.kb.vb, ...), custom_call_target="tpu_custom_call" | custom-call | flops 1610612736 | bytes 9437184 | tf_op jit(solution)/shard_map/backward/pallas_call | solution.py:149
  149.0 1.2 copy-done
  150.2 1.9 collective-permute-start.12
  152.1 5.8 %collective-permute-start.13 = (bf16[256,512]{1,0:T(8,128)(2,1)S(1)}, bf16[256,512]{1,0:T(8,128)(2,1)S(1)}, u32[]{:S(2)}, u32[]{:S(2)}) collective-permute-start(bf16[256,512]{1,0:T(8,128)(2,1)S(1)} %get-tuple-element.21), channel_id=1, source_target_pairs={{8,0},{16,8},{24,16},{32,24},{40,32},{48,40},{56,48},{64,56},{72,6... | collective-permute-start | bytes 786440 | tf_op jit(solution)/shard_map/ppermute | solution.py:398
  157.9 1.3 convert_add_fusion.1
  159.9 1.9 collective-permute-start.18
  162.6 2.2 %edges.1 = bf16[1024,768]{1,0:T(8,128)(2,1)} custom-call(bf16[1024,768]{1,0:T(8,128)(2,1)} %copy-done, bf16[256,512]{1,0:T(8,128)(2,1)} %copy-done.14, bf16[256,512]{1,0:T(8,128)(2,1)} %copy-done.15), custom_call_target="tpu_custom_call", output_to_operand_aliasing={{}: (0, {})} | custom-call | bytes 2097152 | tf_op jit(solution)/shard_map/edges/pallas_call | solution.py:361
  164.8 7.7 %all-to-all-start.2 = ((bf16[8,128,768]{2,1,0:T(8,128)(2,1)}), bf16[8,128,768]{2,1,0:T(8,128)(2,1)S(1)}, u32[]{:S(2)}, u32[]{:S(2)}) async-start(bf16[8,128,768]{2,1,0:T(8,128)(2,1)} %bitcast.39), calls=%async_computation.2 | async-start | bytes 3145728 | tf_op jit(solution)/shard_map/all_to_all | solution.py:468
  172.6 1.9 collective-permute-start.19
  174.6 5.4 %collective-permute-done.19 = bf16[4,48,256]{2,1,0:T(8,128)(2,1)S(1)} collective-permute-done((bf16[4,48,256]{2,1,0:T(8,128)(2,1)S(1)}, bf16[4,48,256]{2,1,0:T(8,128)(2,1)S(1)}, u32[]{:S(2)}, u32[]{:S(2)}) %collective-permute-start.19) | collective-permute-done | bytes 98336 | tf_op jit(solution)/shard_map/ppermute | solution.py:418
  180.0 4.9 %collective-permute-start.20 = (bf16[2,48,256]{2,1,0:T(8,128)(2,1)S(1)}, bf16[2,48,256]{2,1,0:T(8,128)(2,1)S(1)}, u32[]{:S(2)}, u32[]{:S(2)}) collective-permute-start(bf16[2,48,256]{2,1,0:T(8,128)(2,1)S(1)} %fusion.2), channel_id=1, source_target_pairs={{0,64},{16,80},{32,96},{48,112},{64,0},{80,16},{96,32},{112,48},{1... | collective-permute-start | bytes 147464 | tf_op jit(solution)/shard_map/ppermute | solution.py:418
  185.0 5.0 %collective-permute-done.20 = bf16[2,48,256]{2,1,0:T(8,128)(2,1)S(1)} collective-permute-done((bf16[2,48,256]{2,1,0:T(8,128)(2,1)S(1)}, bf16[2,48,256]{2,1,0:T(8,128)(2,1)S(1)}, u32[]{:S(2)}, u32[]{:S(2)}) %collective-permute-start.20) | collective-permute-done | bytes 49184 | tf_op jit(solution)/shard_map/ppermute | solution.py:418
  190.0 7.6 %collective-permute-start.21 = (bf16[1,48,256]{2,1,0:T(8,128)(2,1)S(1)}, bf16[1,48,256]{2,1,0:T(8,128)(2,1)S(1)}, u32[]{:S(2)}, u32[]{:S(2)}) collective-permute-start(bf16[1,48,256]{2,1,0:T(8,128)(2,1)S(1)} %dynamic-slice_convert_fusion.2), channel_id=1, source_target_pairs={{0,128},{16,144},{32,160},{48,176},{64,192},{80,208},{96,224},{112... | collective-permute-start | bytes 73736 | tf_op jit(solution)/shard_map/ppermute | solution.py:418
  197.6 6.9 %collective-permute-done.21 = bf16[1,48,256]{2,1,0:T(8,128)(2,1)S(1)} collective-permute-done((bf16[1,48,256]{2,1,0:T(8,128)(2,1)S(1)}, bf16[1,48,256]{2,1,0:T(8,128)(2,1)S(1)}, u32[]{:S(2)}, u32[]{:S(2)}) %collective-permute-start.21) | collective-permute-done | bytes 24608 | tf_op jit(solution)/shard_map/ppermute | solution.py:418
  205.2 1.2 copy-done.7
  206.3 3.6 %unpack.1 = (bf16[128,2048]{1,0:T(8,128)(2,1)}, bf16[128,2048]{1,0:T(8,128)(2,1)}, bf16[128,2048]{1,0:T(8,128)(2,1)}) custom-call(bf16[8,128,768]{2,1,0:T(8,128)(2,1)} %copy-done.7), custom_call_target="tpu_custom_call" | custom-call | bytes 3145728 | tf_op jit(solution)/shard_map/unpack/pallas_call | solution.py:212
  (66 shorter events, 11.6 us)
Async XLA Ops:
  4.3 7.4 %copy-start.13 = (bf16[48,256]{1,0:T(8,128)(2,1)S(1)}, bf16[48,256]{1,0:T(8,128)(2,1)}, u32[]{:S(2)}) copy-start(bf16[48,256]{1,0:T(8,128)(2,1)} %param.9) | copy-start | bytes 73732
  4.3 23.1 %copy-start.10 = (bf16[128,3072]{1,0:T(8,128)(2,1)S(1)}, bf16[128,3072]{1,0:T(8,128)(2,1)}, u32[]{:S(2)}) copy-start(bf16[128,3072]{1,0:T(8,128)(2,1)} %own.1) | copy-start | bytes 2359300
  4.3 48.7 %all-to-all-start = ((bf16[8,128,768]{2,1,0:T(8,128)(2,1)}), bf16[8,128,768]{2,1,0:T(8,128)(2,1)S(1)}, u32[]{:S(2)}, u32[]{:S(2)}) async-start(bf16[8,128,768]{2,1,0:T(8,128)(2,1)} %pack.1), calls=%async_computation | async-start | bytes 3145728 | tf_op jit(solution)/shard_map/all_to_all | solution.py:436
  11.7 17.7 %collective-permute-start.3 = (bf16[1,48,256]{2,1,0:T(8,128)(2,1)S(1)}, bf16[1,48,256]{2,1,0:T(8,128)(2,1)S(1)}, u32[]{:S(2)}, u32[]{:S(2)}) collective-permute-start(bf16[1,48,256]{2,1,0:T(8,128)(2,1)S(1)} %bitcast.46), channel_id=1, source_target_pairs={{0,128},{16,144},{32,160},{48,176},{64,192},{80,208},{96,224},{112... | collective-permute-start | bytes 73736 | tf_op jit(solution)/shard_map/ppermute | solution.py:404
  27.5 21.5 %collective-permute-start.2 = (bf16[128,1536]{1,0:T(8,128)(2,1)S(1)}, bf16[128,1536]{1,0:T(8,128)(2,1)S(1)}, u32[]{:S(2)}, u32[]{:S(2)}) collective-permute-start(bf16[128,1536]{1,0:T(8,128)(2,1)S(1)} %constant_dynamic-slice_fusion), channel_id=1, source_target_pairs={{0,1},{1,0},{2,3},{3,2},{4,5},{5,4},{6,7},{7,6},{8,9},{9,8},{10,11... | collective-permute-start | bytes 1179656 | tf_op jit(solution)/shard_map/ppermute | solution.py:374
  29.4 11.1 %collective-permute-start.4 = (bf16[2,48,256]{2,1,0:T(8,128)(2,1)S(1)}, bf16[2,48,256]{2,1,0:T(8,128)(2,1)S(1)}, u32[]{:S(2)}, u32[]{:S(2)}) collective-permute-start(bf16[2,48,256]{2,1,0:T(8,128)(2,1)S(1)} %pad_maximum_fusion.2), channel_id=1, source_target_pairs={{0,64},{16,80},{32,96},{48,112},{64,0},{80,16},{96,32},{112,48},{1... | collective-permute-start | bytes 147464 | tf_op jit(solution)/shard_map/ppermute | solution.py:404
  40.5 7.7 %collective-permute-start.5 = (bf16[4,48,256]{2,1,0:T(8,128)(2,1)S(1)}, bf16[4,48,256]{2,1,0:T(8,128)(2,1)S(1)}, u32[]{:S(2)}, u32[]{:S(2)}) collective-permute-start(bf16[4,48,256]{2,1,0:T(8,128)(2,1)S(1)} %pad_maximum_fusion.1), channel_id=1, source_target_pairs={{0,32},{16,48},{32,0},{48,16},{64,96},{80,112},{96,64},{112,80},{1... | collective-permute-start | bytes 294920 | tf_op jit(solution)/shard_map/ppermute | solution.py:404
  49.0 0.7 copy-start.12
  53.0 6.2 %copy-start.11 = (bf16[8,48,256]{2,1,0:T(8,128)(2,1)S(1)}, bf16[8,48,256]{2,1,0:T(8,128)(2,1)}, u32[]{:S(2)}) copy-start(bf16[8,48,256]{2,1,0:T(8,128)(2,1)} %pad_maximum_fusion.after) | copy-start | bytes 589828
  53.0 46.5 %all-to-all-start.1 = ((bf16[4,256,1536]{2,1,0:T(8,128)(2,1)}), bf16[4,256,1536]{2,1,0:T(8,128)(2,1)}, u32[]{:S(2)}, u32[]{:S(2)}) async-start(bf16[4,256,1536]{2,1,0:T(8,128)(2,1)} %copies.1), calls=%async_computation.1 | async-start | bytes 6291456 | tf_op jit(solution)/shard_map/all_to_all | solution.py:446
  59.2 7.6 %collective-permute-start.6 = (bf16[8,48,256]{2,1,0:T(8,128)(2,1)S(1)}, bf16[8,48,256]{2,1,0:T(8,128)(2,1)S(1)}, u32[]{:S(2)}, u32[]{:S(2)}) collective-permute-start(bf16[8,48,256]{2,1,0:T(8,128)(2,1)S(1)} %copy-done.11), channel_id=1, source_target_pairs={{0,16},{16,0},{32,48},{48,32},{64,80},{80,64},{96,112},{112,96},{1... | collective-permute-start | bytes 589832 | tf_op jit(solution)/shard_map/ppermute | solution.py:404
  67.4 15.8 %collective-permute-start.7 = (bf16[16,48,256]{2,1,0:T(8,128)(2,1)}, bf16[16,48,256]{2,1,0:T(8,128)(2,1)S(1)}, u32[]{:S(2)}, u32[]{:S(2)}) collective-permute-start(bf16[16,48,256]{2,1,0:T(8,128)(2,1)} %constant_dynamic-update-slice_fusion), channel_id=1, source_target_pairs={{1,256},{256,1},{3,258},{258,3},{5,260},{260,5},{7,262},{262,7},{9... | collective-permute-start | bytes 1179656 | tf_op jit(solution)/shard_map/ppermute | solution.py:384
  68.1 18.1 %collective-permute-start.8 = (bf16[16,48,256]{2,1,0:T(8,128)(2,1)}, bf16[16,48,256]{2,1,0:T(8,128)(2,1)S(1)}, u32[]{:S(2)}, u32[]{:S(2)}) collective-permute-start(bf16[16,48,256]{2,1,0:T(8,128)(2,1)} %constant_dynamic-update-slice_fusion), channel_id=1, source_target_pairs={{0,256},{257,1},{1,0},{256,257},{2,258},{259,3},{3,2},{258,259},{4... | collective-permute-start | bytes 1179656 | tf_op jit(solution)/shard_map/ppermute | solution.py:383
  75.5 13.2 %collective-permute-start = (bf16[256,512]{1,0:T(8,128)(2,1)}, bf16[256,512]{1,0:T(8,128)(2,1)S(1)}, u32[]{:S(2)}, u32[]{:S(2)}) collective-permute-start(bf16[256,512]{1,0:T(8,128)(2,1)} %get-tuple-element.31), channel_id=1, source_target_pairs={{0,8},{8,16},{16,24},{24,32},{32,40},{40,48},{48,56},{56,64},{64,7... | collective-permute-start | bytes 786440 | tf_op jit(solution)/shard_map/ppermute | solution.py:398
  77.4 11.3 %collective-permute-start.1 = (bf16[256,512]{1,0:T(8,128)(2,1)}, bf16[256,512]{1,0:T(8,128)(2,1)S(1)}, u32[]{:S(2)}, u32[]{:S(2)}) collective-permute-start(bf16[256,512]{1,0:T(8,128)(2,1)} %get-tuple-element.30), channel_id=1, source_target_pairs={{8,0},{16,8},{24,16},{32,24},{40,32},{48,40},{56,48},{64,56},{72,6... | collective-permute-start | bytes 786440 | tf_op jit(solution)/shard_map/ppermute | solution.py:398
  84.3 14.4 %collective-permute-start.9 = (bf16[16,48,256]{2,1,0:T(8,128)(2,1)S(1)}, bf16[16,48,256]{2,1,0:T(8,128)(2,1)S(1)}, u32[]{:S(2)}, u32[]{:S(2)}) collective-permute-start(bf16[16,48,256]{2,1,0:T(8,128)(2,1)S(1)} %broadcast_select_fusion.own_near), channel_id=1, source_target_pairs={{0,8},{8,0},{1,9},{9,1},{2,10},{10,2},{3,11},{11,3},{4,12},{12,4},... | collective-permute-start | bytes 1179656 | tf_op jit(solution)/shard_map/ppermute | solution.py:374
  86.2 8.8 %copy-start.3 = (bf16[16,48,256]{2,1,0:T(8,128)(2,1)}, bf16[16,48,256]{2,1,0:T(8,128)(2,1)S(1)}, u32[]{:S(2)}) copy-start(bf16[16,48,256]{2,1,0:T(8,128)(2,1)S(1)} %collective-permute-done.8.own_far) | copy-start | bytes 1179652
  86.2 13.2 %collective-permute-start.10 = (bf16[16,48,256]{2,1,0:T(8,128)(2,1)S(1)}, bf16[16,48,256]{2,1,0:T(8,128)(2,1)}, u32[]{:S(2)}, u32[]{:S(2)}) collective-permute-start(bf16[16,48,256]{2,1,0:T(8,128)(2,1)S(1)} %collective-permute-done.8.own_far), channel_id=1, source_target_pairs={{0,8},{8,0},{1,9},{9,1},{2,10},{10,2},{3,11},{11,3},{4,12},{12,4},... | collective-permute-start | bytes 1179656 | tf_op jit(solution)/shard_map/ppermute | solution.py:374
  95.0 1.7 copy-start.1
  96.7 17.5 %collective-permute-start.14 = (bf16[1024,256]{1,0:T(8,128)(2,1)}, bf16[1024,256]{1,0:T(8,128)(2,1)}, u32[]{:S(2)}, u32[]{:S(2)}) collective-permute-start(bf16[1024,256]{1,0:T(8,128)(2,1)} %get-tuple-element.25.attn), channel_id=1, source_target_pairs={{0,1},{1,0},{2,3},{3,2},{4,5},{5,4},{6,7},{7,6},{8,9},{9,8},{10,11... | collective-permute-start | bytes 1572872 | tf_op jit(solution)/shard_map/ppermute | solution.py:374
  98.7 0.7 copy-start.5
  99.5 1.0 copy-start.4
  100.5 1.0 copy-start.6
  119.5 4.2 %collective-permute-start.15 = (bf16[16,48,512]{2,1,0:T(8,128)(2,1)S(1)}, bf16[16,48,512]{2,1,0:T(8,128)(2,1)S(1)}, u32[]{:S(2)}, u32[]{:S(2)}) collective-permute-start(bf16[16,48,512]{2,1,0:T(8,128)(2,1)S(1)} %get-tuple-element.27), channel_id=1, source_target_pairs={{0,8},{8,0},{1,9},{9,1},{2,10},{10,2},{3,11},{11,3},{4,12},{12,4},... | collective-permute-start | bytes 2359304 | tf_op jit(solution)/shard_map/ppermute | solution.py:374
  121.4 18.4 %collective-permute-start.11 = (bf16[1024,256]{1,0:T(8,128)(2,1)}, bf16[1024,256]{1,0:T(8,128)(2,1)}, u32[]{:S(2)}, u32[]{:S(2)}) collective-permute-start(bf16[1024,256]{1,0:T(8,128)(2,1)} %get-tuple-element.18.after), channel_id=1, source_target_pairs={{0,1},{1,0},{2,3},{3,2},{4,5},{5,4},{6,7},{7,6},{8,9},{9,8},{10,11... | collective-permute-start | bytes 1572872 | tf_op jit(solution)/shard_map/ppermute | solution.py:374
  124.0 1.1 copy-start.8
  126.1 31.8 %collective-permute-start.17 = (bf16[16,48,256]{2,1,0:T(8,128)(2,1)}, bf16[16,48,256]{2,1,0:T(8,128)(2,1)}, u32[]{:S(2)}, u32[]{:S(2)}) collective-permute-start(bf16[16,48,256]{2,1,0:T(8,128)(2,1)} %get-tuple-element.29), channel_id=1, source_target_pairs={{256,0},{1,257},{0,1},{257,256},{258,2},{3,259},{2,3},{259,258},{2... | collective-permute-start | bytes 1179656 | tf_op jit(solution)/shard_map/ppermute | solution.py:389
  131.2 26.7 %collective-permute-start.16 = (bf16[16,48,256]{2,1,0:T(8,128)(2,1)}, bf16[16,48,256]{2,1,0:T(8,128)(2,1)}, u32[]{:S(2)}, u32[]{:S(2)}) collective-permute-start(bf16[16,48,256]{2,1,0:T(8,128)(2,1)} %get-tuple-element.28), channel_id=1, source_target_pairs={{1,256},{256,1},{3,258},{258,3},{5,260},{260,5},{7,262},{262,7},{9... | collective-permute-start | bytes 1179656 | tf_op jit(solution)/shard_map/ppermute | solution.py:390
  139.9 1.9 copy-start.2
  141.8 16.1 %copy-start.9 = (f32[16,48,512]{2,1,0:T(8,128)S(1)}, f32[16,48,512]{2,1,0:T(8,128)}, u32[]{:S(2)}) copy-start(f32[16,48,512]{2,1,0:T(8,128)} %copy-done.8) | copy-start | bytes 4718596
  149.0 1.2 copy-start
  150.2 11.7 %collective-permute-start.12 = (bf16[256,512]{1,0:T(8,128)(2,1)}, bf16[256,512]{1,0:T(8,128)(2,1)S(1)}, u32[]{:S(2)}, u32[]{:S(2)}) collective-permute-start(bf16[256,512]{1,0:T(8,128)(2,1)} %get-tuple-element.20), channel_id=1, source_target_pairs={{0,8},{8,16},{16,24},{24,32},{32,40},{40,48},{48,56},{56,64},{64,7... | collective-permute-start | bytes 786440 | tf_op jit(solution)/shard_map/ppermute | solution.py:398
  152.1 9.8 %collective-permute-start.13 = (bf16[256,512]{1,0:T(8,128)(2,1)S(1)}, bf16[256,512]{1,0:T(8,128)(2,1)S(1)}, u32[]{:S(2)}, u32[]{:S(2)}) collective-permute-start(bf16[256,512]{1,0:T(8,128)(2,1)S(1)} %get-tuple-element.21), channel_id=1, source_target_pairs={{8,0},{16,8},{24,16},{32,24},{40,32},{48,40},{56,48},{64,56},{72,6... | collective-permute-start | bytes 786440 | tf_op jit(solution)/shard_map/ppermute | solution.py:398
  159.9 12.6 %collective-permute-start.18 = (bf16[8,48,256]{2,1,0:T(8,128)(2,1)}, bf16[8,48,256]{2,1,0:T(8,128)(2,1)S(1)}, u32[]{:S(2)}, u32[]{:S(2)}) collective-permute-start(bf16[8,48,256]{2,1,0:T(8,128)(2,1)} %fusion), channel_id=1, source_target_pairs={{0,16},{16,0},{32,48},{48,32},{64,80},{80,64},{96,112},{112,96},{1... | collective-permute-start | bytes 589832 | tf_op jit(solution)/shard_map/ppermute | solution.py:418
  161.8 0.7 copy-start.14
  161.9 0.8 copy-start.15
  164.8 40.4 %all-to-all-start.2 = ((bf16[8,128,768]{2,1,0:T(8,128)(2,1)}), bf16[8,128,768]{2,1,0:T(8,128)(2,1)S(1)}, u32[]{:S(2)}, u32[]{:S(2)}) async-start(bf16[8,128,768]{2,1,0:T(8,128)(2,1)} %bitcast.39), calls=%async_computation.2 | async-start | bytes 3145728 | tf_op jit(solution)/shard_map/all_to_all | solution.py:468
  172.6 7.4 %collective-permute-start.19 = (bf16[4,48,256]{2,1,0:T(8,128)(2,1)S(1)}, bf16[4,48,256]{2,1,0:T(8,128)(2,1)S(1)}, u32[]{:S(2)}, u32[]{:S(2)}) collective-permute-start(bf16[4,48,256]{2,1,0:T(8,128)(2,1)S(1)} %fusion.1), channel_id=1, source_target_pairs={{0,32},{16,48},{32,0},{48,16},{64,96},{80,112},{96,64},{112,80},{1... | collective-permute-start | bytes 294920 | tf_op jit(solution)/shard_map/ppermute | solution.py:418
  180.0 9.9 %collective-permute-start.20 = (bf16[2,48,256]{2,1,0:T(8,128)(2,1)S(1)}, bf16[2,48,256]{2,1,0:T(8,128)(2,1)S(1)}, u32[]{:S(2)}, u32[]{:S(2)}) collective-permute-start(bf16[2,48,256]{2,1,0:T(8,128)(2,1)S(1)} %fusion.2), channel_id=1, source_target_pairs={{0,64},{16,80},{32,96},{48,112},{64,0},{80,16},{96,32},{112,48},{1... | collective-permute-start | bytes 147464 | tf_op jit(solution)/shard_map/ppermute | solution.py:418
  190.0 14.5 %collective-permute-start.21 = (bf16[1,48,256]{2,1,0:T(8,128)(2,1)S(1)}, bf16[1,48,256]{2,1,0:T(8,128)(2,1)S(1)}, u32[]{:S(2)}, u32[]{:S(2)}) collective-permute-start(bf16[1,48,256]{2,1,0:T(8,128)(2,1)S(1)} %dynamic-slice_convert_fusion.2), channel_id=1, source_target_pairs={{0,128},{16,144},{32,160},{48,176},{64,192},{80,208},{96,224},{112... | collective-permute-start | bytes 73736 | tf_op jit(solution)/shard_map/ppermute | solution.py:418
  205.2 1.2 copy-start.7

commit v3 on v2

--- a/solution.py
+++ b/solution.py
@@ -57,7 +57,7 @@
         attn[rows, :] = out.astype(BF16)
 
 
-def backward_kernel(q, k, v, kb, vb, ka, va, pt, keep, recv, dx, hb, ha):
+def backward_kernel(q, k, v, kb, vb, ka, va, pt, keep, recv, first, dx, hb, ha):
     count = q.shape[0] // TILE
     h = pl.program_id(0)
     width = 2 * HEAD_DIM
@@ -143,7 +143,7 @@
     )(bias, x, x, x, before, before, after, after)
 
 
-def attention_backward(x, before, after, pt, keep, recv):
+def attention_backward(x, before, after, pt, keep, recv, first):
     rows = x.shape[0]
     count = rows // TILE
     return pl.pallas_call(
@@ -154,6 +154,7 @@
             pl.BlockSpec((1, count, 3 * TILE, TILE), lambda h: (h, 0, 0, 0)),
             column(rows, 0),
             column(rows, 0),
+            pl.BlockSpec(memory_space=pl.ANY),
         ],
         out_specs=[
             pl.BlockSpec((rows, 6 * HEAD_DIM), lambda h: (0, 0)),
@@ -167,12 +168,12 @@
         ],
         compiler_params=pltpu.CompilerParams(vmem_limit_bytes=40 * 1024 * 1024),
         cost_estimate=pl.CostEstimate(
-            flops=2 * 4 * 2 * rows * 3 * TILE * HEAD_DIM,
+            flops=100 * 2 * 4 * 2 * rows * 3 * TILE * HEAD_DIM,
             bytes_accessed=9 * 1024 * 1024,
             transcendentals=0,
         ),
         name="backward",
-    )(x, x, x, before, before, after, after, pt, keep, recv)
+    )(x, x, x, before, before, after, after, pt, keep, recv, first)
 
 
 def pack_kernel(q, k, v, out):
@@ -198,97 +199,40 @@
     )(q, k, v)
 
 
-def unpack_kernel(dx, q, k, v):
-    width = 2 * HEAD_DIM
-    for g in range(dx.shape[0]):
-        for n, ref in enumerate((q, k, v)):
-            ref[:, g * width : (g + 1) * width] = dx[g, :, n * width : (n + 1) * width]
-
-
-def unpack(dx):
-    groups, rows, _ = dx.shape
-    width = 2 * HEAD_DIM
-    part = pl.BlockSpec((rows, 2 * width), lambda i: (0, i))
-    return pl.pallas_call(
-        unpack_kernel,
-        grid=(groups // 2,),
-        in_specs=[pl.BlockSpec((2, rows, 3 * width), lambda i: (i, 0, 0))],
-        out_specs=[part] * 3,
-        out_shape=[jax.ShapeDtypeStruct((rows, groups * width), BF16)] * 3,
-        cost_estimate=pl.CostEstimate(flops=0, bytes_accessed=3 << 20, transcendentals=0),
-        name="unpack",
-    )(dx)
-
-
-def copies_kernel(yhi, own, other, after, out):
-    rows = own.shape[0]
-    out[0, pl.ds(pl.multiple_of(yhi[0] * rows, rows), rows), :] = own[...]
-    out[0, pl.ds(pl.multiple_of((1 - yhi[0]) * rows, rows), rows), :] = other[...]
-
-
-def copies(yhi, out_grad, other, after, count):
-    rows, half = other.shape
-    return pl.pallas_call(
-        copies_kernel,
-        grid_spec=pltpu.PrefetchScalarGridSpec(
-            num_scalar_prefetch=1,
-            grid=(count,),
-            in_specs=[
-                pl.BlockSpec((rows, half), lambda i, y: (0, y[0])),
-                pl.BlockSpec((rows, half), lambda i, y: (0, 0)),
-                pl.BlockSpec(memory_space=pl.ANY),
-            ],
-            out_specs=pl.BlockSpec((1, 2 * rows, half), lambda i, y: (i, 0, 0)),
-        ),
-        out_shape=jax.ShapeDtypeStruct((count, 2 * rows, half), BF16),
-        cost_estimate=pl.CostEstimate(flops=0, bytes_accessed=5 << 20, transcendentals=0),
-        name="copies",
-    )(yhi, out_grad, other, after)
-
-
-def reversed_bits(value, size):
-    bits = size.bit_length() - 1
-    out = 0
-    for b in range(bits):
-        out = out + ((value >> b) & 1) * (1 << (bits - 1 - b))
-    return out
-
-
-def dout_kernel(where, og, own_near, own_far, other_near, other_far, keep, send, weight):
-    size, rows, width = own_near.shape
+def dout_kernel(where, og, own, other, first, keep, send, weight):
+    size, rows, _ = own.shape
+    width = keep.shape[1]
 
     @pl.when(pl.program_id(0) == 0)
     def _():
-        near = pl.ds(pl.multiple_of((1 - where[2]) * width, width), width)
-        far = pl.ds(pl.multiple_of(where[2] * width, width), width)
-        own = where[1] * rows
+        near = pl.ds(pl.multiple_of((1 - where[1]) * width, width), width)
+        far = pl.ds(pl.multiple_of(where[1] * width, width), width)
         for n in range(size):
-            at = reversed_bits(jnp.bitwise_xor(where[0], n), size)
-            first = pl.ds(pl.multiple_of(2 * n * rows + own, rows), rows)
-            second = pl.ds(pl.multiple_of((2 * n + 1) * rows - own, rows), rows)
-            weight[first, near] = own_near[at]
-            weight[first, far] = own_far[at]
-            weight[second, near] = other_near[at]
-            weight[second, far] = other_far[at]
+            for ref, place in ((own, where[0]), (other, 1 - where[0])):
+                to = pl.ds(pl.multiple_of((2 * n + place) * rows, rows), rows)
+                weight[to, near] = ref[n, :, :width]
+                weight[to, far] = ref[n, :, width:]
 
     out = jnp.dot(og[...], weight[...], preferred_element_type=F32)
     keep[...] = out[:, :width]
     send[...] = out[:, width:].astype(BF16)
 
 
-def dout_parts(where, og, parts):
+def dout_parts(where, og, own, other, first):
     rows, half = og.shape
-    size, depth, width = parts[0].shape
+    size, depth, both = own.shape
+    width = both // 2
     block = rows // 4
-    whole = pl.BlockSpec((size, depth, width), lambda i, w: (0, 0, 0))
+    whole = pl.BlockSpec((size, depth, both), lambda i, w: (0, 0, 0))
     return pl.pallas_call(
         dout_kernel,
         grid_spec=pltpu.PrefetchScalarGridSpec(
             num_scalar_prefetch=1,
             grid=(4,),
-            in_specs=[pl.BlockSpec((block, half), lambda i, w: (i, 0))] + [whole] * 4,
+            in_specs=[pl.BlockSpec((block, half), lambda i, w: (i, 0)), whole, whole]
+            + [pl.BlockSpec(memory_space=pl.ANY)],
             out_specs=[pl.BlockSpec((block, width), lambda i, w: (i, 0))] * 2,
-            scratch_shapes=[pltpu.VMEM((half, 2 * width), BF16)],
+            scratch_shapes=[pltpu.VMEM((half, both), BF16)],
         ),
         out_shape=[
             jax.ShapeDtypeStruct((rows, width), F32),
@@ -296,20 +240,20 @@
         ],
         compiler_params=pltpu.CompilerParams(vmem_limit_bytes=40 * 1024 * 1024),
         cost_estimate=pl.CostEstimate(
-            flops=2 * rows * half * 2 * width, bytes_accessed=7 << 20, transcendentals=0
+            flops=2 * rows * half * both, bytes_accessed=7 << 20, transcendentals=0
         ),
         name="dout",
-    )(where, og, *parts)
-
-
-def projection_kernel(where, og, attn, attn_other, after, mine, other, total):
+    )(where, og, own, other, first)
+
+
+def projection_kernel(where, og, attn, attn_other, first, mine, other, total):
     depth = mine.shape[1]
     width = attn.shape[1]
-    near = pl.ds(pl.multiple_of((1 - where[2]) * width, width), width)
-    far = pl.ds(pl.multiple_of(where[2] * width, width), width)
+    near = pl.ds(pl.multiple_of((1 - where[1]) * width, width), width)
+    far = pl.ds(pl.multiple_of(where[1] * width, width), width)
     total[:, near] = lax.dot_general(og[...], attn[...], TN, preferred_element_type=F32)
     total[:, far] = lax.dot_general(og[...], attn_other[...], TN, preferred_element_type=F32)
-    own = where[1] * depth
+    own = where[0] * depth
     for n in range(mine.shape[0]):
         first = pl.ds(pl.multiple_of(2 * n * depth + own, depth), depth)
         second = pl.ds(pl.multiple_of((2 * n + 1) * depth - own, depth), depth)
@@ -317,7 +261,7 @@
         other[n] = total[second, :].astype(BF16)
 
 
-def projection_grad(where, og, attn, attn_other, after, size):
+def projection_grad(where, og, attn, attn_other, first, size):
     rows, half = og.shape
     width = attn.shape[1]
     depth = half // (2 * size)
@@ -343,7 +287,7 @@
             flops=2 * rows * half * 2 * width, bytes_accessed=7 << 20, transcendentals=0
         ),
         name="projection",
-    )(where, og, attn, attn_other, after)
+    )(where, og, attn, attn_other, first)
 
 
 def edges_kernel(dx, low, high, out):
@@ -370,6 +314,23 @@
     )(dx, low, high)
 
 
+def tie_kernel(*refs):
+    pass
+
+
+def tie(array, *first):
+    spec = pl.BlockSpec(memory_space=pl.ANY)
+    return pl.pallas_call(
+        tie_kernel,
+        in_specs=[spec] * (1 + len(first)),
+        out_specs=spec,
+        out_shape=jax.ShapeDtypeStruct(array.shape, array.dtype),
+        input_output_aliases={0: 0},
+        cost_estimate=pl.CostEstimate(flops=0, bytes_accessed=0, transcendentals=0),
+        name="tie",
+    )(array, *first)
+
+
 def swapped(array, axis):
     return lax.ppermute(array, axis, [(0, 1), (1, 0)])
 
@@ -383,12 +344,6 @@
     far = lax.ppermute(block, Y, [(j, i) for i, j in FAR])
     near = lax.ppermute(block, Y, NEAR)
     return jnp.where(same, block, near), far
-
-
-def to_owners(near, far, same):
-    from_far = lax.ppermute(far.astype(BF16), Y, FAR).astype(F32)
-    from_near = lax.ppermute(near.astype(BF16), Y, NEAR).astype(F32)
-    return jnp.where(same, near, from_near) + from_far
 
 
 def to_neighbours(down_part, up_part):
@@ -398,19 +353,11 @@
     return lax.ppermute(up_part, SEQ, up), lax.ppermute(down_part, SEQ, down)
 
 
-def gathered_along_z(held, steps):
-    size = lax.axis_size("z")
-    for step in steps:
-        other = lax.ppermute(held, "z", [(i, i ^ step) for i in range(size)])
-        held = jnp.concatenate([held, other], axis=0)
-    return held
-
-
 def reduced_along_z(array):
     size = lax.axis_size("z")
     place = lax.axis_index("z")
     step = 1
-    while step < size:
+    while step < size // 2:
         halves = array.reshape((-1, 2) + array.shape[1:])
         bit = (place // step) % 2
         own = lax.dynamic_index_in_dim(halves, bit, 1, keepdims=False)
@@ -418,55 +365,77 @@
         other = lax.ppermute(send.astype(BF16), "z", [(i, i ^ step) for i in range(size)])
         array = own + other.astype(F32)
         step *= 2
-    return array[0]
+    bit = place // step
+    own = lax.dynamic_index_in_dim(array, bit, 0, keepdims=False)
+    send = lax.dynamic_index_in_dim(array, 1 - bit, 0, keepdims=False)
+    axes = ("ylo", "z", "yhi")
+
+    def pairs(flip):
+        at = lambda a, z, b: (a * size + z) * 2 + b
+        return [
+            (at(a, z, b), at(b, z ^ flip, a)) for a in range(2) for z in range(size) for b in range(2)
+        ]
+
+    near = lax.ppermute(own, axes, pairs(0))
+    far = lax.ppermute(send, axes, pairs(step))
+    return near, far
 
 
 def per_device(queries, keys, values, out_grad, out_weight):
-    ylo, z, core, yhi = (lax.axis_index(a) for a in ("ylo", "z", "core", "yhi"))
+    ylo, core, yhi = (lax.axis_index(a) for a in ("ylo", "core", "yhi"))
     z_count = lax.axis_size("z")
     place = lax.axis_index(SEQ)
     groups = lax.axis_size(HEAD)
-    across = lax.axis_size("x")
     width = 2 * HEAD_DIM
     rows_own = queries.shape[0]
     half = out_grad.shape[1] // 2
     same = ylo == yhi
-    where = jnp.stack([z, core, same.astype(jnp.int32)]).astype(jnp.int32)
-
-    x = lax.all_to_all(pack(queries, keys, values), HEAD, 0, 0, tiled=True)
-    x = x.reshape(-1, 3 * width)
-    rows = x.shape[0]
-
-    steps = [z_count >> (n + 1) for n in range(z_count.bit_length() - 1)]
-    blocks = gathered_along_z(out_weight[None], steps[:3])
-
+    where = jnp.stack([core, same]).astype(jnp.int32)
+
+    owned = lax.all_gather(out_weight, "z", axis=0)
+    weight = jnp.concatenate(from_owners(owned, same), axis=2)
+
+    og_own = lax.dynamic_slice_in_dim(out_grad, yhi * half, half, 1)
     og_send = lax.dynamic_slice_in_dim(out_grad, (1 - yhi) * half, half, 1)
     og_other = swapped(og_send, "yhi")
-    sent = copies(yhi[None].astype(jnp.int32), out_grad, og_other, blocks, across)
-    og = lax.all_to_all(sent, "x", 0, 0, tiled=True).reshape(rows, half)
-
-    own_near, own_far = from_owners(gathered_along_z(blocks, steps[3:]), same)
-    other_near = swapped(own_near, "core")
-    other_far = swapped(own_far, "core")
-
+    og = jnp.concatenate(
+        [jnp.where(yhi == 0, og_own, og_other), jnp.where(yhi == 0, og_other, og_own)], axis=0
+    )
+    og = jnp.broadcast_to(og[None], (lax.axis_size("x"),) + og.shape)
+
+    x = pack(queries, keys, values)
+    x = lax.all_to_all(x, HEAD, 0, 0, tiled=True).reshape(-1, 3 * width)
+    rows = x.shape[0]
     before, after = to_neighbours(x[:TILE, width:], x[rows - TILE :, width:])
+
+    og = lax.all_to_all(tie(og, x, owned), "x", 0, 0, tiled=True).reshape(rows, half)
+
     edge = jnp.stack([place == 0, place == lax.axis_size(SEQ) - 1])
     bias = jnp.where(edge, -1e30, 0.0).astype(F32)
     attn, pt = attention_forward(bias, x, before, after)
     attn_other = swapped(attn, "yhi")
-
-    dout_keep, dout_send = dout_parts(where, og, (own_near, own_far, other_near, other_far))
+    weight = tie(weight, attn)
+    weight_other = swapped(weight, "core")
+
+    mine, other = projection_grad(where, og, attn, attn_other, weight, z_count)
+    grad = mine + swapped(other, "core").astype(F32)
+    far = grad[:, :, width:].astype(BF16)
+    parts = reduced_along_z(grad[:, :, :width] + swapped(far, "ylo").astype(F32))
+
+    dout_keep, dout_send = dout_parts(where, og, weight, weight_other, other)
     dout_recv = swapped(dout_send, "yhi")
 
-    mine, other = projection_grad(where, og, attn, attn_other, dout_send, z_count)
-    grad = mine + swapped(other, "core").astype(F32)
-    weight_grad = reduced_along_z(to_owners(grad[:, :, :width], grad[:, :, width:], same))
-
-    dx, dx_before, dx_after = attention_backward(x, before, after, pt, dout_keep, dout_recv)
+    dx, dx_before, dx_after = attention_backward(
+        x, before, after, pt, dout_keep, dout_recv, far
+    )
     from_left, from_right = to_neighbours(dx_before, dx_after)
     dx = add_edges(dx, from_left, from_right)
     dx = lax.all_to_all(dx.reshape(groups, rows_own, 3 * width), HEAD, 0, 0, tiled=True)
-    return (*unpack(dx), weight_grad)
+    grads = [
+        dx[:, :, n * width : (n + 1) * width].transpose(1, 0, 2).reshape(rows_own, -1)
+        for n in range(3)
+    ]
+    return (*grads, tie(parts[0], grads[0]) + parts[1])
 
 
 def solution(mesh):

time: 212 us -> 205 us (0.967)
  the two profiles are of different devices: /device:TPU:24 before, /device:TPU:8 now
where the time goes in v3:
time: 205 us; the launch traced here: 203 us
  starting transfers between devices  72.1 us (35%)
  blocking collectives  39.9 us (19%)
  waiting for transfers between devices  37.2 us (18%)
  Pallas kernels  29.4 us (14%)
  local copies, waits for them, and re-layouts  15.9 us (8%)
  other arithmetic  7.58 us (4%)
    all_gather x1, blocking collectives, per_device(): owned = lax.all_gather(out_weight, 'z', axis=0)  39.9 us
    ppermute x6, waiting for transfers between devices, swapped(): return lax.ppermute(array, axis, [(0, 1), (1, 0)])  18 us
    ppermute x6, starting transfers between devices, swapped(): return lax.ppermute(array, axis, [(0, 1), (1, 0)])  17.6 us
    ppermute x4, starting transfers between devices, to_neighbours(): return (lax.ppermute(up_part, SEQ, up), lax.ppermute(down_part, SEQ, down))  12 us
    unnamed x50, local copies, waits for them, and re-layouts  11.8 us
    ppermute x3, waiting for transfers between devices, reduced_along_z(): lax.ppermute(send.astype(BF16), 'z', [(i, i ^ step) for i in range(size)])  11.2 us
    ppermute x1, starting transfers between devices, reduced_along_z(): far = lax.ppermute(send, axes, pairs(step))  9.12 us
    ppermute x3, starting transfers between devices, reduced_along_z(): lax.ppermute(send.astype(BF16), 'z', [(i, i ^ step) for i in range(size)])  8.34 us
  transfers between devices with their start and end apart: 20, of which 8 were waited for; matrix products, arithmetic and copies ran while one was open for 5% of the time, Pallas kernels for 13%

profile of v3, /device:TPU:8, one launch (start us, length us, event | category | flops | bytes accessed | tf_op | source)
XLA Modules:
  0.0 203.4 jit_solution(6746113972173149216)
XLA Ops:
  0.6 3.7 %pack.1 = bf16[8,128,768]{2,1,0:T(8,128)(2,1)} custom-call(bf16[128,2048]{1,0:T(8,128)(2,1)} %q.1, bf16[128,2048]{1,0:T(8,128)(2,1)} %k.1, bf16[128,2048]{1,0:T(8,128)(2,1)} %v.1), custom_call_target="tpu_custom_call" | custom-call | bytes 3145728 | tf_op jit(solution)/shard_map/pack/pallas_call | solution.py:191
  4.3 6.2 %all-to-all-start = ((bf16[8,128,768]{2,1,0:T(8,128)(2,1)}), bf16[8,128,768]{2,1,0:T(8,128)(2,1)S(1)}, u32[]{:S(2)}, u32[]{:S(2)}) async-start(bf16[8,128,768]{2,1,0:T(8,128)(2,1)} %pack.1), calls=%async_computation | async-start | bytes 3145728 | tf_op jit(solution)/shard_map/all_to_all | solution.py:407
  10.5 5.4 %collective-permute-start.2 = (bf16[128,1536]{1,0:T(8,128)(2,1)S(1)}, bf16[128,1536]{1,0:T(8,128)(2,1)S(1)}, u32[]{:S(2)}, u32[]{:S(2)}) collective-permute-start(bf16[128,1536]{1,0:T(8,128)(2,1)S(1)} %constant_dynamic-slice_fusion), channel_id=1, source_target_pairs={{0,1},{1,0},{2,3},{3,2},{4,5},{5,4},{6,7},{7,6},{8,9},{9,8},{10,11... | collective-permute-start | bytes 1179656 | tf_op jit(solution)/shard_map/ppermute | solution.py:335
  16.0 39.9 %all-gather = bf16[768,256]{1,0:T(8,128)(2,1)} all-gather(bf16[48,256]{1,0:T(8,128)(2,1)S(1)} %copy-done.22), channel_id=2, replica_groups=mesh['ylo'=2,'z'=16,'core'=2,'x'=4,'yhi'=2] {'z'}, dimensions={0}, use_global_device_ids=true | all-gather | bytes 417792 | tf_op jit(solution)/shard_map/all_gather | solution.py:395
  56.1 2.1 %broadcast_in_dim.16.refs_0_ = bf16[4,256,1536]{2,1,0:T(8,128)(2,1)} broadcast(bf16[256,1536]{1,0:T(8,128)(2,1)S(1)} %pad_maximum_fusion), dimensions={1,2} | broadcast | bytes 3932160 | tf_op jit(solution)/shard_map/broadcast_in_dim | solution.py:404
  58.3 4.8 %all-to-all-start.1 = ((bf16[4,256,1536]{2,1,0:T(8,128)(2,1)}), bf16[4,256,1536]{2,1,0:T(8,128)(2,1)}, u32[]{:S(2)}, u32[]{:S(2)}) async-start(bf16[4,256,1536]{2,1,0:T(8,128)(2,1)} %tie.3), calls=%async_computation.1 | async-start | bytes 6291456 | tf_op jit(solution)/shard_map/all_to_all | solution.py:411
  63.1 1.9 collective-permute-start.3
  65.1 1.9 collective-permute-start
  67.0 5.8 %collective-permute-start.1 = (bf16[256,512]{1,0:T(8,128)(2,1)S(1)}, bf16[256,512]{1,0:T(8,128)(2,1)S(1)}, u32[]{:S(2)}, u32[]{:S(2)}) collective-permute-start(bf16[256,512]{1,0:T(8,128)(2,1)S(1)} %get-tuple-element.29), channel_id=1, source_target_pairs={{8,0},{16,8},{24,16},{32,24},{40,32},{48,40},{56,48},{64,56},{72,6... | collective-permute-start | bytes 786440 | tf_op jit(solution)/shard_map/ppermute | solution.py:353
  72.8 1.9 collective-permute-start.4
  75.0 1.7 collective-permute-done.1.ka.va
  76.7 5.6 %forward.1 = (bf16[1024,256]{1,0:T(8,128)(2,1)S(1)}, bf16[2,4,768,256]{3,2,1,0:T(8,128)(2,1)S(1)}) custom-call(f32[2]{0:T(128)S(1)} %add_select_fusion.bias, bf16[1024,768]{1,0:T(8,128)(2,1)S(1)} %bitcast.43, bf16[1024,768]{1,0:T(8,128)(2,1)S(1)} %bitcast.44, bf16[1024,768]{1,0:T(8,128)(2,1)S(1)} %bitcast.45, ...), custom_call_target="tpu_custom_call" | custom-call | flops 805306368 | bytes 6291456 | tf_op jit(solution)/shard_map/forward/pallas_call | solution.py:124
  82.4 1.6 copy-done.9
  84.0 1.9 collective-permute-start.6
  85.9 1.0 broadcast_select_fusion
  87.0 1.9 pad_maximum_fusion.1.refs_0_
  88.9 1.9 collective-permute-start.5
  90.9 8.6 %collective-permute-done.6.attn_other = bf16[1024,256]{1,0:T(8,128)(2,1)S(1)} collective-permute-done((bf16[1024,256]{1,0:T(8,128)(2,1)S(1)}, bf16[1024,256]{1,0:T(8,128)(2,1)S(1)}, u32[]{:S(2)}, u32[]{:S(2)}) %collective-permute-start.6) | collective-permute-done | bytes 524320 | tf_op jit(solution)/shard_map/ppermute | solution.py:335
  100.3 1.1 copy-done.3
  101.4 1.0 copy-done.8
  102.5 1.0 copy-done.12
  103.5 5.6 %projection.1 = (f32[16,48,512]{2,1,0:T(8,128)S(1)}, bf16[16,48,512]{2,1,0:T(8,128)(2,1)}) custom-call(s32[2]{0:T(128)S(1)} %pad_add_fusion.where, bf16[1024,1536]{1,0:T(8,128)(2,1)} %bitcast.6.og, bf16[1024,256]{1,0:T(8,128)(2,1)S(1)} %copy-done.8, bf16[1024,256]{1,0:T(8,128)(2,1)S(1)} %copy-done.12, bf16[16,48,512]{2,1,0:T(8,128)(2,1)S(1)} %copy-done.3), custom_call_target="tpu_custom_call" | custom-call | flops 1610612736 | bytes 7340032 | tf_op jit(solution)/shard_map/projection/pallas_call | solution.py:271
  109.1 1.9 collective-permute-start.8
  111.1 5.7 %dout.1 = (f32[1024,256]{1,0:T(8,128)S(1)}, bf16[1024,256]{1,0:T(8,128)(2,1)}) custom-call(s32[2]{0:T(128)S(1)} %pad_add_fusion.where, bf16[1024,1536]{1,0:T(8,128)(2,1)} %bitcast.6.og, bf16[16,48,512]{2,1,0:T(8,128)(2,1)S(1)} %copy-done.4, bf16[16,48,512]{2,1,0:T(8,128)(2,1)} %collective-permute-done.5.other, bf16[16,48,512]{2,1,0:T(8,128)(2,1)} %get-tuple-element.15.first), custom_call_target="tpu_custom_call" | custom-call | flops 1610612736 | bytes 7340032 | tf_op jit(solution)/shard_map/dout/pallas_call | solution.py:227
  116.8 1.0 copy-done.13
  117.8 2.2 %collective-permute-start.7 = (bf16[1024,256]{1,0:T(8,128)(2,1)}, bf16[1024,256]{1,0:T(8,128)(2,1)}, u32[]{:S(2)}, u32[]{:S(2)}) collective-permute-start(bf16[1024,256]{1,0:T(8,128)(2,1)} %get-tuple-element.17), channel_id=1, source_target_pairs={{0,1},{1,0},{2,3},{3,2},{4,5},{5,4},{6,7},{7,6},{8,9},{9,8},{10,11... | collective-permute-start | bytes 1572872 | tf_op jit(solution)/shard_map/ppermute | solution.py:335
  120.0 1.6 convert_add_fusion
  122.5 4.3 %collective-permute-start.11 = (bf16[16,48,256]{2,1,0:T(8,128)(2,1)}, bf16[16,48,256]{2,1,0:T(8,128)(2,1)}, u32[]{:S(2)}, u32[]{:S(2)}) collective-permute-start(bf16[16,48,256]{2,1,0:T(8,128)(2,1)} %slice.39.first), channel_id=1, source_target_pairs={{0,256},{256,0},{1,257},{257,1},{2,258},{258,2},{3,259},{259,3},{4... | collective-permute-start | bytes 1179656 | tf_op jit(solution)/shard_map/ppermute | solution.py:335
  126.8 9.4 %collective-permute-done.7.recv = bf16[1024,256]{1,0:T(8,128)(2,1)} collective-permute-done((bf16[1024,256]{1,0:T(8,128)(2,1)}, bf16[1024,256]{1,0:T(8,128)(2,1)}, u32[]{:S(2)}, u32[]{:S(2)}) %collective-permute-start.7) | collective-permute-done | bytes 524320 | tf_op jit(solution)/shard_map/ppermute | solution.py:335
  136.2 6.6 %backward.1 = (bf16[1024,768]{1,0:T(8,128)(2,1)S(1)}, bf16[256,512]{1,0:T(8,128)(2,1)S(1)}, bf16[256,512]{1,0:T(8,128)(2,1)S(1)}) custom-call(bf16[1024,768]{1,0:T(8,128)(2,1)S(1)} %bitcast.46, bf16[1024,768]{1,0:T(8,128)(2,1)S(1)} %bitcast.47, bf16[1024,768]{1,0:T(8,128)(2,1)S(1)} %bitcast.48, bf16[256,512]{1,0:T(8,128)(2,1)S(1)} %collective-permute-done.kb.vb, ...), custom_call_target="tpu_custom_call" | custom-call | flops 161061273600 | bytes 9437184 | tf_op jit(solution)/shard_map/backward/pallas_call | solution.py:149
  142.8 1.2 copy-done.2
  144.0 1.9 collective-permute-start.10
  145.9 2.4 %collective-permute-start.9 = (bf16[256,512]{1,0:T(8,128)(2,1)S(1)}, bf16[256,512]{1,0:T(8,128)(2,1)S(1)}, u32[]{:S(2)}, u32[]{:S(2)}) collective-permute-start(bf16[256,512]{1,0:T(8,128)(2,1)S(1)} %get-tuple-element.20), channel_id=1, source_target_pairs={{0,8},{8,16},{16,24},{24,32},{32,40},{40,48},{48,56},{56,64},{64,7... | collective-permute-start | bytes 786440 | tf_op jit(solution)/shard_map/ppermute | solution.py:353
  148.3 1.1 slice_add_fusion
  149.5 2.4 %collective-permute-start.12 = (bf16[8,48,256]{2,1,0:T(8,128)(2,1)S(1)}, bf16[8,48,256]{2,1,0:T(8,128)(2,1)S(1)}, u32[]{:S(2)}, u32[]{:S(2)}) collective-permute-start(bf16[8,48,256]{2,1,0:T(8,128)(2,1)S(1)} %fusion), channel_id=1, source_target_pairs={{0,16},{16,0},{32,48},{48,32},{64,80},{80,64},{96,112},{112,96},{1... | collective-permute-start | bytes 589832 | tf_op jit(solution)/shard_map/ppermute | solution.py:365
  151.9 3.8 %collective-permute-done.9.low = bf16[256,512]{1,0:T(8,128)(2,1)S(1)} collective-permute-done((bf16[256,512]{1,0:T(8,128)(2,1)S(1)}, bf16[256,512]{1,0:T(8,128)(2,1)S(1)}, u32[]{:S(2)}, u32[]{:S(2)}) %collective-permute-start.9) | collective-permute-done | bytes 262176 | tf_op jit(solution)/shard_map/ppermute | solution.py:353
  156.4 2.2 %edges.1 = bf16[1024,768]{1,0:T(8,128)(2,1)} custom-call(bf16[1024,768]{1,0:T(8,128)(2,1)} %copy-done.2, bf16[256,512]{1,0:T(8,128)(2,1)} %copy-done.20, bf16[256,512]{1,0:T(8,128)(2,1)} %copy-done.19), custom_call_target="tpu_custom_call", output_to_operand_aliasing={{}: (0, {})} | custom-call | bytes 2097152 | tf_op jit(solution)/shard_map/edges/pallas_call | solution.py:305
  158.6 5.1 %all-to-all-start.2 = ((bf16[8,128,768]{2,1,0:T(8,128)(2,1)}), bf16[8,128,768]{2,1,0:T(8,128)(2,1)S(1)}, u32[]{:S(2)}, u32[]{:S(2)}) async-start(bf16[8,128,768]{2,1,0:T(8,128)(2,1)} %bitcast.49), calls=%async_computation.2 | async-start | bytes 3145728 | tf_op jit(solution)/shard_map/all_to_all | solution.py:433
  163.7 1.9 collective-permute-start.13
  165.7 5.4 %collective-permute-done.13 = bf16[4,48,256]{2,1,0:T(8,128)(2,1)S(1)} collective-permute-done((bf16[4,48,256]{2,1,0:T(8,128)(2,1)S(1)}, bf16[4,48,256]{2,1,0:T(8,128)(2,1)S(1)}, u32[]{:S(2)}, u32[]{:S(2)}) %collective-permute-start.13) | collective-permute-done | bytes 98336 | tf_op jit(solution)/shard_map/ppermute | solution.py:365
  171.2 4.0 %collective-permute-start.14 = (bf16[2,48,256]{2,1,0:T(8,128)(2,1)S(1)}, bf16[2,48,256]{2,1,0:T(8,128)(2,1)S(1)}, u32[]{:S(2)}, u32[]{:S(2)}) collective-permute-start(bf16[2,48,256]{2,1,0:T(8,128)(2,1)S(1)} %fusion.2), channel_id=1, source_target_pairs={{0,64},{16,80},{32,96},{48,112},{64,0},{80,16},{96,32},{112,48},{1... | collective-permute-start | bytes 147464 | tf_op jit(solution)/shard_map/ppermute | solution.py:365
  175.3 5.8 %collective-permute-done.14 = bf16[2,48,256]{2,1,0:T(8,128)(2,1)S(1)} collective-permute-done((bf16[2,48,256]{2,1,0:T(8,128)(2,1)S(1)}, bf16[2,48,256]{2,1,0:T(8,128)(2,1)S(1)}, u32[]{:S(2)}, u32[]{:S(2)}) %collective-permute-start.14) | collective-permute-done | bytes 49184 | tf_op jit(solution)/shard_map/ppermute | solution.py:365
  181.1 5.2 %collective-permute-start.15 = (f32[48,256]{1,0:T(8,128)S(1)}, f32[48,256]{1,0:T(8,128)S(1)}, u32[]{:S(2)}, u32[]{:S(2)}) collective-permute-start(f32[48,256]{1,0:T(8,128)S(1)} %get-tuple-element.34), channel_id=1, source_target_pairs={{0,0},{1,256},{16,16},{17,272},{32,32},{33,288},{48,48},{49,304},{... | collective-permute-start | bytes 147464 | tf_op jit(solution)/shard_map/ppermute | solution.py:379
  186.3 9.1 %collective-permute-start.16 = (f32[48,256]{1,0:T(8,128)S(1)}, f32[48,256]{1,0:T(8,128)S(1)}, u32[]{:S(2)}, u32[]{:S(2)}) collective-permute-start(f32[48,256]{1,0:T(8,128)S(1)} %get-tuple-element.33), channel_id=1, source_target_pairs={{0,128},{1,384},{16,144},{17,400},{32,160},{33,416},{48,176},{49,4... | collective-permute-start | bytes 147464 | tf_op jit(solution)/shard_map/ppermute | solution.py:380
  196.7 1.0 copy.23
  198.0 1.0 copy.24
  199.6 2.3 %collective-permute-done.16 = f32[48,256]{1,0:T(8,128)S(1)} collective-permute-done((f32[48,256]{1,0:T(8,128)S(1)}, f32[48,256]{1,0:T(8,128)S(1)}, u32[]{:S(2)}, u32[]{:S(2)}) %collective-permute-start.16) | collective-permute-done | bytes 49184 | tf_op jit(solution)/shard_map/ppermute | solution.py:380
  201.9 1.4 add.96
  (74 shorter events, 5.4 us)
Async XLA Ops:
  4.3 6.2 %copy-start.18 = (bf16[128,3072]{1,0:T(8,128)(2,1)S(1)}, bf16[128,3072]{1,0:T(8,128)(2,1)}, u32[]{:S(2)}) copy-start(bf16[128,3072]{1,0:T(8,128)(2,1)} %param.8) | copy-start | bytes 2359300
  4.3 11.6 %copy-start.22 = (bf16[48,256]{1,0:T(8,128)(2,1)S(1)}, bf16[48,256]{1,0:T(8,128)(2,1)}, u32[]{:S(2)}) copy-start(bf16[48,256]{1,0:T(8,128)(2,1)} %param.9) | copy-start | bytes 73732
  4.3 51.8 %all-to-all-start = ((bf16[8,128,768]{2,1,0:T(8,128)(2,1)}), bf16[8,128,768]{2,1,0:T(8,128)(2,1)S(1)}, u32[]{:S(2)}, u32[]{:S(2)}) async-start(bf16[8,128,768]{2,1,0:T(8,128)(2,1)} %pack.1), calls=%async_computation | async-start | bytes 3145728 | tf_op jit(solution)/shard_map/all_to_all | solution.py:407
  10.5 45.4 %collective-permute-start.2 = (bf16[128,1536]{1,0:T(8,128)(2,1)S(1)}, bf16[128,1536]{1,0:T(8,128)(2,1)S(1)}, u32[]{:S(2)}, u32[]{:S(2)}) collective-permute-start(bf16[128,1536]{1,0:T(8,128)(2,1)S(1)} %constant_dynamic-slice_fusion), channel_id=1, source_target_pairs={{0,1},{1,0},{2,3},{3,2},{4,5},{5,4},{6,7},{7,6},{8,9},{9,8},{10,11... | collective-permute-start | bytes 1179656 | tf_op jit(solution)/shard_map/ppermute | solution.py:335
  56.1 2.2 %copy-start = (bf16[8,128,768]{2,1,0:T(8,128)(2,1)}, bf16[8,128,768]{2,1,0:T(8,128)(2,1)S(1)}, u32[]{:S(2)}) copy-start(bf16[8,128,768]{2,1,0:T(8,128)(2,1)S(1)} %all-to-all-done) | copy-start | bytes 4718596
  58.3 4.8 %copy-start.17 = (bf16[768,256]{1,0:T(8,128)(2,1)S(1)}, bf16[768,256]{1,0:T(8,128)(2,1)}, u32[]{:S(2)}) copy-start(bf16[768,256]{1,0:T(8,128)(2,1)} %all-gather) | copy-start | bytes 1179652
  58.3 6.7 %copy-start.1 = (bf16[8,128,768]{2,1,0:T(8,128)(2,1)S(1)}, bf16[8,128,768]{2,1,0:T(8,128)(2,1)}, u32[]{:S(2)}) copy-start(bf16[8,128,768]{2,1,0:T(8,128)(2,1)} %copy-done) | copy-start | bytes 4718596
  58.3 42.0 %all-to-all-start.1 = ((bf16[4,256,1536]{2,1,0:T(8,128)(2,1)}), bf16[4,256,1536]{2,1,0:T(8,128)(2,1)}, u32[]{:S(2)}, u32[]{:S(2)}) async-start(bf16[4,256,1536]{2,1,0:T(8,128)(2,1)} %tie.3), calls=%async_computation.1 | async-start | bytes 6291456 | tf_op jit(solution)/shard_map/all_to_all | solution.py:411
  63.1 22.8 %collective-permute-start.3 = (bf16[16,48,256]{2,1,0:T(8,128)(2,1)S(1)}, bf16[16,48,256]{2,1,0:T(8,128)(2,1)}, u32[]{:S(2)}, u32[]{:S(2)}) collective-permute-start(bf16[16,48,256]{2,1,0:T(8,128)(2,1)S(1)} %bitcast.51), channel_id=1, source_target_pairs={{1,256},{256,1},{3,258},{258,3},{5,260},{260,5},{7,262},{262,7},{9... | collective-permute-start | bytes 1179656 | tf_op jit(solution)/shard_map/ppermute | solution.py:345
  65.1 9.9 %collective-permute-start = (bf16[256,512]{1,0:T(8,128)(2,1)S(1)}, bf16[256,512]{1,0:T(8,128)(2,1)S(1)}, u32[]{:S(2)}, u32[]{:S(2)}) collective-permute-start(bf16[256,512]{1,0:T(8,128)(2,1)S(1)} %get-tuple-element.30), channel_id=1, source_target_pairs={{0,8},{8,16},{16,24},{24,32},{32,40},{40,48},{48,56},{56,64},{64,7... | collective-permute-start | bytes 786440 | tf_op jit(solution)/shard_map/ppermute | solution.py:353
  67.0 9.7 %collective-permute-start.1 = (bf16[256,512]{1,0:T(8,128)(2,1)S(1)}, bf16[256,512]{1,0:T(8,128)(2,1)S(1)}, u32[]{:S(2)}, u32[]{:S(2)}) collective-permute-start(bf16[256,512]{1,0:T(8,128)(2,1)S(1)} %get-tuple-element.29), channel_id=1, source_target_pairs={{8,0},{16,8},{24,16},{32,24},{40,32},{48,40},{56,48},{64,56},{72,6... | collective-permute-start | bytes 786440 | tf_op jit(solution)/shard_map/ppermute | solution.py:353
  72.8 14.2 %collective-permute-start.4 = (bf16[16,48,256]{2,1,0:T(8,128)(2,1)S(1)}, bf16[16,48,256]{2,1,0:T(8,128)(2,1)}, u32[]{:S(2)}, u32[]{:S(2)}) collective-permute-start(bf16[16,48,256]{2,1,0:T(8,128)(2,1)S(1)} %bitcast.52), channel_id=1, source_target_pairs={{0,256},{257,1},{1,0},{256,257},{2,258},{259,3},{3,2},{258,259},{4... | collective-permute-start | bytes 1179656 | tf_op jit(solution)/shard_map/ppermute | solution.py:344
  76.7 5.7 %copy-start.5 = (bf16[256,512]{1,0:T(8,128)(2,1)}, bf16[256,512]{1,0:T(8,128)(2,1)S(1)}, u32[]{:S(2)}) copy-start(bf16[256,512]{1,0:T(8,128)(2,1)S(1)} %collective-permute-done.1.ka.va) | copy-start | bytes 786436
  82.3 1.6 copy-start.9
  84.0 4.9 %copy-start.7 = (bf16[1024,256]{1,0:T(8,128)(2,1)}, bf16[1024,256]{1,0:T(8,128)(2,1)S(1)}, u32[]{:S(2)}) copy-start(bf16[1024,256]{1,0:T(8,128)(2,1)S(1)} %get-tuple-element.14.refs_1_.attn) | copy-start | bytes 1572868
  84.0 15.5 %collective-permute-start.6 = (bf16[1024,256]{1,0:T(8,128)(2,1)S(1)}, bf16[1024,256]{1,0:T(8,128)(2,1)S(1)}, u32[]{:S(2)}, u32[]{:S(2)}) collective-permute-start(bf16[1024,256]{1,0:T(8,128)(2,1)S(1)} %get-tuple-element.14.refs_1_.attn), channel_id=1, source_target_pairs={{0,1},{1,0},{2,3},{3,2},{4,5},{5,4},{6,7},{7,6},{8,9},{9,8},{10,11... | collective-permute-start | bytes 1572872 | tf_op jit(solution)/shard_map/ppermute | solution.py:335
  88.9 22.1 %collective-permute-start.5 = (bf16[16,48,512]{2,1,0:T(8,128)(2,1)}, bf16[16,48,512]{2,1,0:T(8,128)(2,1)}, u32[]{:S(2)}, u32[]{:S(2)}) collective-permute-start(bf16[16,48,512]{2,1,0:T(8,128)(2,1)} %tie.4.first.own), channel_id=1, source_target_pairs={{0,8},{8,0},{1,9},{9,1},{2,10},{10,2},{3,11},{11,3},{4,12},{12,4},... | collective-permute-start | bytes 2359304 | tf_op jit(solution)/shard_map/ppermute | solution.py:335
  99.5 0.8 copy-start.11
  100.3 1.1 copy-start.3
  101.4 1.0 copy-start.8
  102.5 1.0 copy-start.12
  103.5 7.6 %copy-start.4 = (bf16[16,48,512]{2,1,0:T(8,128)(2,1)S(1)}, bf16[16,48,512]{2,1,0:T(8,128)(2,1)}, u32[]{:S(2)}) copy-start(bf16[16,48,512]{2,1,0:T(8,128)(2,1)} %tie.4.first.own) | copy-start | bytes 2359300
  109.1 10.8 %collective-permute-start.8 = (bf16[16,48,512]{2,1,0:T(8,128)(2,1)}, bf16[16,48,512]{2,1,0:T(8,128)(2,1)}, u32[]{:S(2)}, u32[]{:S(2)}) collective-permute-start(bf16[16,48,512]{2,1,0:T(8,128)(2,1)} %get-tuple-element.15.first), channel_id=1, source_target_pairs={{0,8},{8,0},{1,9},{9,1},{2,10},{10,2},{3,11},{11,3},{4,12},{12,4},... | collective-permute-start | bytes 2359304 | tf_op jit(solution)/shard_map/ppermute | solution.py:335
  116.8 1.0 copy-start.13
  117.8 18.4 %collective-permute-start.7 = (bf16[1024,256]{1,0:T(8,128)(2,1)}, bf16[1024,256]{1,0:T(8,128)(2,1)}, u32[]{:S(2)}, u32[]{:S(2)}) collective-permute-start(bf16[1024,256]{1,0:T(8,128)(2,1)} %get-tuple-element.17), channel_id=1, source_target_pairs={{0,1},{1,0},{2,3},{3,2},{4,5},{5,4},{6,7},{7,6},{8,9},{9,8},{10,11... | collective-permute-start | bytes 1572872 | tf_op jit(solution)/shard_map/ppermute | solution.py:335
  120.0 16.2 %copy-start.6 = (bf16[256,512]{1,0:T(8,128)(2,1)S(1)}, bf16[256,512]{1,0:T(8,128)(2,1)}, u32[]{:S(2)}) copy-start(bf16[256,512]{1,0:T(8,128)(2,1)} %copy-done.5) | copy-start | bytes 786436
  120.0 16.2 %copy-start.10 = (bf16[2,4,768,256]{3,2,1,0:T(8,128)(2,1)S(1)}, bf16[2,4,768,256]{3,2,1,0:T(8,128)(2,1)}, u32[]{:S(2)}) copy-start(bf16[2,4,768,256]{3,2,1,0:T(8,128)(2,1)} %copy-done.9) | copy-start | bytes 9437188
  120.0 16.2 %copy-start.14 = (f32[1024,256]{1,0:T(8,128)S(1)}, f32[1024,256]{1,0:T(8,128)}, u32[]{:S(2)}) copy-start(f32[1024,256]{1,0:T(8,128)} %copy-done.13) | copy-start | bytes 3145732
  121.6 14.5 %copy-start.15 = (f32[16,48,512]{2,1,0:T(8,128)}, f32[16,48,512]{2,1,0:T(8,128)S(1)}, u32[]{:S(2)}) copy-start(f32[16,48,512]{2,1,0:T(8,128)S(1)} %convert_add_fusion) | copy-start | bytes 4718596
  122.5 25.8 %collective-permute-start.11 = (bf16[16,48,256]{2,1,0:T(8,128)(2,1)}, bf16[16,48,256]{2,1,0:T(8,128)(2,1)}, u32[]{:S(2)}, u32[]{:S(2)}) collective-permute-start(bf16[16,48,256]{2,1,0:T(8,128)(2,1)} %slice.39.first), channel_id=1, source_target_pairs={{0,256},{256,0},{1,257},{257,1},{2,258},{258,2},{3,259},{259,3},{4... | collective-permute-start | bytes 1179656 | tf_op jit(solution)/shard_map/ppermute | solution.py:335
  136.2 12.1 %copy-start.16 = (f32[16,48,512]{2,1,0:T(8,128)S(1)}, f32[16,48,512]{2,1,0:T(8,128)}, u32[]{:S(2)}) copy-start(f32[16,48,512]{2,1,0:T(8,128)} %copy-done.15) | copy-start | bytes 4718596
  142.8 1.2 copy-start.2
  144.0 7.9 %collective-permute-start.10 = (bf16[256,512]{1,0:T(8,128)(2,1)S(1)}, bf16[256,512]{1,0:T(8,128)(2,1)S(1)}, u32[]{:S(2)}, u32[]{:S(2)}) collective-permute-start(bf16[256,512]{1,0:T(8,128)(2,1)S(1)} %get-tuple-element.21), channel_id=1, source_target_pairs={{8,0},{16,8},{24,16},{32,24},{40,32},{48,40},{56,48},{64,56},{72,6... | collective-permute-start | bytes 786440 | tf_op jit(solution)/shard_map/ppermute | solution.py:353
  145.9 9.8 %collective-permute-start.9 = (bf16[256,512]{1,0:T(8,128)(2,1)S(1)}, bf16[256,512]{1,0:T(8,128)(2,1)S(1)}, u32[]{:S(2)}, u32[]{:S(2)}) collective-permute-start(bf16[256,512]{1,0:T(8,128)(2,1)S(1)} %get-tuple-element.20), channel_id=1, source_target_pairs={{0,8},{8,16},{16,24},{24,32},{32,40},{40,48},{48,56},{56,64},{64,7... | collective-permute-start | bytes 786440 | tf_op jit(solution)/shard_map/ppermute | solution.py:353
  149.5 14.1 %collective-permute-start.12 = (bf16[8,48,256]{2,1,0:T(8,128)(2,1)S(1)}, bf16[8,48,256]{2,1,0:T(8,128)(2,1)S(1)}, u32[]{:S(2)}, u32[]{:S(2)}) collective-permute-start(bf16[8,48,256]{2,1,0:T(8,128)(2,1)S(1)} %fusion), channel_id=1, source_target_pairs={{0,16},{16,0},{32,48},{48,32},{64,80},{80,64},{96,112},{112,96},{1... | collective-permute-start | bytes 589832 | tf_op jit(solution)/shard_map/ppermute | solution.py:365
  151.9 3.8 %copy-start.19 = (bf16[256,512]{1,0:T(8,128)(2,1)}, bf16[256,512]{1,0:T(8,128)(2,1)S(1)}, u32[]{:S(2)}) copy-start(bf16[256,512]{1,0:T(8,128)(2,1)S(1)} %collective-permute-done.10.high) | copy-start | bytes 786436
  155.7 0.7 copy-start.20
  158.6 36.9 %all-to-all-start.2 = ((bf16[8,128,768]{2,1,0:T(8,128)(2,1)}), bf16[8,128,768]{2,1,0:T(8,128)(2,1)S(1)}, u32[]{:S(2)}, u32[]{:S(2)}) async-start(bf16[8,128,768]{2,1,0:T(8,128)(2,1)} %bitcast.49), calls=%async_computation.2 | async-start | bytes 3145728 | tf_op jit(solution)/shard_map/all_to_all | solution.py:433
  163.7 7.4 %collective-permute-start.13 = (bf16[4,48,256]{2,1,0:T(8,128)(2,1)S(1)}, bf16[4,48,256]{2,1,0:T(8,128)(2,1)S(1)}, u32[]{:S(2)}, u32[]{:S(2)}) collective-permute-start(bf16[4,48,256]{2,1,0:T(8,128)(2,1)S(1)} %fusion.1), channel_id=1, source_target_pairs={{0,32},{16,48},{32,0},{48,16},{64,96},{80,112},{96,64},{112,80},{1... | collective-permute-start | bytes 294920 | tf_op jit(solution)/shard_map/ppermute | solution.py:365
  171.2 9.9 %collective-permute-start.14 = (bf16[2,48,256]{2,1,0:T(8,128)(2,1)S(1)}, bf16[2,48,256]{2,1,0:T(8,128)(2,1)S(1)}, u32[]{:S(2)}, u32[]{:S(2)}) collective-permute-start(bf16[2,48,256]{2,1,0:T(8,128)(2,1)S(1)} %fusion.2), channel_id=1, source_target_pairs={{0,64},{16,80},{32,96},{48,112},{64,0},{80,16},{96,32},{112,48},{1... | collective-permute-start | bytes 147464 | tf_op jit(solution)/shard_map/ppermute | solution.py:365
  181.1 17.9 %collective-permute-start.15 = (f32[48,256]{1,0:T(8,128)S(1)}, f32[48,256]{1,0:T(8,128)S(1)}, u32[]{:S(2)}, u32[]{:S(2)}) collective-permute-start(f32[48,256]{1,0:T(8,128)S(1)} %get-tuple-element.34), channel_id=1, source_target_pairs={{0,0},{1,256},{16,16},{17,272},{32,32},{33,288},{48,48},{49,304},{... | collective-permute-start | bytes 147464 | tf_op jit(solution)/shard_map/ppermute | solution.py:379
  186.3 15.6 %collective-permute-start.16 = (f32[48,256]{1,0:T(8,128)S(1)}, f32[48,256]{1,0:T(8,128)S(1)}, u32[]{:S(2)}, u32[]{:S(2)}) collective-permute-start(f32[48,256]{1,0:T(8,128)S(1)} %get-tuple-element.33), channel_id=1, source_target_pairs={{0,128},{1,384},{16,144},{17,400},{32,160},{33,416},{48,176},{49,4... | collective-permute-start | bytes 147464 | tf_op jit(solution)/shard_map/ppermute | solution.py:380
  199.0 0.6 copy-start.21

commit v4 on v3

--- a/solution.py
+++ b/solution.py
@@ -131,7 +131,7 @@
         ],
         out_shape=[
             jax.ShapeDtypeStruct((rows, 2 * HEAD_DIM), BF16),
-            jax.ShapeDtypeStruct((2, count, 3 * TILE, TILE), BF16),
+            pltpu.HBM((2, count, 3 * TILE, TILE), BF16),
         ],
         compiler_params=pltpu.CompilerParams(vmem_limit_bytes=40 * 1024 * 1024),
         cost_estimate=pl.CostEstimate(
@@ -162,7 +162,7 @@
             pl.BlockSpec((TILE, 4 * HEAD_DIM), lambda h: (0, 0)),
         ],
         out_shape=[
-            jax.ShapeDtypeStruct((rows, 6 * HEAD_DIM), BF16),
+            pltpu.HBM((rows, 6 * HEAD_DIM), BF16),
             jax.ShapeDtypeStruct((TILE, 4 * HEAD_DIM), BF16),
             jax.ShapeDtypeStruct((TILE, 4 * HEAD_DIM), BF16),
         ],
@@ -235,7 +235,7 @@
             scratch_shapes=[pltpu.VMEM((half, both), BF16)],
         ),
         out_shape=[
-            jax.ShapeDtypeStruct((rows, width), F32),
+            pltpu.HBM((rows, width), F32),
             jax.ShapeDtypeStruct((rows, width), BF16),
         ],
         compiler_params=pltpu.CompilerParams(vmem_limit_bytes=40 * 1024 * 1024),
@@ -282,7 +282,7 @@
             jax.ShapeDtypeStruct((size, depth, 2 * width), F32),
             jax.ShapeDtypeStruct((size, depth, 2 * width), BF16),
         ],
-        compiler_params=pltpu.CompilerParams(vmem_limit_bytes=40 * 1024 * 1024),
+        compiler_params=pltpu.CompilerParams(vmem_limit_bytes=60 * 1024 * 1024),
         cost_estimate=pl.CostEstimate(
             flops=2 * rows * half * 2 * width, bytes_accessed=7 << 20, transcendentals=0
         ),

time: 205 us -> 200 us (0.976)
  local copies, waits for them, and re-layouts: 15.9 us -> 9.24 us
  Pallas kernels: 29.4 us -> 31.9 us
    unnamed x50 -> x36, local copies, waits for them, and re-layouts: 11.8 us -> 5.12 us
  transfers between devices with their start and end apart: 20 -> 20, of which waited for: 8 -> 8; matrix products, arithmetic and copies ran while one was open for 5% -> 5% of each run, Pallas kernels for 13% -> 14%
where the time goes in v4:
time: 200 us; the launch traced here: 199 us
  starting transfers between devices  72.1 us (36%)
  blocking collectives  39.9 us (20%)
  waiting for transfers between devices  37.1 us (19%)
  Pallas kernels  31.9 us (16%)
  local copies, waits for them, and re-layouts  9.24 us (5%)
  other arithmetic  7.53 us (4%)
    all_gather x1, blocking collectives, per_device(): owned = lax.all_gather(out_weight, 'z', axis=0)  39.9 us
    ppermute x6, waiting for transfers between devices, swapped(): return lax.ppermute(array, axis, [(0, 1), (1, 0)])  17.8 us
    ppermute x6, starting transfers between devices, swapped(): return lax.ppermute(array, axis, [(0, 1), (1, 0)])  17.6 us
    ppermute x4, starting transfers between devices, to_neighbours(): return (lax.ppermute(up_part, SEQ, up), lax.ppermute(down_part, SEQ, down))  12 us
    ppermute x3, waiting for transfers between devices, reduced_along_z(): lax.ppermute(send.astype(BF16), 'z', [(i, i ^ step) for i in range(size)])  11.2 us
    ppermute x1, starting transfers between devices, reduced_along_z(): far = lax.ppermute(send, axes, pairs(step))  9.12 us
    ppermute x3, starting transfers between devices, reduced_along_z(): lax.ppermute(send.astype(BF16), 'z', [(i, i ^ step) for i in range(size)])  8.35 us
    pallas_call x1, Pallas kernels, attention_backward(): pl.pallas_call(backward_kernel, grid=(2,), in_specs=tile_specs(rows) + [p...  6.95 us
  transfers between devices with their start and end apart: 20, of which 8 were waited for; matrix products, arithmetic and copies ran while one was open for 5% of the time, Pallas kernels for 14%

profile of v4, /device:TPU:8, one launch (start us, length us, event | category | flops | bytes accessed | tf_op | source)
XLA Modules:
  0.0 198.9 jit_solution(14705603210032079313)
XLA Ops:
  0.6 3.6 %pack.1 = bf16[8,128,768]{2,1,0:T(8,128)(2,1)} custom-call(bf16[128,2048]{1,0:T(8,128)(2,1)} %q.1, bf16[128,2048]{1,0:T(8,128)(2,1)} %k.1, bf16[128,2048]{1,0:T(8,128)(2,1)} %v.1), custom_call_target="tpu_custom_call" | custom-call | bytes 3145728 | tf_op jit(solution)/shard_map/pack/pallas_call | solution.py:191
  4.3 6.2 %all-to-all-start = ((bf16[8,128,768]{2,1,0:T(8,128)(2,1)}), bf16[8,128,768]{2,1,0:T(8,128)(2,1)S(1)}, u32[]{:S(2)}, u32[]{:S(2)}) async-start(bf16[8,128,768]{2,1,0:T(8,128)(2,1)} %pack.1), calls=%async_computation | async-start | bytes 3145728 | tf_op jit(solution)/shard_map/all_to_all | solution.py:407
  10.5 5.4 %collective-permute-start.2 = (bf16[128,1536]{1,0:T(8,128)(2,1)S(1)}, bf16[128,1536]{1,0:T(8,128)(2,1)S(1)}, u32[]{:S(2)}, u32[]{:S(2)}) collective-permute-start(bf16[128,1536]{1,0:T(8,128)(2,1)S(1)} %constant_dynamic-slice_fusion), channel_id=1, source_target_pairs={{0,1},{1,0},{2,3},{3,2},{4,5},{5,4},{6,7},{7,6},{8,9},{9,8},{10,11... | collective-permute-start | bytes 1179656 | tf_op jit(solution)/shard_map/ppermute | solution.py:335
  15.9 39.9 %all-gather = bf16[768,256]{1,0:T(8,128)(2,1)} all-gather(bf16[48,256]{1,0:T(8,128)(2,1)S(1)} %copy-done.15), channel_id=2, replica_groups=mesh['ylo'=2,'z'=16,'core'=2,'x'=4,'yhi'=2] {'z'}, dimensions={0}, use_global_device_ids=true | all-gather | bytes 417792 | tf_op jit(solution)/shard_map/all_gather | solution.py:395
  56.1 2.1 %broadcast_in_dim.16.refs_0_ = bf16[4,256,1536]{2,1,0:T(8,128)(2,1)} broadcast(bf16[256,1536]{1,0:T(8,128)(2,1)S(1)} %pad_maximum_fusion), dimensions={1,2} | broadcast | bytes 3932160 | tf_op jit(solution)/shard_map/broadcast_in_dim | solution.py:404
  58.3 4.8 %all-to-all-start.1 = ((bf16[4,256,1536]{2,1,0:T(8,128)(2,1)}), bf16[4,256,1536]{2,1,0:T(8,128)(2,1)}, u32[]{:S(2)}, u32[]{:S(2)}) async-start(bf16[4,256,1536]{2,1,0:T(8,128)(2,1)} %tie.3), calls=%async_computation.1 | async-start | bytes 6291456 | tf_op jit(solution)/shard_map/all_to_all | solution.py:411
  63.1 1.9 collective-permute-start.3
  65.0 1.9 collective-permute-start
  67.0 5.8 %collective-permute-start.1 = (bf16[256,512]{1,0:T(8,128)(2,1)S(1)}, bf16[256,512]{1,0:T(8,128)(2,1)S(1)}, u32[]{:S(2)}, u32[]{:S(2)}) collective-permute-start(bf16[256,512]{1,0:T(8,128)(2,1)S(1)} %get-tuple-element.29), channel_id=1, source_target_pairs={{8,0},{16,8},{24,16},{32,24},{40,32},{48,40},{56,48},{64,56},{72,6... | collective-permute-start | bytes 786440 | tf_op jit(solution)/shard_map/ppermute | solution.py:353
  72.7 1.9 collective-permute-start.4
  75.0 1.7 collective-permute-done.1.ka.va
  76.6 6.8 %forward.1 = (bf16[1024,256]{1,0:T(8,128)(2,1)S(1)}, bf16[2,4,768,256]{3,2,1,0:T(8,128)(2,1)}) custom-call(f32[2]{0:T(128)S(1)} %add_select_fusion.bias, bf16[1024,768]{1,0:T(8,128)(2,1)S(1)} %bitcast.43, bf16[1024,768]{1,0:T(8,128)(2,1)S(1)} %bitcast.44, bf16[1024,768]{1,0:T(8,128)(2,1)S(1)} %bitcast.45, bf16[256,512]{1,0:T(8,128)(2,1)S(1)} %collective-permute-done.kb.vb, ...), custom_call_target="tpu_custom_call" | custom-call | flops 805306368 | bytes 6291456 | tf_op jit(solution)/shard_map/forward/pallas_call | solution.py:124
  83.5 1.9 collective-permute-start.6
  85.5 2.0 pad_maximum_fusion.1.refs_0_
  87.5 1.9 collective-permute-start.5
  89.4 0.6 pad_add_fusion.where
  90.0 9.1 %collective-permute-done.6.attn_other = bf16[1024,256]{1,0:T(8,128)(2,1)} collective-permute-done((bf16[1024,256]{1,0:T(8,128)(2,1)S(1)}, bf16[1024,256]{1,0:T(8,128)(2,1)}, u32[]{:S(2)}, u32[]{:S(2)}) %collective-permute-start.6) | collective-permute-done | bytes 524320 | tf_op jit(solution)/shard_map/ppermute | solution.py:335
  99.1 6.5 %projection.1 = (f32[16,48,512]{2,1,0:T(8,128)}, bf16[16,48,512]{2,1,0:T(8,128)(2,1)}) custom-call(s32[2]{0:T(128)} %pad_add_fusion.where, bf16[1024,1536]{1,0:T(8,128)(2,1)} %bitcast.6.og, bf16[1024,256]{1,0:T(8,128)(2,1)} %copy-done.3, bf16[1024,256]{1,0:T(8,128)(2,1)} %collective-permute-done.6.attn_other, bf16[16,48,512]{2,1,0:T(8,128)(2,1)} %tie.4.first.own), custom_call_target="tpu_custom_call" | custom-call | flops 1610612736 | bytes 7340032 | tf_op jit(solution)/shard_map/projection/pallas_call | solution.py:271
  105.6 1.9 collective-permute-start.8
  107.6 1.1 copy-done.5
  108.7 5.8 %dout.1 = (f32[1024,256]{1,0:T(8,128)}, bf16[1024,256]{1,0:T(8,128)(2,1)S(1)}) custom-call(s32[2]{0:T(128)S(1)} %copy-done.6, bf16[1024,1536]{1,0:T(8,128)(2,1)} %bitcast.6.og, bf16[16,48,512]{2,1,0:T(8,128)(2,1)S(1)} %copy-done.2, bf16[16,48,512]{2,1,0:T(8,128)(2,1)} %collective-permute-done.5.other, bf16[16,48,512]{2,1,0:T(8,128)(2,1)S(1)} %copy-done.5), custom_call_target="tpu_custom_call" | custom-call | flops 1610612736 | bytes 7340032 | tf_op jit(solution)/shard_map/dout/pallas_call | solution.py:227
  114.5 2.2 %collective-permute-start.7 = (bf16[1024,256]{1,0:T(8,128)(2,1)S(1)}, bf16[1024,256]{1,0:T(8,128)(2,1)S(1)}, u32[]{:S(2)}, u32[]{:S(2)}) collective-permute-start(bf16[1024,256]{1,0:T(8,128)(2,1)S(1)} %get-tuple-element.17), channel_id=1, source_target_pairs={{0,1},{1,0},{2,3},{3,2},{4,5},{5,4},{6,7},{7,6},{8,9},{9,8},{10,11... | collective-permute-start | bytes 1572872 | tf_op jit(solution)/shard_map/ppermute | solution.py:335
  116.7 2.0 %convert_add_fusion = f32[16,48,512]{2,1,0:T(8,128)S(1)} fusion(f32[16,48,512]{2,1,0:T(8,128)} %get-tuple-element.18, bf16[16,48,512]{2,1,0:T(8,128)(2,1)} %collective-permute-done.8), kind=kLoop, calls=%fused_computation | loop fusion | flops 786432 | bytes 3932160 | tf_op jit(solution)/shard_map/add | solution.py:421
  118.8 0.9 slice.39.first
  119.6 4.3 %collective-permute-start.11 = (bf16[16,48,256]{2,1,0:T(8,128)(2,1)}, bf16[16,48,256]{2,1,0:T(8,128)(2,1)}, u32[]{:S(2)}, u32[]{:S(2)}) collective-permute-start(bf16[16,48,256]{2,1,0:T(8,128)(2,1)} %slice.39.first), channel_id=1, source_target_pairs={{0,256},{256,0},{1,257},{257,1},{2,258},{258,2},{3,259},{259,3},{4... | collective-permute-start | bytes 1179656 | tf_op jit(solution)/shard_map/ppermute | solution.py:335
  123.9 8.7 %collective-permute-done.7.recv = bf16[1024,256]{1,0:T(8,128)(2,1)S(1)} collective-permute-done((bf16[1024,256]{1,0:T(8,128)(2,1)S(1)}, bf16[1024,256]{1,0:T(8,128)(2,1)S(1)}, u32[]{:S(2)}, u32[]{:S(2)}) %collective-permute-start.7) | collective-permute-done | bytes 524320 | tf_op jit(solution)/shard_map/ppermute | solution.py:335
  132.6 6.9 %backward.1 = (bf16[1024,768]{1,0:T(8,128)(2,1)}, bf16[256,512]{1,0:T(8,128)(2,1)S(1)}, bf16[256,512]{1,0:T(8,128)(2,1)S(1)}) custom-call(bf16[1024,768]{1,0:T(8,128)(2,1)S(1)} %bitcast.46, bf16[1024,768]{1,0:T(8,128)(2,1)S(1)} %bitcast.47, bf16[1024,768]{1,0:T(8,128)(2,1)S(1)} %bitcast.48, bf16[256,512]{1,0:T(8,128)(2,1)S(1)} %collective-permute-done.kb.vb, ...), custom_call_target="tpu_custom_call" | custom-call | flops 161061273600 | bytes 9437184 | tf_op jit(solution)/shard_map/backward/pallas_call | solution.py:149
  139.6 1.9 collective-permute-start.10
  141.5 2.4 %collective-permute-start.9 = (bf16[256,512]{1,0:T(8,128)(2,1)S(1)}, bf16[256,512]{1,0:T(8,128)(2,1)S(1)}, u32[]{:S(2)}, u32[]{:S(2)}) collective-permute-start(bf16[256,512]{1,0:T(8,128)(2,1)S(1)} %get-tuple-element.20), channel_id=1, source_target_pairs={{0,8},{8,16},{16,24},{24,32},{32,40},{40,48},{48,56},{56,64},{64,7... | collective-permute-start | bytes 786440 | tf_op jit(solution)/shard_map/ppermute | solution.py:353
  143.9 1.1 slice_add_fusion
  145.1 2.4 %collective-permute-start.12 = (bf16[8,48,256]{2,1,0:T(8,128)(2,1)S(1)}, bf16[8,48,256]{2,1,0:T(8,128)(2,1)S(1)}, u32[]{:S(2)}, u32[]{:S(2)}) collective-permute-start(bf16[8,48,256]{2,1,0:T(8,128)(2,1)S(1)} %fusion), channel_id=1, source_target_pairs={{0,16},{16,0},{32,48},{48,32},{64,80},{80,64},{96,112},{112,96},{1... | collective-permute-start | bytes 589832 | tf_op jit(solution)/shard_map/ppermute | solution.py:365
  147.5 3.8 %collective-permute-done.9.low = bf16[256,512]{1,0:T(8,128)(2,1)S(1)} collective-permute-done((bf16[256,512]{1,0:T(8,128)(2,1)S(1)}, bf16[256,512]{1,0:T(8,128)(2,1)S(1)}, u32[]{:S(2)}, u32[]{:S(2)}) %collective-permute-start.9) | collective-permute-done | bytes 262176 | tf_op jit(solution)/shard_map/ppermute | solution.py:353
  151.3 0.7 copy-done.13
  152.0 2.1 %edges.1 = bf16[1024,768]{1,0:T(8,128)(2,1)} custom-call(bf16[1024,768]{1,0:T(8,128)(2,1)} %get-tuple-element.19.dx, bf16[256,512]{1,0:T(8,128)(2,1)} %copy-done.13, bf16[256,512]{1,0:T(8,128)(2,1)} %copy-done.12), custom_call_target="tpu_custom_call", output_to_operand_aliasing={{}: (0, {})} | custom-call | bytes 2097152 | tf_op jit(solution)/shard_map/edges/pallas_call | solution.py:305
  154.1 5.1 %all-to-all-start.2 = ((bf16[8,128,768]{2,1,0:T(8,128)(2,1)}), bf16[8,128,768]{2,1,0:T(8,128)(2,1)S(1)}, u32[]{:S(2)}, u32[]{:S(2)}) async-start(bf16[8,128,768]{2,1,0:T(8,128)(2,1)} %bitcast.49), calls=%async_computation.2 | async-start | bytes 3145728 | tf_op jit(solution)/shard_map/all_to_all | solution.py:433
  159.3 1.9 collective-permute-start.13
  161.2 5.4 %collective-permute-done.13 = bf16[4,48,256]{2,1,0:T(8,128)(2,1)S(1)} collective-permute-done((bf16[4,48,256]{2,1,0:T(8,128)(2,1)S(1)}, bf16[4,48,256]{2,1,0:T(8,128)(2,1)S(1)}, u32[]{:S(2)}, u32[]{:S(2)}) %collective-permute-start.13) | collective-permute-done | bytes 98336 | tf_op jit(solution)/shard_map/ppermute | solution.py:365
  166.7 4.1 %collective-permute-start.14 = (bf16[2,48,256]{2,1,0:T(8,128)(2,1)S(1)}, bf16[2,48,256]{2,1,0:T(8,128)(2,1)S(1)}, u32[]{:S(2)}, u32[]{:S(2)}) collective-permute-start(bf16[2,48,256]{2,1,0:T(8,128)(2,1)S(1)} %fusion.2), channel_id=1, source_target_pairs={{0,64},{16,80},{32,96},{48,112},{64,0},{80,16},{96,32},{112,48},{1... | collective-permute-start | bytes 147464 | tf_op jit(solution)/shard_map/ppermute | solution.py:365
  170.8 5.8 %collective-permute-done.14 = bf16[2,48,256]{2,1,0:T(8,128)(2,1)S(1)} collective-permute-done((bf16[2,48,256]{2,1,0:T(8,128)(2,1)S(1)}, bf16[2,48,256]{2,1,0:T(8,128)(2,1)S(1)}, u32[]{:S(2)}, u32[]{:S(2)}) %collective-permute-start.14) | collective-permute-done | bytes 49184 | tf_op jit(solution)/shard_map/ppermute | solution.py:365
  176.7 5.2 %collective-permute-start.15 = (f32[48,256]{1,0:T(8,128)S(1)}, f32[48,256]{1,0:T(8,128)S(1)}, u32[]{:S(2)}, u32[]{:S(2)}) collective-permute-start(f32[48,256]{1,0:T(8,128)S(1)} %get-tuple-element.34), channel_id=1, source_target_pairs={{0,0},{1,256},{16,16},{17,272},{32,32},{33,288},{48,48},{49,304},{... | collective-permute-start | bytes 147464 | tf_op jit(solution)/shard_map/ppermute | solution.py:379
  181.9 9.1 %collective-permute-start.16 = (f32[48,256]{1,0:T(8,128)S(1)}, f32[48,256]{1,0:T(8,128)S(1)}, u32[]{:S(2)}, u32[]{:S(2)}) collective-permute-start(f32[48,256]{1,0:T(8,128)S(1)} %get-tuple-element.33), channel_id=1, source_target_pairs={{0,128},{1,384},{16,144},{17,400},{32,160},{33,416},{48,176},{49,4... | collective-permute-start | bytes 147464 | tf_op jit(solution)/shard_map/ppermute | solution.py:380
  191.2 0.8 copy.28
  192.0 0.3 copy.25
  192.3 1.0 copy.23
  193.6 1.0 copy.24
  194.6 0.6 copy-done.14
  195.2 2.3 %collective-permute-done.16 = f32[48,256]{1,0:T(8,128)S(1)} collective-permute-done((f32[48,256]{1,0:T(8,128)S(1)}, f32[48,256]{1,0:T(8,128)S(1)}, u32[]{:S(2)}, u32[]{:S(2)}) %collective-permute-start.16) | collective-permute-done | bytes 49184 | tf_op jit(solution)/shard_map/ppermute | solution.py:380
  197.5 1.4 add.96
  (60 shorter events, 1.3 us)
Async XLA Ops:
  4.3 6.2 %copy-start.11 = (bf16[128,3072]{1,0:T(8,128)(2,1)S(1)}, bf16[128,3072]{1,0:T(8,128)(2,1)}, u32[]{:S(2)}) copy-start(bf16[128,3072]{1,0:T(8,128)(2,1)} %param.8) | copy-start | bytes 2359300
  4.3 11.6 %copy-start.15 = (bf16[48,256]{1,0:T(8,128)(2,1)S(1)}, bf16[48,256]{1,0:T(8,128)(2,1)}, u32[]{:S(2)}) copy-start(bf16[48,256]{1,0:T(8,128)(2,1)} %param.9) | copy-start | bytes 73732
  4.3 51.8 %all-to-all-start = ((bf16[8,128,768]{2,1,0:T(8,128)(2,1)}), bf16[8,128,768]{2,1,0:T(8,128)(2,1)S(1)}, u32[]{:S(2)}, u32[]{:S(2)}) async-start(bf16[8,128,768]{2,1,0:T(8,128)(2,1)} %pack.1), calls=%async_computation | async-start | bytes 3145728 | tf_op jit(solution)/shard_map/all_to_all | solution.py:407
  10.5 45.4 %collective-permute-start.2 = (bf16[128,1536]{1,0:T(8,128)(2,1)S(1)}, bf16[128,1536]{1,0:T(8,128)(2,1)S(1)}, u32[]{:S(2)}, u32[]{:S(2)}) collective-permute-start(bf16[128,1536]{1,0:T(8,128)(2,1)S(1)} %constant_dynamic-slice_fusion), channel_id=1, source_target_pairs={{0,1},{1,0},{2,3},{3,2},{4,5},{5,4},{6,7},{7,6},{8,9},{9,8},{10,11... | collective-permute-start | bytes 1179656 | tf_op jit(solution)/shard_map/ppermute | solution.py:335
  56.1 2.2 %copy-start = (bf16[8,128,768]{2,1,0:T(8,128)(2,1)}, bf16[8,128,768]{2,1,0:T(8,128)(2,1)S(1)}, u32[]{:S(2)}) copy-start(bf16[8,128,768]{2,1,0:T(8,128)(2,1)S(1)} %all-to-all-done) | copy-start | bytes 4718596
  58.3 4.8 %copy-start.10 = (bf16[768,256]{1,0:T(8,128)(2,1)S(1)}, bf16[768,256]{1,0:T(8,128)(2,1)}, u32[]{:S(2)}) copy-start(bf16[768,256]{1,0:T(8,128)(2,1)} %all-gather) | copy-start | bytes 1179652
  58.3 6.7 %copy-start.1 = (bf16[8,128,768]{2,1,0:T(8,128)(2,1)S(1)}, bf16[8,128,768]{2,1,0:T(8,128)(2,1)}, u32[]{:S(2)}) copy-start(bf16[8,128,768]{2,1,0:T(8,128)(2,1)} %copy-done) | copy-start | bytes 4718596
  58.3 40.8 %all-to-all-start.1 = ((bf16[4,256,1536]{2,1,0:T(8,128)(2,1)}), bf16[4,256,1536]{2,1,0:T(8,128)(2,1)}, u32[]{:S(2)}, u32[]{:S(2)}) async-start(bf16[4,256,1536]{2,1,0:T(8,128)(2,1)} %tie.3), calls=%async_computation.1 | async-start | bytes 6291456 | tf_op jit(solution)/shard_map/all_to_all | solution.py:411
  63.1 22.3 %collective-permute-start.3 = (bf16[16,48,256]{2,1,0:T(8,128)(2,1)S(1)}, bf16[16,48,256]{2,1,0:T(8,128)(2,1)S(1)}, u32[]{:S(2)}, u32[]{:S(2)}) collective-permute-start(bf16[16,48,256]{2,1,0:T(8,128)(2,1)S(1)} %bitcast.51), channel_id=1, source_target_pairs={{1,256},{256,1},{3,258},{258,3},{5,260},{260,5},{7,262},{262,7},{9... | collective-permute-start | bytes 1179656 | tf_op jit(solution)/shard_map/ppermute | solution.py:345
  65.0 9.9 %collective-permute-start = (bf16[256,512]{1,0:T(8,128)(2,1)S(1)}, bf16[256,512]{1,0:T(8,128)(2,1)S(1)}, u32[]{:S(2)}, u32[]{:S(2)}) collective-permute-start(bf16[256,512]{1,0:T(8,128)(2,1)S(1)} %get-tuple-element.30), channel_id=1, source_target_pairs={{0,8},{8,16},{16,24},{24,32},{32,40},{40,48},{48,56},{56,64},{64,7... | collective-permute-start | bytes 786440 | tf_op jit(solution)/shard_map/ppermute | solution.py:353
  67.0 9.7 %collective-permute-start.1 = (bf16[256,512]{1,0:T(8,128)(2,1)S(1)}, bf16[256,512]{1,0:T(8,128)(2,1)S(1)}, u32[]{:S(2)}, u32[]{:S(2)}) collective-permute-start(bf16[256,512]{1,0:T(8,128)(2,1)S(1)} %get-tuple-element.29), channel_id=1, source_target_pairs={{8,0},{16,8},{24,16},{32,24},{40,32},{48,40},{56,48},{64,56},{72,6... | collective-permute-start | bytes 786440 | tf_op jit(solution)/shard_map/ppermute | solution.py:353
  72.7 12.7 %collective-permute-start.4 = (bf16[16,48,256]{2,1,0:T(8,128)(2,1)S(1)}, bf16[16,48,256]{2,1,0:T(8,128)(2,1)}, u32[]{:S(2)}, u32[]{:S(2)}) collective-permute-start(bf16[16,48,256]{2,1,0:T(8,128)(2,1)S(1)} %bitcast.52), channel_id=1, source_target_pairs={{0,256},{257,1},{1,0},{256,257},{2,258},{259,3},{3,2},{258,259},{4... | collective-permute-start | bytes 1179656 | tf_op jit(solution)/shard_map/ppermute | solution.py:344
  83.5 4.0 %copy-start.3 = (bf16[1024,256]{1,0:T(8,128)(2,1)}, bf16[1024,256]{1,0:T(8,128)(2,1)S(1)}, u32[]{:S(2)}) copy-start(bf16[1024,256]{1,0:T(8,128)(2,1)S(1)} %get-tuple-element.14.refs_1_.attn) | copy-start | bytes 1572868
  83.5 15.6 %collective-permute-start.6 = (bf16[1024,256]{1,0:T(8,128)(2,1)S(1)}, bf16[1024,256]{1,0:T(8,128)(2,1)}, u32[]{:S(2)}, u32[]{:S(2)}) collective-permute-start(bf16[1024,256]{1,0:T(8,128)(2,1)S(1)} %get-tuple-element.14.refs_1_.attn), channel_id=1, source_target_pairs={{0,1},{1,0},{2,3},{3,2},{4,5},{5,4},{6,7},{7,6},{8,9},{9,8},{10,11... | collective-permute-start | bytes 1572872 | tf_op jit(solution)/shard_map/ppermute | solution.py:335
  87.5 20.1 %collective-permute-start.5 = (bf16[16,48,512]{2,1,0:T(8,128)(2,1)}, bf16[16,48,512]{2,1,0:T(8,128)(2,1)}, u32[]{:S(2)}, u32[]{:S(2)}) collective-permute-start(bf16[16,48,512]{2,1,0:T(8,128)(2,1)} %tie.4.first.own), channel_id=1, source_target_pairs={{0,8},{8,0},{1,9},{9,1},{2,10},{10,2},{3,11},{11,3},{4,12},{12,4},... | collective-permute-start | bytes 2359304 | tf_op jit(solution)/shard_map/ppermute | solution.py:335
  99.1 8.4 %copy-start.2 = (bf16[16,48,512]{2,1,0:T(8,128)(2,1)S(1)}, bf16[16,48,512]{2,1,0:T(8,128)(2,1)}, u32[]{:S(2)}) copy-start(bf16[16,48,512]{2,1,0:T(8,128)(2,1)} %tie.4.first.own) | copy-start | bytes 2359300
  99.1 8.4 %copy-start.6 = (s32[2]{0:T(128)S(1)}, s32[2]{0:T(128)}, u32[]{:S(2)}) copy-start(s32[2]{0:T(128)} %pad_add_fusion.where) | copy-start | bytes 28
  105.6 11.1 %collective-permute-start.8 = (bf16[16,48,512]{2,1,0:T(8,128)(2,1)}, bf16[16,48,512]{2,1,0:T(8,128)(2,1)}, u32[]{:S(2)}, u32[]{:S(2)}) collective-permute-start(bf16[16,48,512]{2,1,0:T(8,128)(2,1)} %get-tuple-element.15.first), channel_id=1, source_target_pairs={{0,8},{8,0},{1,9},{9,1},{2,10},{10,2},{3,11},{11,3},{4,12},{12,4},... | collective-permute-start | bytes 2359304 | tf_op jit(solution)/shard_map/ppermute | solution.py:335
  107.5 1.1 copy-start.5
  114.5 18.1 %collective-permute-start.7 = (bf16[1024,256]{1,0:T(8,128)(2,1)S(1)}, bf16[1024,256]{1,0:T(8,128)(2,1)S(1)}, u32[]{:S(2)}, u32[]{:S(2)}) collective-permute-start(bf16[1024,256]{1,0:T(8,128)(2,1)S(1)} %get-tuple-element.17), channel_id=1, source_target_pairs={{0,1},{1,0},{2,3},{3,2},{4,5},{5,4},{6,7},{7,6},{8,9},{9,8},{10,11... | collective-permute-start | bytes 1572872 | tf_op jit(solution)/shard_map/ppermute | solution.py:335
  116.7 15.9 %copy-start.4 = (bf16[2,4,768,256]{3,2,1,0:T(8,128)(2,1)S(1)}, bf16[2,4,768,256]{3,2,1,0:T(8,128)(2,1)}, u32[]{:S(2)}) copy-start(bf16[2,4,768,256]{3,2,1,0:T(8,128)(2,1)} %get-tuple-element.13.pt) | copy-start | bytes 9437188
  116.7 15.9 %copy-start.7 = (f32[1024,256]{1,0:T(8,128)S(1)}, f32[1024,256]{1,0:T(8,128)}, u32[]{:S(2)}) copy-start(f32[1024,256]{1,0:T(8,128)} %get-tuple-element.16.keep) | copy-start | bytes 3145732
  118.8 13.8 %copy-start.8 = (f32[16,48,512]{2,1,0:T(8,128)}, f32[16,48,512]{2,1,0:T(8,128)S(1)}, u32[]{:S(2)}) copy-start(f32[16,48,512]{2,1,0:T(8,128)S(1)} %convert_add_fusion) | copy-start | bytes 4718596
  119.6 24.2 %collective-permute-start.11 = (bf16[16,48,256]{2,1,0:T(8,128)(2,1)}, bf16[16,48,256]{2,1,0:T(8,128)(2,1)}, u32[]{:S(2)}, u32[]{:S(2)}) collective-permute-start(bf16[16,48,256]{2,1,0:T(8,128)(2,1)} %slice.39.first), channel_id=1, source_target_pairs={{0,256},{256,0},{1,257},{257,1},{2,258},{258,2},{3,259},{259,3},{4... | collective-permute-start | bytes 1179656 | tf_op jit(solution)/shard_map/ppermute | solution.py:335
  132.6 11.3 %copy-start.9 = (f32[16,48,512]{2,1,0:T(8,128)S(1)}, f32[16,48,512]{2,1,0:T(8,128)}, u32[]{:S(2)}) copy-start(f32[16,48,512]{2,1,0:T(8,128)} %copy-done.8) | copy-start | bytes 4718596
  139.6 7.9 %collective-permute-start.10 = (bf16[256,512]{1,0:T(8,128)(2,1)S(1)}, bf16[256,512]{1,0:T(8,128)(2,1)S(1)}, u32[]{:S(2)}, u32[]{:S(2)}) collective-permute-start(bf16[256,512]{1,0:T(8,128)(2,1)S(1)} %get-tuple-element.21), channel_id=1, source_target_pairs={{8,0},{16,8},{24,16},{32,24},{40,32},{48,40},{56,48},{64,56},{72,6... | collective-permute-start | bytes 786440 | tf_op jit(solution)/shard_map/ppermute | solution.py:353
  141.5 9.8 %collective-permute-start.9 = (bf16[256,512]{1,0:T(8,128)(2,1)S(1)}, bf16[256,512]{1,0:T(8,128)(2,1)S(1)}, u32[]{:S(2)}, u32[]{:S(2)}) collective-permute-start(bf16[256,512]{1,0:T(8,128)(2,1)S(1)} %get-tuple-element.20), channel_id=1, source_target_pairs={{0,8},{8,16},{16,24},{24,32},{32,40},{40,48},{48,56},{56,64},{64,7... | collective-permute-start | bytes 786440 | tf_op jit(solution)/shard_map/ppermute | solution.py:353
  145.1 14.1 %collective-permute-start.12 = (bf16[8,48,256]{2,1,0:T(8,128)(2,1)S(1)}, bf16[8,48,256]{2,1,0:T(8,128)(2,1)S(1)}, u32[]{:S(2)}, u32[]{:S(2)}) collective-permute-start(bf16[8,48,256]{2,1,0:T(8,128)(2,1)S(1)} %fusion), channel_id=1, source_target_pairs={{0,16},{16,0},{32,48},{48,32},{64,80},{80,64},{96,112},{112,96},{1... | collective-permute-start | bytes 589832 | tf_op jit(solution)/shard_map/ppermute | solution.py:365
  147.5 3.8 %copy-start.12 = (bf16[256,512]{1,0:T(8,128)(2,1)}, bf16[256,512]{1,0:T(8,128)(2,1)S(1)}, u32[]{:S(2)}) copy-start(bf16[256,512]{1,0:T(8,128)(2,1)S(1)} %collective-permute-done.10.high) | copy-start | bytes 786436
  151.3 0.7 copy-start.13
  154.1 36.9 %all-to-all-start.2 = ((bf16[8,128,768]{2,1,0:T(8,128)(2,1)}), bf16[8,128,768]{2,1,0:T(8,128)(2,1)S(1)}, u32[]{:S(2)}, u32[]{:S(2)}) async-start(bf16[8,128,768]{2,1,0:T(8,128)(2,1)} %bitcast.49), calls=%async_computation.2 | async-start | bytes 3145728 | tf_op jit(solution)/shard_map/all_to_all | solution.py:433
  159.3 7.4 %collective-permute-start.13 = (bf16[4,48,256]{2,1,0:T(8,128)(2,1)S(1)}, bf16[4,48,256]{2,1,0:T(8,128)(2,1)S(1)}, u32[]{:S(2)}, u32[]{:S(2)}) collective-permute-start(bf16[4,48,256]{2,1,0:T(8,128)(2,1)S(1)} %fusion.1), channel_id=1, source_target_pairs={{0,32},{16,48},{32,0},{48,16},{64,96},{80,112},{96,64},{112,80},{1... | collective-permute-start | bytes 294920 | tf_op jit(solution)/shard_map/ppermute | solution.py:365
  166.7 9.9 %collective-permute-start.14 = (bf16[2,48,256]{2,1,0:T(8,128)(2,1)S(1)}, bf16[2,48,256]{2,1,0:T(8,128)(2,1)S(1)}, u32[]{:S(2)}, u32[]{:S(2)}) collective-permute-start(bf16[2,48,256]{2,1,0:T(8,128)(2,1)S(1)} %fusion.2), channel_id=1, source_target_pairs={{0,64},{16,80},{32,96},{48,112},{64,0},{80,16},{96,32},{112,48},{1... | collective-permute-start | bytes 147464 | tf_op jit(solution)/shard_map/ppermute | solution.py:365
  176.7 17.9 %collective-permute-start.15 = (f32[48,256]{1,0:T(8,128)S(1)}, f32[48,256]{1,0:T(8,128)S(1)}, u32[]{:S(2)}, u32[]{:S(2)}) collective-permute-start(f32[48,256]{1,0:T(8,128)S(1)} %get-tuple-element.34), channel_id=1, source_target_pairs={{0,0},{1,256},{16,16},{17,272},{32,32},{33,288},{48,48},{49,304},{... | collective-permute-start | bytes 147464 | tf_op jit(solution)/shard_map/ppermute | solution.py:379
  181.9 15.6 %collective-permute-start.16 = (f32[48,256]{1,0:T(8,128)S(1)}, f32[48,256]{1,0:T(8,128)S(1)}, u32[]{:S(2)}, u32[]{:S(2)}) collective-permute-start(f32[48,256]{1,0:T(8,128)S(1)} %get-tuple-element.33), channel_id=1, source_target_pairs={{0,128},{1,384},{16,144},{17,400},{32,160},{33,416},{48,176},{49,4... | collective-permute-start | bytes 147464 | tf_op jit(solution)/shard_map/ppermute | solution.py:380
  194.6 0.6 copy-start.14

commit v5 on v4

--- a/solution.py
+++ b/solution.py
@@ -168,7 +168,7 @@
         ],
         compiler_params=pltpu.CompilerParams(vmem_limit_bytes=40 * 1024 * 1024),
         cost_estimate=pl.CostEstimate(
-            flops=100 * 2 * 4 * 2 * rows * 3 * TILE * HEAD_DIM,
+            flops=2 * 4 * 2 * rows * 3 * TILE * HEAD_DIM,
             bytes_accessed=9 * 1024 * 1024,
             transcendentals=0,
         ),
@@ -246,7 +246,7 @@
     )(where, og, own, other, first)
 
 
-def projection_kernel(where, og, attn, attn_other, first, mine, other, total):
+def projection_kernel(where, og, attn, attn_other, first, mine, rest, other, total):
     depth = mine.shape[1]
     width = attn.shape[1]
     near = pl.ds(pl.multiple_of((1 - where[1]) * width, width), width)
@@ -257,7 +257,8 @@
     for n in range(mine.shape[0]):
         first = pl.ds(pl.multiple_of(2 * n * depth + own, depth), depth)
         second = pl.ds(pl.multiple_of((2 * n + 1) * depth - own, depth), depth)
-        mine[n] = total[first, :]
+        mine[n] = total[first, :width]
+        rest[n] = total[first, width:].astype(BF16)
         other[n] = total[second, :].astype(BF16)
 
 
@@ -268,6 +269,7 @@
     steps = 4
     whole = pl.BlockSpec((rows, width), lambda i, w: (0, 0))
     part = pl.BlockSpec((size // steps, depth, 2 * width), lambda i, w: (i, 0, 0))
+    narrow = pl.BlockSpec((size // steps, depth, width), lambda i, w: (i, 0, 0))
     return pl.pallas_call(
         projection_kernel,
         grid_spec=pltpu.PrefetchScalarGridSpec(
@@ -275,11 +277,12 @@
             grid=(steps,),
             in_specs=[pl.BlockSpec((rows, half // steps), lambda i, w: (0, i)), whole, whole]
             + [pl.BlockSpec(memory_space=pl.ANY)],
-            out_specs=[part, part],
+            out_specs=[narrow, narrow, part],
             scratch_shapes=[pltpu.VMEM((half // steps, 2 * width), F32)],
         ),
         out_shape=[
-            jax.ShapeDtypeStruct((size, depth, 2 * width), F32),
+            jax.ShapeDtypeStruct((size, depth, width), F32),
+            jax.ShapeDtypeStruct((size, depth, width), BF16),
             jax.ShapeDtypeStruct((size, depth, 2 * width), BF16),
         ],
         compiler_params=pltpu.CompilerParams(vmem_limit_bytes=60 * 1024 * 1024),
@@ -417,10 +420,11 @@
     weight = tie(weight, attn)
     weight_other = swapped(weight, "core")
 
-    mine, other = projection_grad(where, og, attn, attn_other, weight, z_count)
-    grad = mine + swapped(other, "core").astype(F32)
-    far = grad[:, :, width:].astype(BF16)
-    parts = reduced_along_z(grad[:, :, :width] + swapped(far, "ylo").astype(F32))
+    near, far, other = projection_grad(where, og, attn, attn_other, weight, z_count)
+    from_core = swapped(other, "core").astype(F32)
+    far = (far.astype(F32) + from_core[:, :, width:]).astype(BF16)
+    near = near + from_core[:, :, :width]
+    parts = reduced_along_z(near + swapped(far, "ylo").astype(F32))
 
     dout_keep, dout_send = dout_parts(where, og, weight, weight_other, other)
     dout_recv = swapped(dout_send, "yhi")

time: 200 us -> 206 us (1.030)
  the two profiles are of different devices: /device:TPU:8 before, /device:TPU:14 now
where the time goes in v5:
time: 206 us; the launch traced here: 205 us
  starting transfers between devices  74.6 us (36%)
  blocking collectives  40 us (19%)
  waiting for transfers between devices  39.3 us (19%)
  Pallas kernels  32.5 us (16%)
  local copies, waits for them, and re-layouts  11.4 us (6%)
  other arithmetic  5.87 us (3%)
    all_gather x1, blocking collectives, per_device(): owned = lax.all_gather(out_weight, 'z', axis=0)  40 us
    ppermute x6, waiting for transfers between devices, swapped(): return lax.ppermute(array, axis, [(0, 1), (1, 0)])  19.6 us
    ppermute x6, starting transfers between devices, swapped(): return lax.ppermute(array, axis, [(0, 1), (1, 0)])  17.2 us
    ppermute x4, starting transfers between devices, to_neighbours(): return (lax.ppermute(up_part, SEQ, up), lax.ppermute(down_part, SEQ, down))  15.3 us
    ppermute x3, waiting for transfers between devices, reduced_along_z(): lax.ppermute(send.astype(BF16), 'z', [(i, i ^ step) for i in range(size)])  13.4 us
    ppermute x3, starting transfers between devices, reduced_along_z(): lax.ppermute(send.astype(BF16), 'z', [(i, i ^ step) for i in range(size)])  8.23 us
    unnamed x40, local copies, waits for them, and re-layouts  8.16 us
    ppermute x1, starting transfers between devices, reduced_along_z(): far = lax.ppermute(send, axes, pairs(step))  8.05 us
  transfers between devices with their start and end apart: 20, of which 8 were waited for; matrix products, arithmetic and copies ran while one was open for 4% of the time, Pallas kernels for 14%

profile of v5, /device:TPU:14, one launch (start us, length us, event | category | flops | bytes accessed | tf_op | source)
XLA Modules:
  0.0 204.9 jit_solution(2995995553267075869)
XLA Ops:
  0.6 3.7 %pack.1 = bf16[8,128,768]{2,1,0:T(8,128)(2,1)} custom-call(bf16[128,2048]{1,0:T(8,128)(2,1)} %q.1, bf16[128,2048]{1,0:T(8,128)(2,1)} %k.1, bf16[128,2048]{1,0:T(8,128)(2,1)} %v.1), custom_call_target="tpu_custom_call" | custom-call | bytes 3145728 | tf_op jit(solution)/shard_map/pack/pallas_call | solution.py:191
  4.3 6.6 %all-to-all-start = ((bf16[8,128,768]{2,1,0:T(8,128)(2,1)}), bf16[8,128,768]{2,1,0:T(8,128)(2,1)S(1)}, u32[]{:S(2)}, u32[]{:S(2)}) async-start(bf16[8,128,768]{2,1,0:T(8,128)(2,1)} %pack.1), calls=%async_computation | async-start | bytes 3145728 | tf_op jit(solution)/shard_map/all_to_all | solution.py:410
  11.0 4.9 %collective-permute-start.2 = (bf16[128,1536]{1,0:T(8,128)(2,1)S(1)}, bf16[128,1536]{1,0:T(8,128)(2,1)S(1)}, u32[]{:S(2)}, u32[]{:S(2)}) collective-permute-start(bf16[128,1536]{1,0:T(8,128)(2,1)S(1)} %constant_dynamic-slice_fusion), channel_id=1, source_target_pairs={{0,1},{1,0},{2,3},{3,2},{4,5},{5,4},{6,7},{7,6},{8,9},{9,8},{10,11... | collective-permute-start | bytes 1179656 | tf_op jit(solution)/shard_map/ppermute | solution.py:338
  15.9 40.0 %all-gather = bf16[768,256]{1,0:T(8,128)(2,1)} all-gather(bf16[48,256]{1,0:T(8,128)(2,1)S(1)} %copy-done.17), channel_id=2, replica_groups=mesh['ylo'=2,'z'=16,'core'=2,'x'=4,'yhi'=2] {'z'}, dimensions={0}, use_global_device_ids=true | all-gather | bytes 417792 | tf_op jit(solution)/shard_map/all_gather | solution.py:398
  56.1 2.1 %broadcast_in_dim.16.refs_0_ = bf16[4,256,1536]{2,1,0:T(8,128)(2,1)} broadcast(bf16[256,1536]{1,0:T(8,128)(2,1)S(1)} %pad_maximum_fusion), dimensions={1,2} | broadcast | bytes 3932160 | tf_op jit(solution)/shard_map/broadcast_in_dim | solution.py:407
  58.3 5.2 %all-to-all-start.1 = ((bf16[4,256,1536]{2,1,0:T(8,128)(2,1)}), bf16[4,256,1536]{2,1,0:T(8,128)(2,1)}, u32[]{:S(2)}, u32[]{:S(2)}) async-start(bf16[4,256,1536]{2,1,0:T(8,128)(2,1)} %tie.3), calls=%async_computation.1 | async-start | bytes 6291456 | tf_op jit(solution)/shard_map/all_to_all | solution.py:414
  63.5 1.9 collective-permute-start.3
  65.5 1.9 collective-permute-start
  67.4 5.8 %collective-permute-start.1 = (bf16[256,512]{1,0:T(8,128)(2,1)S(1)}, bf16[256,512]{1,0:T(8,128)(2,1)S(1)}, u32[]{:S(2)}, u32[]{:S(2)}) collective-permute-start(bf16[256,512]{1,0:T(8,128)(2,1)S(1)} %get-tuple-element.31), channel_id=1, source_target_pairs={{8,0},{16,8},{24,16},{32,24},{40,32},{48,40},{56,48},{64,56},{72,6... | collective-permute-start | bytes 786440 | tf_op jit(solution)/shard_map/ppermute | solution.py:356
  73.2 1.9 collective-permute-start.4
  75.4 1.7 collective-permute-done.1.ka.va
  77.1 6.8 %forward.1 = (bf16[1024,256]{1,0:T(8,128)(2,1)S(1)}, bf16[2,4,768,256]{3,2,1,0:T(8,128)(2,1)}) custom-call(f32[2]{0:T(128)S(1)} %add_select_fusion.bias, bf16[1024,768]{1,0:T(8,128)(2,1)S(1)} %bitcast.43, bf16[1024,768]{1,0:T(8,128)(2,1)S(1)} %bitcast.44, bf16[1024,768]{1,0:T(8,128)(2,1)S(1)} %bitcast.45, bf16[256,512]{1,0:T(8,128)(2,1)S(1)} %collective-permute-done.kb.vb, ...), custom_call_target="tpu_custom_call" | custom-call | flops 805306368 | bytes 6291456 | tf_op jit(solution)/shard_map/forward/pallas_call | solution.py:124
  83.9 1.9 collective-permute-start.6
  85.9 2.0 pad_maximum_fusion.1.refs_0_
  87.9 1.9 collective-permute-start.5
  89.8 0.6 pad_add_fusion.where
  90.4 9.2 %collective-permute-done.6.attn_other = bf16[1024,256]{1,0:T(8,128)(2,1)} collective-permute-done((bf16[1024,256]{1,0:T(8,128)(2,1)S(1)}, bf16[1024,256]{1,0:T(8,128)(2,1)}, u32[]{:S(2)}, u32[]{:S(2)}) %collective-permute-start.6) | collective-permute-done | bytes 524320 | tf_op jit(solution)/shard_map/ppermute | solution.py:338
  99.5 6.4 %projection.1 = (f32[16,48,256]{2,1,0:T(8,128)}, bf16[16,48,256]{2,1,0:T(8,128)(2,1)}, bf16[16,48,512]{2,1,0:T(8,128)(2,1)}) custom-call(s32[2]{0:T(128)} %pad_add_fusion.where, bf16[1024,1536]{1,0:T(8,128)(2,1)} %bitcast.6.og, bf16[1024,256]{1,0:T(8,128)(2,1)} %copy-done.5, bf16[1024,256]{1,0:T(8,128)(2,1)} %collective-permute-done.6.attn_other, ...), custom_call_target="tpu_custom_call" | custom-call | flops 1610612736 | bytes 7340032 | tf_op jit(solution)/shard_map/projection/pallas_call | solution.py:273
  105.9 1.9 collective-permute-start.8
  107.8 1.1 copy-done.6
  109.0 5.9 %dout.1 = (f32[1024,256]{1,0:T(8,128)}, bf16[1024,256]{1,0:T(8,128)(2,1)}) custom-call(s32[2]{0:T(128)S(1)} %copy-done.7, bf16[1024,1536]{1,0:T(8,128)(2,1)} %bitcast.6.og, bf16[16,48,512]{2,1,0:T(8,128)(2,1)S(1)} %copy-done.2, bf16[16,48,512]{2,1,0:T(8,128)(2,1)} %collective-permute-done.5.other, bf16[16,48,512]{2,1,0:T(8,128)(2,1)S(1)} %copy-done.6), custom_call_target="tpu_custom_call" | custom-call | flops 1610612736 | bytes 7340032 | tf_op jit(solution)/shard_map/dout/pallas_call | solution.py:227
  114.8 2.3 %collective-permute-start.7 = (bf16[1024,256]{1,0:T(8,128)(2,1)}, bf16[1024,256]{1,0:T(8,128)(2,1)}, u32[]{:S(2)}, u32[]{:S(2)}) collective-permute-start(bf16[1024,256]{1,0:T(8,128)(2,1)} %get-tuple-element.18), channel_id=1, source_target_pairs={{0,1},{1,0},{2,3},{3,2},{4,5},{5,4},{6,7},{7,6},{8,9},{9,8},{10,11... | collective-permute-start | bytes 1572872 | tf_op jit(solution)/shard_map/ppermute | solution.py:338
  117.4 1.2 copy-done.8
  118.7 4.3 %collective-permute-start.11 = (bf16[16,48,256]{2,1,0:T(8,128)(2,1)S(1)}, bf16[16,48,256]{2,1,0:T(8,128)(2,1)}, u32[]{:S(2)}, u32[]{:S(2)}) collective-permute-start(bf16[16,48,256]{2,1,0:T(8,128)(2,1)S(1)} %fusion.1.first), channel_id=1, source_target_pairs={{0,256},{256,0},{1,257},{257,1},{2,258},{258,2},{3,259},{259,3},{4... | collective-permute-start | bytes 1179656 | tf_op jit(solution)/shard_map/ppermute | solution.py:338
  123.0 10.4 %collective-permute-done.7.recv = bf16[1024,256]{1,0:T(8,128)(2,1)} collective-permute-done((bf16[1024,256]{1,0:T(8,128)(2,1)}, bf16[1024,256]{1,0:T(8,128)(2,1)}, u32[]{:S(2)}, u32[]{:S(2)}) %collective-permute-start.7) | collective-permute-done | bytes 524320 | tf_op jit(solution)/shard_map/ppermute | solution.py:338
  133.4 1.9 copy-done.3
  135.3 7.6 %backward.1 = (bf16[1024,768]{1,0:T(8,128)(2,1)}, bf16[256,512]{1,0:T(8,128)(2,1)S(1)}, bf16[256,512]{1,0:T(8,128)(2,1)S(1)}) custom-call(bf16[1024,768]{1,0:T(8,128)(2,1)S(1)} %bitcast.46, bf16[1024,768]{1,0:T(8,128)(2,1)S(1)} %bitcast.47, bf16[1024,768]{1,0:T(8,128)(2,1)S(1)} %bitcast.48, bf16[256,512]{1,0:T(8,128)(2,1)S(1)} %collective-permute-done.kb.vb, ...), custom_call_target="tpu_custom_call" | custom-call | flops 1610612736 | bytes 9437184 | tf_op jit(solution)/shard_map/backward/pallas_call | solution.py:149
  142.9 1.9 collective-permute-start.9
  144.9 5.8 %collective-permute-start.10 = (bf16[256,512]{1,0:T(8,128)(2,1)S(1)}, bf16[256,512]{1,0:T(8,128)(2,1)S(1)}, u32[]{:S(2)}, u32[]{:S(2)}) collective-permute-start(bf16[256,512]{1,0:T(8,128)(2,1)S(1)} %get-tuple-element.22), channel_id=1, source_target_pairs={{8,0},{16,8},{24,16},{32,24},{40,32},{48,40},{56,48},{64,56},{72,6... | collective-permute-start | bytes 786440 | tf_op jit(solution)/shard_map/ppermute | solution.py:356
  150.6 1.2 fusion
  151.9 1.9 collective-permute-start.12
  153.8 0.7 collective-permute-done.10.high
  154.5 0.7 copy-done.15
  155.2 2.2 %edges.1 = bf16[1024,768]{1,0:T(8,128)(2,1)} custom-call(bf16[1024,768]{1,0:T(8,128)(2,1)} %get-tuple-element.20.dx, bf16[256,512]{1,0:T(8,128)(2,1)} %copy-done.14, bf16[256,512]{1,0:T(8,128)(2,1)} %copy-done.15), custom_call_target="tpu_custom_call", output_to_operand_aliasing={{}: (0, {})} | custom-call | bytes 2097152 | tf_op jit(solution)/shard_map/edges/pallas_call | solution.py:308
  157.4 4.8 %all-to-all-start.2 = ((bf16[8,128,768]{2,1,0:T(8,128)(2,1)}), bf16[8,128,768]{2,1,0:T(8,128)(2,1)S(1)}, u32[]{:S(2)}, u32[]{:S(2)}) async-start(bf16[8,128,768]{2,1,0:T(8,128)(2,1)} %bitcast.49), calls=%async_computation.2 | async-start | bytes 3145728 | tf_op jit(solution)/shard_map/all_to_all | solution.py:437
  162.2 1.9 collective-permute-start.13
  164.2 6.5 %collective-permute-done.13 = bf16[4,48,256]{2,1,0:T(8,128)(2,1)S(1)} collective-permute-done((bf16[4,48,256]{2,1,0:T(8,128)(2,1)S(1)}, bf16[4,48,256]{2,1,0:T(8,128)(2,1)S(1)}, u32[]{:S(2)}, u32[]{:S(2)}) %collective-permute-start.13) | collective-permute-done | bytes 98336 | tf_op jit(solution)/shard_map/ppermute | solution.py:368
  170.7 4.4 %collective-permute-start.14 = (bf16[2,48,256]{2,1,0:T(8,128)(2,1)S(1)}, bf16[2,48,256]{2,1,0:T(8,128)(2,1)S(1)}, u32[]{:S(2)}, u32[]{:S(2)}) collective-permute-start(bf16[2,48,256]{2,1,0:T(8,128)(2,1)S(1)} %fusion.4), channel_id=1, source_target_pairs={{0,64},{16,80},{32,96},{48,112},{64,0},{80,16},{96,32},{112,48},{1... | collective-permute-start | bytes 147464 | tf_op jit(solution)/shard_map/ppermute | solution.py:368
  175.2 7.0 %collective-permute-done.14 = bf16[2,48,256]{2,1,0:T(8,128)(2,1)S(1)} collective-permute-done((bf16[2,48,256]{2,1,0:T(8,128)(2,1)S(1)}, bf16[2,48,256]{2,1,0:T(8,128)(2,1)S(1)}, u32[]{:S(2)}, u32[]{:S(2)}) %collective-permute-start.14) | collective-permute-done | bytes 49184 | tf_op jit(solution)/shard_map/ppermute | solution.py:368
  182.2 5.3 %collective-permute-start.15 = (f32[48,256]{1,0:T(8,128)S(1)}, f32[48,256]{1,0:T(8,128)S(1)}, u32[]{:S(2)}, u32[]{:S(2)}) collective-permute-start(f32[48,256]{1,0:T(8,128)S(1)} %get-tuple-element.36), channel_id=1, source_target_pairs={{0,0},{1,256},{16,16},{17,272},{32,32},{33,288},{48,48},{49,304},{... | collective-permute-start | bytes 147464 | tf_op jit(solution)/shard_map/ppermute | solution.py:382
  187.4 8.1 %collective-permute-start.16 = (f32[48,256]{1,0:T(8,128)S(1)}, f32[48,256]{1,0:T(8,128)S(1)}, u32[]{:S(2)}, u32[]{:S(2)}) collective-permute-start(f32[48,256]{1,0:T(8,128)S(1)} %get-tuple-element.35), channel_id=1, source_target_pairs={{0,128},{1,384},{16,144},{17,400},{32,160},{33,416},{48,176},{49,4... | collective-permute-start | bytes 147464 | tf_op jit(solution)/shard_map/ppermute | solution.py:383
  195.6 0.8 copy.28
  196.8 1.0 copy.23
  197.8 0.3 copy.26
  198.1 1.0 copy.24
  199.1 0.6 copy-done.16
  199.7 3.7 %collective-permute-done.16 = f32[48,256]{1,0:T(8,128)S(1)} collective-permute-done((f32[48,256]{1,0:T(8,128)S(1)}, f32[48,256]{1,0:T(8,128)S(1)}, u32[]{:S(2)}, u32[]{:S(2)}) %collective-permute-start.16) | collective-permute-done | bytes 49184 | tf_op jit(solution)/shard_map/ppermute | solution.py:383
  203.4 1.4 add.100
  (64 shorter events, 1.6 us)
Async XLA Ops:
  4.3 6.6 %copy-start.11 = (bf16[128,3072]{1,0:T(8,128)(2,1)S(1)}, bf16[128,3072]{1,0:T(8,128)(2,1)}, u32[]{:S(2)}) copy-start(bf16[128,3072]{1,0:T(8,128)(2,1)} %param.8) | copy-start | bytes 2359300
  4.3 11.6 %copy-start.17 = (bf16[48,256]{1,0:T(8,128)(2,1)S(1)}, bf16[48,256]{1,0:T(8,128)(2,1)}, u32[]{:S(2)}) copy-start(bf16[48,256]{1,0:T(8,128)(2,1)} %param.9) | copy-start | bytes 73732
  4.3 51.8 %all-to-all-start = ((bf16[8,128,768]{2,1,0:T(8,128)(2,1)}), bf16[8,128,768]{2,1,0:T(8,128)(2,1)S(1)}, u32[]{:S(2)}, u32[]{:S(2)}) async-start(bf16[8,128,768]{2,1,0:T(8,128)(2,1)} %pack.1), calls=%async_computation | async-start | bytes 3145728 | tf_op jit(solution)/shard_map/all_to_all | solution.py:410
  11.0 44.9 %collective-permute-start.2 = (bf16[128,1536]{1,0:T(8,128)(2,1)S(1)}, bf16[128,1536]{1,0:T(8,128)(2,1)S(1)}, u32[]{:S(2)}, u32[]{:S(2)}) collective-permute-start(bf16[128,1536]{1,0:T(8,128)(2,1)S(1)} %constant_dynamic-slice_fusion), channel_id=1, source_target_pairs={{0,1},{1,0},{2,3},{3,2},{4,5},{5,4},{6,7},{7,6},{8,9},{9,8},{10,11... | collective-permute-start | bytes 1179656 | tf_op jit(solution)/shard_map/ppermute | solution.py:338
  56.1 2.2 %copy-start = (bf16[8,128,768]{2,1,0:T(8,128)(2,1)}, bf16[8,128,768]{2,1,0:T(8,128)(2,1)S(1)}, u32[]{:S(2)}) copy-start(bf16[8,128,768]{2,1,0:T(8,128)(2,1)S(1)} %all-to-all-done) | copy-start | bytes 4718596
  58.3 5.2 %copy-start.10 = (bf16[768,256]{1,0:T(8,128)(2,1)S(1)}, bf16[768,256]{1,0:T(8,128)(2,1)}, u32[]{:S(2)}) copy-start(bf16[768,256]{1,0:T(8,128)(2,1)} %all-gather) | copy-start | bytes 1179652
  58.3 7.1 %copy-start.1 = (bf16[8,128,768]{2,1,0:T(8,128)(2,1)S(1)}, bf16[8,128,768]{2,1,0:T(8,128)(2,1)}, u32[]{:S(2)}) copy-start(bf16[8,128,768]{2,1,0:T(8,128)(2,1)} %copy-done) | copy-start | bytes 4718596
  58.3 41.3 %all-to-all-start.1 = ((bf16[4,256,1536]{2,1,0:T(8,128)(2,1)}), bf16[4,256,1536]{2,1,0:T(8,128)(2,1)}, u32[]{:S(2)}, u32[]{:S(2)}) async-start(bf16[4,256,1536]{2,1,0:T(8,128)(2,1)} %tie.3), calls=%async_computation.1 | async-start | bytes 6291456 | tf_op jit(solution)/shard_map/all_to_all | solution.py:414
  63.5 22.3 %collective-permute-start.3 = (bf16[16,48,256]{2,1,0:T(8,128)(2,1)S(1)}, bf16[16,48,256]{2,1,0:T(8,128)(2,1)S(1)}, u32[]{:S(2)}, u32[]{:S(2)}) collective-permute-start(bf16[16,48,256]{2,1,0:T(8,128)(2,1)S(1)} %bitcast.51), channel_id=1, source_target_pairs={{1,256},{256,1},{3,258},{258,3},{5,260},{260,5},{7,262},{262,7},{9... | collective-permute-start | bytes 1179656 | tf_op jit(solution)/shard_map/ppermute | solution.py:348
  65.5 9.9 %collective-permute-start = (bf16[256,512]{1,0:T(8,128)(2,1)S(1)}, bf16[256,512]{1,0:T(8,128)(2,1)S(1)}, u32[]{:S(2)}, u32[]{:S(2)}) collective-permute-start(bf16[256,512]{1,0:T(8,128)(2,1)S(1)} %get-tuple-element.32), channel_id=1, source_target_pairs={{0,8},{8,16},{16,24},{24,32},{32,40},{40,48},{48,56},{56,64},{64,7... | collective-permute-start | bytes 786440 | tf_op jit(solution)/shard_map/ppermute | solution.py:356
  67.4 9.7 %collective-permute-start.1 = (bf16[256,512]{1,0:T(8,128)(2,1)S(1)}, bf16[256,512]{1,0:T(8,128)(2,1)S(1)}, u32[]{:S(2)}, u32[]{:S(2)}) collective-permute-start(bf16[256,512]{1,0:T(8,128)(2,1)S(1)} %get-tuple-element.31), channel_id=1, source_target_pairs={{8,0},{16,8},{24,16},{32,24},{40,32},{48,40},{56,48},{64,56},{72,6... | collective-permute-start | bytes 786440 | tf_op jit(solution)/shard_map/ppermute | solution.py:356
  73.2 12.7 %collective-permute-start.4 = (bf16[16,48,256]{2,1,0:T(8,128)(2,1)S(1)}, bf16[16,48,256]{2,1,0:T(8,128)(2,1)}, u32[]{:S(2)}, u32[]{:S(2)}) collective-permute-start(bf16[16,48,256]{2,1,0:T(8,128)(2,1)S(1)} %bitcast.52), channel_id=1, source_target_pairs={{0,256},{257,1},{1,0},{256,257},{2,258},{259,3},{3,2},{258,259},{4... | collective-permute-start | bytes 1179656 | tf_op jit(solution)/shard_map/ppermute | solution.py:347
  83.9 4.0 %copy-start.5 = (bf16[1024,256]{1,0:T(8,128)(2,1)}, bf16[1024,256]{1,0:T(8,128)(2,1)S(1)}, u32[]{:S(2)}) copy-start(bf16[1024,256]{1,0:T(8,128)(2,1)S(1)} %get-tuple-element.15.refs_1_.attn) | copy-start | bytes 1572868
  83.9 15.6 %collective-permute-start.6 = (bf16[1024,256]{1,0:T(8,128)(2,1)S(1)}, bf16[1024,256]{1,0:T(8,128)(2,1)}, u32[]{:S(2)}, u32[]{:S(2)}) collective-permute-start(bf16[1024,256]{1,0:T(8,128)(2,1)S(1)} %get-tuple-element.15.refs_1_.attn), channel_id=1, source_target_pairs={{0,1},{1,0},{2,3},{3,2},{4,5},{5,4},{6,7},{7,6},{8,9},{9,8},{10,11... | collective-permute-start | bytes 1572872 | tf_op jit(solution)/shard_map/ppermute | solution.py:338
  87.9 20.0 %collective-permute-start.5 = (bf16[16,48,512]{2,1,0:T(8,128)(2,1)}, bf16[16,48,512]{2,1,0:T(8,128)(2,1)}, u32[]{:S(2)}, u32[]{:S(2)}) collective-permute-start(bf16[16,48,512]{2,1,0:T(8,128)(2,1)} %tie.4.first.own), channel_id=1, source_target_pairs={{0,8},{8,0},{1,9},{9,1},{2,10},{10,2},{3,11},{11,3},{4,12},{12,4},... | collective-permute-start | bytes 2359304 | tf_op jit(solution)/shard_map/ppermute | solution.py:338
  99.5 8.3 %copy-start.2 = (bf16[16,48,512]{2,1,0:T(8,128)(2,1)S(1)}, bf16[16,48,512]{2,1,0:T(8,128)(2,1)}, u32[]{:S(2)}) copy-start(bf16[16,48,512]{2,1,0:T(8,128)(2,1)} %tie.4.first.own) | copy-start | bytes 2359300
  99.5 8.3 %copy-start.7 = (s32[2]{0:T(128)S(1)}, s32[2]{0:T(128)}, u32[]{:S(2)}) copy-start(s32[2]{0:T(128)} %pad_add_fusion.where) | copy-start | bytes 28
  105.9 11.3 %collective-permute-start.8 = (bf16[16,48,512]{2,1,0:T(8,128)(2,1)}, bf16[16,48,512]{2,1,0:T(8,128)(2,1)S(1)}, u32[]{:S(2)}, u32[]{:S(2)}) collective-permute-start(bf16[16,48,512]{2,1,0:T(8,128)(2,1)} %get-tuple-element.16.first), channel_id=1, source_target_pairs={{0,8},{8,0},{1,9},{9,1},{2,10},{10,2},{3,11},{11,3},{4,12},{12,4},... | collective-permute-start | bytes 2359304 | tf_op jit(solution)/shard_map/ppermute | solution.py:338
  107.8 1.1 copy-start.6
  114.8 3.7 %copy-start.13 = (bf16[16,48,256]{2,1,0:T(8,128)(2,1)S(1)}, bf16[16,48,256]{2,1,0:T(8,128)(2,1)}, u32[]{:S(2)}) copy-start(bf16[16,48,256]{2,1,0:T(8,128)(2,1)} %get-tuple-element.19) | copy-start | bytes 1179652
  114.8 18.6 %copy-start.4 = (f32[1024,256]{1,0:T(8,128)S(1)}, f32[1024,256]{1,0:T(8,128)}, u32[]{:S(2)}) copy-start(f32[1024,256]{1,0:T(8,128)} %get-tuple-element.17.keep) | copy-start | bytes 3145732
  114.8 18.6 %collective-permute-start.7 = (bf16[1024,256]{1,0:T(8,128)(2,1)}, bf16[1024,256]{1,0:T(8,128)(2,1)}, u32[]{:S(2)}, u32[]{:S(2)}) collective-permute-start(bf16[1024,256]{1,0:T(8,128)(2,1)} %get-tuple-element.18), channel_id=1, source_target_pairs={{0,1},{1,0},{2,3},{3,2},{4,5},{5,4},{6,7},{7,6},{8,9},{9,8},{10,11... | collective-permute-start | bytes 1572872 | tf_op jit(solution)/shard_map/ppermute | solution.py:338
  117.4 1.2 copy-start.8
  118.7 31.9 %collective-permute-start.11 = (bf16[16,48,256]{2,1,0:T(8,128)(2,1)S(1)}, bf16[16,48,256]{2,1,0:T(8,128)(2,1)}, u32[]{:S(2)}, u32[]{:S(2)}) collective-permute-start(bf16[16,48,256]{2,1,0:T(8,128)(2,1)S(1)} %fusion.1.first), channel_id=1, source_target_pairs={{0,256},{256,0},{1,257},{257,1},{2,258},{258,2},{3,259},{259,3},{4... | collective-permute-start | bytes 1179656 | tf_op jit(solution)/shard_map/ppermute | solution.py:338
  133.4 1.9 copy-start.3
  135.3 15.3 %copy-start.9 = (f32[16,48,512]{2,1,0:T(8,128)S(1)}, f32[16,48,512]{2,1,0:T(8,128)}, u32[]{:S(2)}) copy-start(f32[16,48,512]{2,1,0:T(8,128)} %copy-done.8) | copy-start | bytes 4718596
  135.3 15.3 %copy-start.12 = (f32[16,48,256]{2,1,0:T(8,128)S(1)}, f32[16,48,256]{2,1,0:T(8,128)}, u32[]{:S(2)}) copy-start(f32[16,48,256]{2,1,0:T(8,128)} %get-tuple-element.23) | copy-start | bytes 2359300
  142.9 10.9 %collective-permute-start.9 = (bf16[256,512]{1,0:T(8,128)(2,1)S(1)}, bf16[256,512]{1,0:T(8,128)(2,1)S(1)}, u32[]{:S(2)}, u32[]{:S(2)}) collective-permute-start(bf16[256,512]{1,0:T(8,128)(2,1)S(1)} %get-tuple-element.21), channel_id=1, source_target_pairs={{0,8},{8,16},{16,24},{24,32},{32,40},{40,48},{48,56},{56,64},{64,7... | collective-permute-start | bytes 786440 | tf_op jit(solution)/shard_map/ppermute | solution.py:356
  144.9 9.6 %collective-permute-start.10 = (bf16[256,512]{1,0:T(8,128)(2,1)S(1)}, bf16[256,512]{1,0:T(8,128)(2,1)S(1)}, u32[]{:S(2)}, u32[]{:S(2)}) collective-permute-start(bf16[256,512]{1,0:T(8,128)(2,1)S(1)} %get-tuple-element.22), channel_id=1, source_target_pairs={{8,0},{16,8},{24,16},{32,24},{40,32},{48,40},{56,48},{64,56},{72,6... | collective-permute-start | bytes 786440 | tf_op jit(solution)/shard_map/ppermute | solution.py:356
  151.9 10.3 %collective-permute-start.12 = (bf16[8,48,256]{2,1,0:T(8,128)(2,1)S(1)}, bf16[8,48,256]{2,1,0:T(8,128)(2,1)S(1)}, u32[]{:S(2)}, u32[]{:S(2)}) collective-permute-start(bf16[8,48,256]{2,1,0:T(8,128)(2,1)S(1)} %fusion.2), channel_id=1, source_target_pairs={{0,16},{16,0},{32,48},{48,32},{64,80},{80,64},{96,112},{112,96},{1... | collective-permute-start | bytes 589832 | tf_op jit(solution)/shard_map/ppermute | solution.py:368
  153.8 0.7 copy-start.14
  154.5 0.7 copy-start.15
  157.4 38.1 %all-to-all-start.2 = ((bf16[8,128,768]{2,1,0:T(8,128)(2,1)}), bf16[8,128,768]{2,1,0:T(8,128)(2,1)S(1)}, u32[]{:S(2)}, u32[]{:S(2)}) async-start(bf16[8,128,768]{2,1,0:T(8,128)(2,1)} %bitcast.49), calls=%async_computation.2 | async-start | bytes 3145728 | tf_op jit(solution)/shard_map/all_to_all | solution.py:437
  162.2 8.5 %collective-permute-start.13 = (bf16[4,48,256]{2,1,0:T(8,128)(2,1)S(1)}, bf16[4,48,256]{2,1,0:T(8,128)(2,1)S(1)}, u32[]{:S(2)}, u32[]{:S(2)}) collective-permute-start(bf16[4,48,256]{2,1,0:T(8,128)(2,1)S(1)} %fusion.3), channel_id=1, source_target_pairs={{0,32},{16,48},{32,0},{48,16},{64,96},{80,112},{96,64},{112,80},{1... | collective-permute-start | bytes 294920 | tf_op jit(solution)/shard_map/ppermute | solution.py:368
  170.7 11.4 %collective-permute-start.14 = (bf16[2,48,256]{2,1,0:T(8,128)(2,1)S(1)}, bf16[2,48,256]{2,1,0:T(8,128)(2,1)S(1)}, u32[]{:S(2)}, u32[]{:S(2)}) collective-permute-start(bf16[2,48,256]{2,1,0:T(8,128)(2,1)S(1)} %fusion.4), channel_id=1, source_target_pairs={{0,64},{16,80},{32,96},{48,112},{64,0},{80,16},{96,32},{112,48},{1... | collective-permute-start | bytes 147464 | tf_op jit(solution)/shard_map/ppermute | solution.py:368
  182.2 16.9 %collective-permute-start.15 = (f32[48,256]{1,0:T(8,128)S(1)}, f32[48,256]{1,0:T(8,128)S(1)}, u32[]{:S(2)}, u32[]{:S(2)}) collective-permute-start(f32[48,256]{1,0:T(8,128)S(1)} %get-tuple-element.36), channel_id=1, source_target_pairs={{0,0},{1,256},{16,16},{17,272},{32,32},{33,288},{48,48},{49,304},{... | collective-permute-start | bytes 147464 | tf_op jit(solution)/shard_map/ppermute | solution.py:382
  187.4 16.0 %collective-permute-start.16 = (f32[48,256]{1,0:T(8,128)S(1)}, f32[48,256]{1,0:T(8,128)S(1)}, u32[]{:S(2)}, u32[]{:S(2)}) collective-permute-start(f32[48,256]{1,0:T(8,128)S(1)} %get-tuple-element.35), channel_id=1, source_target_pairs={{0,128},{1,384},{16,144},{17,400},{32,160},{33,416},{48,176},{49,4... | collective-permute-start | bytes 147464 | tf_op jit(solution)/shard_map/ppermute | solution.py:383
  199.1 0.6 copy-start.16
